TPU v7x, 128 devices: a whole 4x4x4 slice. The times are simulated.
128 devices in a mesh: dp: 32 (over x, y, core), space: 4 (over z).
Axes of the slice: x: 4, y: 4, z: 4, core: 2. Of those that a mesh axis runs over, the one named last changes fastest.
Arguments:
- features: bfloat16 [32, 8, 128, 512], P('dp', 'space'), may hold values from -6 to 6
- latent_bank: float32 [1024, 512], replicated, may hold values from -6 to 6
- latent_ids: int32 [32], P('dp'), may hold values from 0 to 1023
- conv_kernel: bfloat16 [3, 3, 512, 512], P(None, None, 'dp'), may hold values from -0.09375 to 0.09375
- style_one: float32 [512, 512], replicated, may hold values from -0.25 to 0.25
- bias_one: float32 [512], replicated, may hold values from 0.1 to 1.9
- style_two: float32 [512, 512], replicated, may hold values from -0.25 to 0.25
- bias_two: float32 [512], replicated, may hold values from 0.1 to 1.9
- rgb_weight: float32 [512, 3], replicated, may hold values from -0.25 to 0.25
- conv_bias: float32 [512], replicated, may hold values from -3 to 3
- direction: float32 [32, 3, 8, 128], P('dp', None, 'space'), may hold values from -60 to 60
- length_target: float32 [1], replicated, may hold values from 0.5 to 3
Outputs:
- kernel_grad: float32 [3, 3, 512, 512], P(None, None, 'dp')
- path_lengths: float32 [32], P('dp')
- new_target: float32 [1], replicated
All inputs are finite; a program needn't handle non-finite values.
Results may differ from a plain program's by a relative error of at most 0.025.
Values may be sent and summed in bfloat16 or wider, within the bound.
No kernel may reach another device: no remote copies, remote signals or barrier semaphores. Data moves between devices by JAX's collectives and lax.ppermute only.
A program may use at most 64 MiB of HBM per device.

v0:
```python
import math

import jax
import jax.numpy as jnp
from jax import lax
from jax.sharding import PartitionSpec as P

PL_WEIGHT = 8.0
PL_DECAY = 0.5
SQRT_TWO = math.sqrt(2.0)
HIGHEST = lax.Precision.HIGHEST


def extended(block, sides, width):
    for axis, dim in sides:
        count = lax.axis_size(axis)
        forward = [(i, i + 1) for i in range(count - 1)]
        backward = [(target, source) for source, target in forward]
        low = lax.ppermute(
            lax.slice_in_dim(block, block.shape[dim] - width, None, axis=dim), axis, forward
        )
        high = lax.ppermute(lax.slice_in_dim(block, 0, width, axis=dim), axis, backward)
        block = jnp.concatenate([low, block, high], axis=dim)
    return block


def synth(padded, latent, kernel_full, params, target_dir, scaling):
    style_one, bias_one, style_two, bias_two, rgb_weight, conv_bias = params
    tile_rows = padded.shape[0] - 2
    tile_cols = padded.shape[1] - 2
    channels = padded.shape[2]
    style_in = jnp.dot(latent, style_one, precision=HIGHEST) + bias_one
    energy = jnp.sum(kernel_full * kernel_full, axis=(0, 1))
    demodulation = lax.rsqrt(jnp.dot(style_in * style_in, energy, precision=HIGHEST) + 1e-08)
    modulated = (
        kernel_full * style_in[None, None, :, None] * demodulation[None, None, None, :]
    ).astype(jnp.bfloat16)
    hidden = jnp.zeros((tile_rows * tile_cols, modulated.shape[3]), jnp.float32) + conv_bias
    for row_off in range(3):
        for col_off in range(3):
            window = padded[row_off : row_off + tile_rows, col_off : col_off + tile_cols].reshape(
                tile_rows * tile_cols, channels
            )
            hidden = hidden + jnp.dot(
                window, modulated[row_off, col_off], preferred_element_type=jnp.float32
            )
    activated = ((0.6 * hidden + 0.4 * jnp.sqrt(hidden * hidden + 0.25)) * SQRT_TWO).astype(
        jnp.bfloat16
    )
    colour = jnp.dot(latent, style_two, precision=HIGHEST) + bias_two
    rgb_mod = (rgb_weight * colour[:, None]).astype(jnp.bfloat16)
    picture = jnp.dot(activated, rgb_mod, preferred_element_type=jnp.float32)
    return jnp.sum(picture * target_dir.reshape(3, tile_rows * tile_cols).T) * scaling


def per_device(
    features,
    latent_bank,
    latent_ids,
    conv_kernel,
    style_one,
    bias_one,
    style_two,
    bias_two,
    rgb_weight,
    conv_bias,
    direction,
    length_target,
):
    kernel_whole = lax.all_gather(conv_kernel, "dp", axis=2, tiled=True)
    kernel_full = kernel_whole.astype(jnp.float32)
    bordered = extended(features, (("space", 1),), 1)
    padded = jnp.pad(bordered, ((0, 0), (0, 0), (1, 1), (0, 0)))
    latents = jnp.take(latent_bank, latent_ids, axis=0)
    scaling = 1.0 / math.sqrt(features.shape[1] * lax.axis_size("space") * features.shape[2])
    params = (style_one, bias_one, style_two, bias_two, rgb_weight, conv_bias)

    def one_grad(pad_one, latent, dir_one):
        return jax.grad(synth, argnums=1)(pad_one, latent, kernel_full, params, dir_one, scaling)

    partial_grads = jax.vmap(one_grad)(padded, latents, direction)
    style_grads = lax.psum(partial_grads, "space")
    lengths = jnp.sqrt(jnp.sum(style_grads * style_grads, axis=1) + 1e-08)
    total = lax.psum(jnp.sum(lengths), "dp")
    target = length_target + PL_DECAY * (
        total / (lengths.shape[0] * lax.axis_size("dp")) - length_target
    )
    factor = 2.0 * PL_WEIGHT * (lengths - target) / lengths
    tangents = factor[:, None] * style_grads

    def total_of(kernel_var):

        def along(pad_one, latent, tangent, dir_one):
            return jax.jvp(
                lambda point: synth(pad_one, point, kernel_var, params, dir_one, scaling),
                (latent,),
                (tangent,),
            )[1]

        return jnp.sum(jax.vmap(along)(padded, latents, tangents, direction))

    kernel_sum = jax.grad(total_of)(kernel_full)
    shard_sum = lax.psum_scatter(
        kernel_sum.astype(jnp.bfloat16), "dp", scatter_dimension=2, tiled=True
    )
    kernel_grad = lax.psum(shard_sum, "space").astype(jnp.float32)
    return (kernel_grad, lengths, target)


def solution(mesh):
    in_specs = (
        P("dp", "space", None, None),
        P(),
        P("dp"),
        P(None, None, "dp", None),
        P(),
        P(),
        P(),
        P(),
        P(),
        P(),
        P("dp", None, "space", None),
        P(),
    )
    out_specs = (P(None, None, "dp", None), P("dp"), P())
    return jax.shard_map(
        per_device, mesh=mesh, in_specs=in_specs, out_specs=out_specs, check_vma=False
    )
```

profile of v0, /device:TPU:0, one launch (start us, length us, event | category | flops | bytes accessed | tf_op | source)
XLA Modules:
  0.0 311.9 jit_solution(5924090728413507393)
XLA Ops:
  7.2 0.7 all-gather.2.cloned.1.call-update
  8.0 1.0 fusion.108
  9.0 3.9 %collective-permute-start = (bf16[1,1,128,512]{3,2,1,0:T(8,128)(2,1)S(1)}, bf16[1,1,128,512]{3,2,1,0:T(8,128)(2,1)S(1)}, u32[]{:S(2)}, u32[]{:S(2)}) collective-permute-start(bf16[1,1,128,512]{3,2,1,0:T(8,128)(2,1)S(1)} %get-tuple-element.29), channel_id=1, source_target_pairs={{0,1},{1,2},{2,3},{4,5},{5,6},{6,7},{8,9},{9,10},{10,11},{12,13},{... | collective-permute-start | bytes 393224 | tf_op jit(solution)/shard_map/ppermute | solution.py:19
  12.9 1.3 collective-permute-start.1
  14.8 1.3 fusion.100
  16.2 0.7 add.176
  16.9 0.7 broadcast_multiply_fusion
  17.5 1.8 fusion.49
  19.3 1.8 fusion.102
  21.2 0.7 fusion.106
  21.9 1.8 pad_maximum_fusion
  23.7 1.1 fusion.61
  24.8 1.0 fusion.107
  25.8 33.8 %all-gather.2.cloned.1.call-done = bf16[3,3,512,512]{3,2,1,0:T(8,128)(2,1)} async-done(((bf16[3,3,16,512]{3,2,1,0:T(8,128)(2,1)}), bf16[3,3,512,512]{3,2,1,0:T(8,128)(2,1)}) %all-gather.2.cloned.1.call-update) | async-done | bytes 4718608 | tf_op jit(solution)/shard_map/all_gather | solution.py:70
  59.6 3.5 %fusion.19 = f32[512,512]{1,0:T(8,128)S(1)} fusion(bf16[3,3,512,512]{3,2,1,0:T(8,128)(2,1)} %all-gather.2.cloned.1.call-done), kind=kLoop, calls=%fused_computation.31 | loop fusion | flops 6815744 | bytes 5767168 | tf_op jit(solution)/shard_map/jvp(vmap(jvp()))/reduce_sum | solution.py:33
  63.1 0.6 fusion.109
  63.8 1.3 fusion.20
  67.6 0.6 multiply_add_fusion.1
  68.2 0.3 fusion.22
  70.3 0.3 fusion.29
  70.7 0.3 fusion.26
  71.4 5.6 %fusion.17 = (f32[512]{0:T(512)S(1)}, f32[512]{0:T(512)S(1)}, bf16[1,3,3,512,512]{4,3,2,1,0:T(8,128)(2,1)}) fusion(bf16[3,3,512,512]{3,2,1,0:T(8,128)(2,1)S(1)} %copy-done.1, f32[512]{0:T(512)S(1)} %get-tuple-element.20, f32[512]{0:T(512)S(1)} %add_rsqrt_fusion, bf16[1,1,1,512,512]{4,3,2,1,0:T(8,128)(2,1)S(1)} %fusion.30, ...), kind=kLoop, calls=%fused_computation.29 | loop fusion | flops 37747712 | bytes 14163968 | tf_op jit(solution)/shard_map/vmap(transpose(jvp()))/reduce_sum | solution.py:36
  77.0 1.0 fusion.111
  78.0 1.0 fusion.112
  79.0 0.4 fusion.56
  79.4 1.0 fusion.110
  80.3 10.7 %psum.21 = f32[1,512]{1,0:T(1,128)S(1)} all-reduce(f32[1,512]{1,0:T(1,128)S(1)} %bitcast.414), channel_id=1, replica_groups=mesh['dp'=32,'space'=4] {'space'}, use_global_device_ids=true, to_apply=%region_4.5 | all-reduce | flops 512 | bytes 4096 | tf_op jit(solution)/shard_map/psum | solution.py:82
  91.0 0.6 multiply_reduce_fusion
  93.0 64.2 %psum.22 = f32[]{:T(128)} all-reduce(f32[]{:T(128)} %sqrt.12), channel_id=1, replica_groups=mesh['dp'=32,'space'=4] {'dp'}, use_global_device_ids=true, to_apply=%region_6.7 | all-reduce | flops 1 | bytes 8 | tf_op jit(solution)/shard_map/psum | solution.py:84
  157.9 0.6 fusion.88
  158.5 0.6 fusion.90
  159.1 0.6 fusion.113
  159.8 4.7 %fusion.21 = bf16[1,3,3,512,512]{4,3,2,1,0:T(8,128)(2,1)S(1)} fusion(bf16[3,3,512,512]{3,2,1,0:T(8,128)(2,1)} %all-gather.2.cloned.1.call-done, f32[512]{0:T(512)S(1)} %fusion.104, f32[512]{0:T(512)S(1)} %bitcast.396, f32[512]{0:T(512)S(1)} %add_rsqrt_fusion, f32[512]{0:T(512)S(1)} %get-tuple-element.20), kind=kLoop, calls=%fused_computation.33 | loop fusion | flops 16515072 | bytes 9445376 | tf_op jit(solution)/shard_map/jvp(vmap(jvp()))/convert_element_type | solution.py:37
  167.3 0.8 fusion.62
  168.1 0.4 fusion.31
  168.5 0.4 fusion.33
  168.8 0.4 fusion.34
  169.2 0.3 fusion.36
  169.5 0.3 fusion.32
  169.9 0.3 fusion.37
  170.2 0.4 fusion.38
  170.6 0.4 fusion.35
  170.9 0.4 fusion.39
  171.4 3.1 fusion.14
  174.7 5.6 %fusion.16 = bf16[3,3,512,512]{3,2,1,0:T(8,128)(2,1)} fusion(bf16[1,3,3,512,512]{4,3,2,1,0:T(8,128)(2,1)S(1)} %bitcast.354, bf16[3,3,512,512]{3,2,1,0:T(8,128)(2,1)S(1)} %bitcast.352, f32[512,512]{1,0:T(8,128)S(1)} %multiply_add_fusion, f32[512]{0:T(512)S(1)} %get-tuple-element.20, f32[512]{0:T(512)S(1)} %fusion.104, f32[512]{0:T(512)S(1)} %bitcast.398, ...), kind=kLoop, calls=%fused_computation.28 | loop fusion | flops 51904512 | bytes 19931136 | tf_op jit(solution)/shard_map/convert_element_type | solution.py:104
  180.3 77.7 %reduce-scatter.2.cloned.1.call-done = bf16[3,3,16,512]{3,2,1,0:T(8,128)(2,1)} async-done(((bf16[3,3,512,512]{3,2,1,0:T(8,128)(2,1)}), bf16[3,3,16,512]{3,2,1,0:T(8,128)(2,1)}) %reduce-scatter.2.cloned.1.call-update) | async-done | bytes 147472 | tf_op jit(solution)/shard_map/reduce_scatter | solution.py:103
  258.1 43.3 %all-reduce.21.cloned.1.call-done = bf16[3,3,16,512]{3,2,1,0:T(8,128)(2,1)} async-done(((bf16[3,3,16,512]{3,2,1,0:T(8,128)(2,1)}), bf16[3,3,16,512]{3,2,1,0:T(8,128)(2,1)}) %all-reduce.21.cloned.1.call-update) | async-done | bytes 147472 | tf_op jit(solution)/shard_map/psum | solution.py:106
  301.4 1.7 convert_element_type.320
  (100 shorter events, 7.7 us)
Async XLA Ops:
  7.2 7.7 %copy-start = (f32[512,512]{1,0:T(8,128)S(1)}, f32[512,512]{1,0:T(8,128)}, u32[]{:S(2)}) copy-start(f32[512,512]{1,0:T(8,128)} %param.18) | copy-start | bytes 3145732
  7.2 52.4 %all-gather.2.cloned.1.call-start = ((), (), s32[]{:S(2)}) async-start(), calls=%async_computation.1 | async-start | bytes 4866048 | tf_op jit(solution)/shard_map/all_gather | solution.py:70
  7.9 250.1 %reduce-scatter.2.cloned.1.call-start = ((), (), s32[]{:S(2)}) async-start(), calls=%async_computation.2 | async-start | bytes 4866048 | tf_op jit(solution)/shard_map/reduce_scatter | solution.py:103
  9.0 12.9 %collective-permute-start = (bf16[1,1,128,512]{3,2,1,0:T(8,128)(2,1)S(1)}, bf16[1,1,128,512]{3,2,1,0:T(8,128)(2,1)S(1)}, u32[]{:S(2)}, u32[]{:S(2)}) collective-permute-start(bf16[1,1,128,512]{3,2,1,0:T(8,128)(2,1)S(1)} %get-tuple-element.29), channel_id=1, source_target_pairs={{0,1},{1,2},{2,3},{4,5},{5,6},{6,7},{8,9},{9,10},{10,11},{12,13},{... | collective-permute-start | bytes 393224 | tf_op jit(solution)/shard_map/ppermute | solution.py:19
  12.9 9.0 %collective-permute-start.1 = (bf16[1,1,128,512]{3,2,1,0:T(8,128)(2,1)S(1)}, bf16[1,1,128,512]{3,2,1,0:T(8,128)(2,1)S(1)}, u32[]{:S(2)}, u32[]{:S(2)}) collective-permute-start(bf16[1,1,128,512]{3,2,1,0:T(8,128)(2,1)S(1)} %get-tuple-element.30), channel_id=1, source_target_pairs={{1,0},{2,1},{3,2},{5,4},{6,5},{7,6},{9,8},{10,9},{11,10},{13,12},{... | collective-permute-start | bytes 393224 | tf_op jit(solution)/shard_map/ppermute | solution.py:22
  25.7 43.2 %copy-start.10 = (bf16[1,2,128,512]{3,2,1,0:T(8,128)(2,1)}, bf16[1,2,128,512]{3,2,1,0:T(8,128)(2,1)S(1)}, u32[]{:S(2)}) copy-start(bf16[1,2,128,512]{3,2,1,0:T(8,128)(2,1)S(1)} %get-tuple-element.23) | copy-start | bytes 786436
  25.7 43.5 %copy-start.8 = (bf16[1,2,128,512]{3,2,1,0:T(8,128)(2,1)}, bf16[1,2,128,512]{3,2,1,0:T(8,128)(2,1)S(1)}, u32[]{:S(2)}) copy-start(bf16[1,2,128,512]{3,2,1,0:T(8,128)(2,1)S(1)} %get-tuple-element.21) | copy-start | bytes 786436
  25.7 44.2 %copy-start.6 = (bf16[1,2,128,512]{3,2,1,0:T(8,128)(2,1)}, bf16[1,2,128,512]{3,2,1,0:T(8,128)(2,1)S(1)}, u32[]{:S(2)}) copy-start(bf16[1,2,128,512]{3,2,1,0:T(8,128)(2,1)S(1)} %get-tuple-element.24) | copy-start | bytes 786436
  25.7 45.3 %copy-start.4 = (bf16[1,2,128,512]{3,2,1,0:T(8,128)(2,1)}, bf16[1,2,128,512]{3,2,1,0:T(8,128)(2,1)S(1)}, u32[]{:S(2)}) copy-start(bf16[1,2,128,512]{3,2,1,0:T(8,128)(2,1)S(1)} %get-tuple-element.25) | copy-start | bytes 786436
  59.6 4.1 %copy-start.1 = (bf16[3,3,512,512]{3,2,1,0:T(8,128)(2,1)S(1)}, bf16[3,3,512,512]{3,2,1,0:T(8,128)(2,1)}, u32[]{:S(2)}) copy-start(bf16[3,3,512,512]{3,2,1,0:T(8,128)(2,1)} %all-gather.2.cloned.1.call-done) | copy-start | bytes 14155780
  63.7 1.6 copy-start.12
  63.7 2.3 copy-start.14
  65.0 1.3 copy-start.23
  65.1 1.6 copy-start.16
  65.4 1.9 copy-start.2
  66.0 1.6 copy-start.18
  66.0 1.6 copy-start.20
  68.2 10.8 %copy-start.24 = (f32[256,512]{1,0:T(8,128)}, f32[256,512]{1,0:T(8,128)S(1)}, u32[]{:S(2)}) copy-start(f32[256,512]{1,0:T(8,128)S(1)} %get-tuple-element.32) | copy-start | bytes 1572868
  71.4 6.6 %copy-start.3 = (f32[512,512]{1,0:T(8,128)S(1)}, f32[512,512]{1,0:T(8,128)}, u32[]{:S(2)}) copy-start(f32[512,512]{1,0:T(8,128)} %param.16) | copy-start | bytes 3145732
  71.4 7.6 %copy-start.22 = (f32[512,3]{0,1:T(4,128)S(1)}, f32[512,3]{0,1:T(4,128)}, u32[]{:S(2)}) copy-start(f32[512,3]{0,1:T(4,128)} %param.20) | copy-start | bytes 18436
  159.7 4.7 %copy-start.5 = (bf16[1,2,128,512]{3,2,1,0:T(8,128)(2,1)S(1)}, bf16[1,2,128,512]{3,2,1,0:T(8,128)(2,1)}, u32[]{:S(2)}) copy-start(bf16[1,2,128,512]{3,2,1,0:T(8,128)(2,1)} %copy-done.4) | copy-start | bytes 786436
  159.7 5.0 %copy-start.11 = (bf16[1,2,128,512]{3,2,1,0:T(8,128)(2,1)S(1)}, bf16[1,2,128,512]{3,2,1,0:T(8,128)(2,1)}, u32[]{:S(2)}) copy-start(bf16[1,2,128,512]{3,2,1,0:T(8,128)(2,1)} %copy-done.10) | copy-start | bytes 786436
  159.8 5.3 %copy-start.13 = (bf16[1,2,128,512]{3,2,1,0:T(8,128)(2,1)S(1)}, bf16[1,2,128,512]{3,2,1,0:T(8,128)(2,1)}, u32[]{:S(2)}) copy-start(bf16[1,2,128,512]{3,2,1,0:T(8,128)(2,1)} %get-tuple-element.22) | copy-start | bytes 786436
  159.8 5.6 %copy-start.15 = (bf16[1,2,128,512]{3,2,1,0:T(8,128)(2,1)S(1)}, bf16[1,2,128,512]{3,2,1,0:T(8,128)(2,1)}, u32[]{:S(2)}) copy-start(bf16[1,2,128,512]{3,2,1,0:T(8,128)(2,1)} %get-tuple-element.26) | copy-start | bytes 786436
  164.4 1.6 copy-start.17
  164.5 1.9 copy-start.7
  164.5 2.2 copy-start.9
  165.7 1.6 copy-start.19
  165.7 1.6 copy-start.21
  165.7 1.6 copy-start.25
  167.3 4.0 %slice-start = ((s8[4718592]{0:T(1024)(128)(4,1)}), s8[4194304]{0:T(1024)(128)(4,1)S(1)}, s32[]{:S(2)}) async-start(s8[4718592]{0:T(1024)(128)(4,1)} %bitcast.351), calls=%async_computation.4 | async-start | bytes 8388608
  167.3 4.0 %slice-start.2 = ((s8[4718592]{0:T(1024)(128)(4,1)}), s8[4194304]{0:T(1024)(128)(4,1)S(1)}, s32[]{:S(2)}) async-start(s8[4718592]{0:T(1024)(128)(4,1)} %bitcast.353), calls=%async_computation.6 | async-start | bytes 8388608
  168.1 3.2 %slice-start.1 = ((s8[4718592]{0:T(1024)(128)(4,1)}), s8[524288]{0:T(1024)(128)(4,1)S(1)}, s32[]{:S(2)}) async-start(s8[4718592]{0:T(1024)(128)(4,1)} %bitcast.351), calls=%async_computation.5 | async-start | bytes 1048576
  168.1 3.2 %slice-start.3 = ((s8[4718592]{0:T(1024)(128)(4,1)}), s8[524288]{0:T(1024)(128)(4,1)S(1)}, s32[]{:S(2)}) async-start(s8[4718592]{0:T(1024)(128)(4,1)} %bitcast.353), calls=%async_computation.7 | async-start | bytes 1048576
  180.3 121.2 %all-reduce.21.cloned.1.call-start = ((), (), s32[]{:S(2)}) async-start(), calls=%async_computation.3 | async-start | bytes 294912 | tf_op jit(solution)/shard_map/psum | solution.py:106
Sparse Core Ops, SparseCore 0:
  10.4 49.1 all-gather.1
  180.4 77.6 reduce-scatter.1
  260.5 40.8 all-reduce.20
where the time goes:
time: 312 us
  waiting for transfers between devices  156 us (50%)
  blocking collectives  74.9 us (24%)
  other arithmetic  31.2 us (10%)
  matrix products  23.2 us (7%)
  between operations  19.4 us (6%)
  starting transfers between devices  5.32 us (2%)
    reduce_scatter x1, waiting for transfers between devices, per_device(): lax.psum_scatter(kernel_sum.astype(jnp.bfloat16), 'dp', scatter_dimension...  77.7 us
    psum x1, blocking collectives, per_device(): total = lax.psum(jnp.sum(lengths), 'dp')  64.2 us
    psum x1, waiting for transfers between devices, per_device(): kernel_grad = lax.psum(shard_sum, 'space').astype(jnp.float32)  43.3 us
    all_gather x1, waiting for transfers between devices, per_device(): kernel_whole = lax.all_gather(conv_kernel, 'dp', axis=2, tiled=True)  33.8 us
    dot_general x36, matrix products, synth(): jnp.dot(window, modulated[row_off, col_off], preferred_element_type=jnp.f...  12.3 us
    psum x1, blocking collectives, per_device(): style_grads = lax.psum(partial_grads, 'space')  10.7 us
    reduce_sum x2, other arithmetic, synth(): kernel_full * style_in[None, None, :, None]  8.7 us
  transfers between devices with their start and end apart: 5, of which 3 were waited for; matrix products, arithmetic and copies ran while one was open for 4% of the time, Pallas kernels for 0%

commit v1 on v0

v1 whole, which is shorter than its diff:
```python
import functools
import math

import jax
import jax.numpy as jnp
from jax import lax
from jax.experimental import pallas as pl
from jax.experimental.pallas import tpu as pltpu
from jax.sharding import PartitionSpec as P

PL_WEIGHT = 8.0
PL_DECAY = 0.5
SQRT_TWO = math.sqrt(2.0)
F32 = jnp.float32
BF16 = jnp.bfloat16

CH = 512
OC = 128
NPOS = 1024
COLS = 128
NDP = 32
VMEM = pltpu.VMEM
SMEM = pltpu.SMEM


def full(space=VMEM):
    return pl.BlockSpec(memory_space=space)


def params(mib):
    return pltpu.CompilerParams(vmem_limit_bytes=mib * 1024 * 1024)


def dot(a, b):
    return jnp.dot(a, b, preferred_element_type=F32)


def lanes_of(row):
    return jnp.transpose(jnp.broadcast_to(row, (OC, row.shape[1])))


def row_of(lanes):
    return jnp.sum(jnp.transpose(lanes), axis=0, keepdims=True)


def styles_kernel(z_ref, id_ref, bank_ref, w1_ref, b1_ref, w2_ref, b2_ref, s_ref, c_ref, w_buf, sem):
    copy = pltpu.make_async_copy(bank_ref.at[pl.ds(id_ref[0], 1)], w_buf, sem)
    copy.start()
    copy.wait()
    z = z_ref[0]
    lo = pl.multiple_of(z * OC, OC)
    w = lanes_of(w_buf[...])
    for j in range(4):
        block = pl.ds(j * OC, OC)
        s_ref[:, block] = jnp.sum(w * w1_ref[:, block], axis=0, keepdims=True) + b1_ref[:, block]
    mine = pl.ds(lo, OC)
    c_ref[...] = jnp.sum(w * w2_ref[:, mine], axis=0, keepdims=True) + b2_ref[:, mine]


def image_kernel(z_ref, m0, m1, m2, m3, f_ref, ft_ref, d_ref, dt_ref):
    z = z_ref[0]
    zero = jnp.zeros((COLS, CH), BF16)
    f_ref[0:COLS, :] = zero
    f_ref[NPOS + COLS :, :] = zero
    ft_ref[:, 0:COLS] = jnp.zeros((CH, COLS), BF16)
    ft_ref[:, NPOS + COLS :] = jnp.zeros((CH, COLS), BF16)
    for k, m in enumerate((m0, m1, m2, m3)):
        at = pl.multiple_of(lax.rem(z + 4 - k, 4) * 256, 256)
        feat = m[0:256, :]
        f_ref[pl.ds(at + COLS, 256), :] = feat
        ft_ref[:, pl.ds(at + COLS, 256)] = jnp.transpose(feat)
        part = m[256:272, 0:256]
        d_ref[:, pl.ds(at, 256)] = part
        wide = jnp.concatenate([part.astype(F32), jnp.zeros((112, 256), F32)], axis=0)
        dt_ref[pl.ds(at, 256), :] = jnp.transpose(wide).astype(BF16)


def column():
    return lax.rem(lax.broadcasted_iota(jnp.int32, (NPOS, OC), 0), COLS)


def from_left(x):
    return jnp.where(column() == 0, 0.0, pltpu.roll(x, 1, 0))


def from_right(x):
    return jnp.where(column() == COLS - 1, 0.0, pltpu.roll(x, NPOS - 1, 0))


def tap(k_ref, t):
    return k_ref[:, t].reshape(CH, OC).astype(F32)


def conv(f_ref, mod_of):
    total = None
    for dy in range(3):
        part = dot(f_ref[dy * COLS : dy * COLS + NPOS, :], mod_of(dy))
        total = part if total is None else total + part
    return from_left(total[:, 0:OC]) + total[:, OC : 2 * OC] + from_right(total[:, 2 * OC :])


def spread(h):
    return jnp.concatenate([from_right(h), h, from_left(h)], axis=1).astype(BF16)


def colours_of(rgb_ref, colour, z):
    lo = pl.multiple_of(z * OC, OC)
    rgb = rgb_ref[:, pl.ds(lo, OC)]
    mod = (rgb * colour).astype(BF16).astype(F32)[0:3]
    return rgb, jnp.concatenate([mod, mod, mod, jnp.zeros((119, OC), F32)], axis=0).astype(BF16)


def first_kernel(
    z_ref, f_ref, ft_ref, d_ref, dt_ref, k_ref, s_ref, c_ref, rgb_ref, bias_ref, w1_ref, w2_ref,
    u_ref, pre_ref, ga_ref, gm_ref, e_ref, rows_ref,
):
    z = z_ref[0]
    lo = pl.multiple_of(z * OC, OC)
    scaling = 1.0 / math.sqrt(NPOS)
    energy = None
    for t in range(9):
        k = tap(k_ref, t)
        energy = k * k if energy is None else energy + k * k
    e_ref[...] = energy
    s = lanes_of(s_ref[...])
    demod = lax.rsqrt(jnp.sum(s * s * energy, axis=0, keepdims=True) + 1e-08)
    sd = s * demod

    def mod_of(dy):
        return jnp.concatenate([(tap(k_ref, 3 * dy + dx) * sd).astype(BF16) for dx in range(3)], axis=1)

    bare = conv(f_ref, mod_of)
    pre = bare + bias_ref[:, pl.ds(lo, OC)]
    pre_ref[...] = pre
    square = pre * pre + 0.25
    root = lax.rsqrt(square)
    act = ((0.6 * pre + 0.4 * (square * root)) * SQRT_TWO).astype(BF16)
    rgb, mix = colours_of(rgb_ref, c_ref[...], z)
    ga = (dot(dt_ref[...], mix) * scaling).astype(BF16)
    ga_ref[...] = ga
    h = ga.astype(F32) * ((0.6 + 0.4 * (pre * root)) * SQRT_TWO)
    parts = dot(d_ref[...], act)
    grad_mix = ((parts[0:3] + parts[3:6] + parts[6:9]) * scaling).astype(BF16).astype(F32)
    grad_colour = jnp.sum(grad_mix * rgb[0:3], axis=0, keepdims=True)
    grad_demod = jnp.sum(h * bare, axis=0, keepdims=True) / demod
    grad_q = -0.5 * demod * demod * demod * grad_demod
    hs = spread(h)
    along = None
    for dy in range(3):
        gm = dot(ft_ref[:, dy * COLS : dy * COLS + NPOS], hs).astype(BF16)
        gm_ref[dy] = gm
        gm = gm.astype(F32)
        for dx in range(3):
            term = tap(k_ref, 3 * dy + dx) * gm[:, dx * OC : (dx + 1) * OC]
            along = term if along is None else along + term
    grad_s = row_of(along * demod + 2.0 * s * energy * grad_q)
    total = jnp.broadcast_to(grad_colour, (CH, OC)) * w2_ref[:, pl.ds(lo, OC)]
    for j in range(4):
        total = total + w1_ref[:, j * OC : (j + 1) * OC] * grad_s[:, j * OC : (j + 1) * OC]
    u_ref[...] = row_of(total)
    rows_ref[0:1, :] = demod
    rows_ref[1:2, :] = grad_demod


def second_kernel(
    z_ref, u0, u1, u2, u3, f_ref, ft_ref, dt_ref, k_ref, s_ref, rgb_ref, bias_ref, w1_ref, w2_ref,
    pre_ref, ga_ref, gm_ref, e_ref, rows_ref,
    out_ref, len_ref, u_buf,
):
    z = z_ref[0]
    lo = pl.multiple_of(z * OC, OC)
    scaling = 1.0 / math.sqrt(NPOS)
    for k, u in enumerate((u0, u1, u2, u3)):
        u_buf[pl.ds(lax.rem(z + 4 - k, 4), 1), :] = u[...]
    grad = (u_buf[0:1, :] + u_buf[1:2, :]) + (u_buf[2:3, :] + u_buf[3:4, :])
    length = jnp.sqrt(jnp.sum(grad * grad, axis=1, keepdims=True) + 1e-08)
    len_ref[...] = jnp.broadcast_to(length, (8, OC))
    point = lanes_of(grad)
    ds = lanes_of(
        jnp.concatenate(
            [jnp.sum(point * w1_ref[:, j * OC : (j + 1) * OC], axis=0, keepdims=True) for j in range(4)], axis=1
        )
    )
    dc = jnp.sum(point * w2_ref[:, pl.ds(lo, OC)], axis=0, keepdims=True)
    s = lanes_of(s_ref[...])
    energy = e_ref[...]
    demod = rows_ref[0:1, :]
    grad_demod = rows_ref[1:2, :]
    cube = demod * demod * demod
    dq = jnp.sum(2.0 * s * ds * energy, axis=0, keepdims=True)
    dd = -0.5 * cube * dq
    sd = s * demod
    dsd = ds * demod + s * dd

    def mod_of(dy):
        return jnp.concatenate([(tap(k_ref, 3 * dy + dx) * dsd).astype(BF16) for dx in range(3)], axis=1)

    dpre = conv(f_ref, mod_of)
    pre = pre_ref[...]
    root = lax.rsqrt(pre * pre + 0.25)
    slope = (0.6 + 0.4 * (pre * root)) * SQRT_TWO
    bend = (0.1 * SQRT_TWO) * (root * root * root)
    _, mix = colours_of(rgb_ref, dc, z)
    dga = (dot(dt_ref[...], mix) * scaling).astype(BF16).astype(F32)
    ga = ga_ref[...].astype(F32)
    h2 = ga * bend * dpre + dga * slope
    bare = pre - bias_ref[:, pl.ds(lo, OC)]
    cot_demod = (jnp.sum(h2 * bare + ga * slope * dpre, axis=0, keepdims=True) - dd * grad_demod) / demod
    cot_q = -0.5 * cube * cot_demod + 0.75 * cube * demod * demod * dq * grad_demod
    cot_dq = -0.5 * cube * grad_demod
    cot_e = 2.0 * s * (cot_q * s + 2.0 * cot_dq * ds)
    hs = spread(h2)
    for dy in range(3):
        gm2 = dot(ft_ref[:, dy * COLS : dy * COLS + NPOS], hs)
        for dx in range(3):
            t = 3 * dy + dx
            cut = slice(dx * OC, (dx + 1) * OC)
            value = gm2[:, cut] * sd + gm_ref[dy, :, cut].astype(F32) * dsd + tap(k_ref, t) * cot_e
            out_ref[:, t] = value.astype(BF16).reshape(NDP, 16, OC)
    high = length.astype(BF16)
    rest = length - high.astype(F32)
    middle = rest.astype(BF16)
    low = (rest - middle.astype(F32)).astype(BF16)
    row = lax.broadcasted_iota(jnp.int32, (16, OC), 0)
    pieces = jnp.where(row == 0, high.astype(F32), jnp.where(row == 1, middle.astype(F32), low.astype(F32)))
    out_ref[:, 9] = jnp.broadcast_to(pieces.astype(BF16)[None], (NDP, 16, OC))


def sum_kernel(part_ref, target_ref, out_ref, new_ref):
    lengths = []
    for b in range(NDP):
        tile = part_ref[b, 9].astype(F32)
        lengths.append(tile[0:1] + tile[1:2] + tile[2:3])
    total = lengths[0]
    for b in range(1, NDP):
        total = total + lengths[b]
    old = target_ref[0]
    target = old + PL_DECAY * (total / NDP - old)
    new_ref[...] = jnp.broadcast_to(target, (8, OC))
    value = None
    for b in range(NDP):
        factor = 2.0 * PL_WEIGHT * (lengths[b] - target) / lengths[b]
        term = part_ref[b, 0:9].astype(F32).reshape(144, OC) * factor
        value = term if value is None else value + term
    out_ref[...] = value.astype(BF16)


def last_kernel(z_ref, p0, p1, p2, p3, out_ref):
    z = z_ref[0]
    for k, p in enumerate((p0, p1, p2, p3)):
        at = pl.multiple_of(lax.rem(z + 4 - k, 4) * OC, OC)
        out_ref[:, pl.ds(at, OC)] = p[...].astype(F32)


def shape(dims, kind):
    return jax.ShapeDtypeStruct(dims, kind)


def call(kernel, outs, specs, mib, scratch=()):
    return pl.pallas_call(
        kernel,
        out_shape=outs,
        in_specs=specs,
        out_specs=jax.tree.map(lambda _: full(), outs),
        scratch_shapes=list(scratch),
        compiler_params=params(mib),
    )


def ring(x, axis, size):
    return [lax.ppermute(x, axis, [(i, (i + k) % size) for i in range(size)]) for k in range(1, size)]


def thirds(x):
    high = lax.reduce_precision(x, 8, 7)
    middle = lax.reduce_precision(x - high, 8, 7)
    return [high.astype(BF16), middle.astype(BF16), ((x - high) - middle).astype(BF16)]


def per_device(
    features, latent_bank, latent_ids, conv_kernel, style_one, bias_one, style_two, bias_two,
    rgb_weight, conv_bias, direction, length_target,
):
    zi = lax.axis_index("space")
    z = zi.reshape(1)
    mine = lax.dynamic_slice_in_dim(conv_kernel.reshape(9, 16, CH), zi * OC, OC, axis=2)
    kernel = lax.all_to_all(jnp.broadcast_to(mine[None], (NDP, 9, 16, OC)), "dp", 0, 0, tiled=True)
    marks = jnp.stack(thirds(direction.reshape(3, 256))).reshape(9, 256)
    message = jnp.concatenate([features.reshape(256, CH), jnp.pad(marks, ((0, 7), (0, 256)))], axis=0)
    others = ring(message, "space", 4)
    b1 = bias_one.reshape(1, CH)
    b2 = bias_two.reshape(1, CH)
    bias = conv_bias.reshape(1, CH)
    rgb = jnp.pad(rgb_weight.T, ((0, 5), (0, 0)))
    s, c = call(
        styles_kernel,
        (shape((1, CH), F32), shape((1, OC), F32)),
        [full(SMEM), full(SMEM), full(pl.ANY)] + [full()] * 4,
        16,
        [VMEM((1, CH), F32), pltpu.SemaphoreType.DMA],
    )(z, latent_ids, latent_bank, style_one, b1, style_two, b2)
    image, turned, marks_all, marks_turned = call(
        image_kernel,
        (shape((NPOS + 256, CH), BF16), shape((CH, NPOS + 256), BF16), shape((16, NPOS), BF16), shape((NPOS, OC), BF16)),
        [full(SMEM)] + [full()] * 4,
        24,
    )(z, message, *others)
    u, pre, ga, gm, energy, rows = call(
        first_kernel,
        (
            shape((1, CH), F32),
            shape((NPOS, OC), F32),
            shape((NPOS, OC), BF16),
            shape((3, CH, 3 * OC), BF16),
            shape((CH, OC), F32),
            shape((8, OC), F32),
        ),
        [full(SMEM)] + [full()] * 11,
        48,
    )(z, image, turned, marks_all, marks_turned, kernel, s, c, rgb, bias, style_one, style_two)
    parts, length = call(
        second_kernel,
        (shape((NDP, 10, 16, OC), BF16), shape((8, OC), F32)),
        [full(SMEM)] + [full()] * 18,
        48,
        [VMEM((8, CH), F32)],
    )(
        z, u, *ring(u, "space", 4), image, turned, marks_turned, kernel, s, rgb, bias, style_one, style_two,
        pre, ga, gm, energy, rows,
    )
    received = lax.all_to_all(parts, "dp", 0, 0, tiled=True)
    shard, target = call(
        sum_kernel,
        (shape((144, OC), BF16), shape((8, OC), F32)),
        [full(), full(SMEM)],
        16,
    )(received, length_target)
    kernel_grad = call(
        last_kernel,
        shape((144, CH), F32),
        [full(SMEM)] + [full()] * 4,
        16,
    )(z, shard, *ring(shard, "space", 4))
    return (kernel_grad.reshape(3, 3, 16, CH), length[0, 0:1], target[0, 0:1])


def solution(mesh):
    in_specs = (
        P("dp", "space", None, None),
        P(),
        P("dp"),
        P(None, None, "dp", None),
        P(),
        P(),
        P(),
        P(),
        P(),
        P(),
        P("dp", None, "space", None),
        P(),
    )
    out_specs = (P(None, None, "dp", None), P("dp"), P())
    return jax.shard_map(per_device, mesh=mesh, in_specs=in_specs, out_specs=out_specs, check_vma=False)
```

time: 312 us -> 91.3 us (0.29)
  waiting for transfers between devices: 156 us -> 33.6 us
  blocking collectives: 74.9 us -> 0 us
  other arithmetic: 31.2 us -> 1 us
  starting transfers between devices: 5.32 us -> 30.6 us
  matrix products: 23.2 us -> 0 us
  between operations: 19.4 us -> 2.11 us
  Pallas kernels: 0 us -> 14.9 us
  local copies, waits for them, and re-layouts: 2.12 us -> 8.55 us
    reduce_scatter x1 -> x0, waiting for transfers between devices: 77.7 us -> none  [per_device(): lax.psum_scatter(kernel_sum.astype(jnp.bfloat16), 'dp', scatter_dimension...]
    psum x2 -> x0, blocking collectives: 74.9 us -> none  [the longest x1 64.2 us: per_device(): total = lax.psum(jnp.sum(lengths), 'dp')]
    psum x1 -> x0, waiting for transfers between devices: 43.3 us -> none  [per_device(): kernel_grad = lax.psum(shard_sum, 'space').astype(jnp.float32)]
    all_gather x1 -> x0, waiting for transfers between devices: 33.8 us -> none  [per_device(): kernel_whole = lax.all_gather(conv_kernel, 'dp', axis=2, tiled=True)]
    dot_general x48 -> x0, matrix products: 23.2 us -> none  [the longest x36 12.3 us: synth(): jnp.dot(window, modulated[row_off, col_off], preferred_element_type=jnp.f...]
    all_to_all x0 -> x2, waiting for transfers between devices: none -> 19.3 us  [the longest x1 19.3 us: per_device(): received = lax.all_to_all(parts, 'dp', 0, 0, tiled=True)]
    pallas_call x0 -> x6, Pallas kernels: none -> 14.9 us  [the longest x1 7.14 us: per_device(): call(second_kernel, (shape((NDP, 10, 16, OC), BF16), shape((8, OC), F32))...]
    all_to_all x0 -> x2, starting transfers between devices: none -> 14.8 us  [the longest x1 7.55 us: per_device(): lax.all_to_all(jnp.broadcast_to(mine[None], (NDP, 9, 16, OC)), 'dp', 0, 0...]
  transfers between devices with their start and end apart: 5 -> 11, of which waited for: 3 -> 8; matrix products, arithmetic and copies ran while one was open for 4% -> 2% of each run, Pallas kernels for 0% -> 1%
where the time goes in v1:
time: 91.3 us; the launch traced here: 90.7 us
  waiting for transfers between devices  33.6 us (37%)
  starting transfers between devices  30.6 us (34%)
  Pallas kernels  14.9 us (16%)
  local copies, waits for them, and re-layouts  8.55 us (9%)
  between operations  2.11 us (2%)
  other arithmetic  1 us (1%)
    all_to_all x1, waiting for transfers between devices, per_device(): received = lax.all_to_all(parts, 'dp', 0, 0, tiled=True)  19.3 us
    ppermute x9, starting transfers between devices, ring(): lax.ppermute(x, axis, [(i, (i + k) % size) for i in range(size)])  15.7 us
    ppermute x9, waiting for transfers between devices, ring(): lax.ppermute(x, axis, [(i, (i + k) % size) for i in range(size)])  14.3 us
    all_to_all x1, starting transfers between devices, per_device(): lax.all_to_all(jnp.broadcast_to(mine[None], (NDP, 9, 16, OC)), 'dp', 0, 0...  7.55 us
    all_to_all x1, starting transfers between devices, per_device(): received = lax.all_to_all(parts, 'dp', 0, 0, tiled=True)  7.26 us
    pallas_call x1, Pallas kernels, per_device(): call(second_kernel, (shape((NDP, 10, 16, OC), BF16), shape((8, OC), F32))...  7.14 us
    unnamed x26, local copies, waits for them, and re-layouts  6.32 us
    pallas_call x1, Pallas kernels, per_device(): call(first_kernel, (shape((1, CH), F32), shape((NPOS, OC), F32), shape((N...  6.03 us
  transfers between devices with their start and end apart: 11, of which 8 were waited for; matrix products, arithmetic and copies ran while one was open for 2% of the time, Pallas kernels for 1%

profile of v1, /device:TPU:0, one launch (start us, length us, event | category | flops | bytes accessed | tf_op | source)
XLA Modules:
  0.0 90.7 jit_solution(8737818806683005687)
XLA Ops:
  0.6 0.0 copy-start
  0.6 0.9 copy-done
  1.6 1.2 %broadcast_in_dim.2 = bf16[32,9,16,128]{3,2,1,0:T(8,128)(2,1)} broadcast(bf16[9,16,128]{2,1,0:T(8,128)(2,1)S(1)} %constant_dynamic-slice_fusion), dimensions={1,2,3} | broadcast | bytes 1216512 | tf_op jit(solution)/shard_map/broadcast_in_dim | solution.py:287
  2.7 0.0 copy-start.9
  2.8 0.0 copy-start.10
  2.8 7.5 %all-to-all-start = ((bf16[32,9,16,128]{3,2,1,0:T(8,128)(2,1)}), bf16[32,9,16,128]{3,2,1,0:T(8,128)(2,1)S(1)}, u32[]{:S(2)}, u32[]{:S(2)}) async-start(bf16[32,9,16,128]{3,2,1,0:T(8,128)(2,1)} %broadcast_in_dim.2), calls=%async_computation | async-start | bytes 2359296 | tf_op jit(solution)/shard_map/all_to_all | solution.py:287
  10.3 0.0 copy-done.12
  10.4 1.0 %fusion.1.m0 = bf16[272,512]{1,0:T(8,128)(2,1)S(1)} fusion(bf16[9,256]{1,0:T(8,128)(2,1)S(1)} %reshape.82, bf16[256,512]{1,0:T(8,128)(2,1)} %bitcast.17), kind=kLoop, calls=%fused_computation.2 | loop fusion | flops 835584 | bytes 545280 | tf_op jit(solution)/shard_map/concatenate | solution.py:289
  11.4 2.0 %collective-permute-start = (bf16[272,512]{1,0:T(8,128)(2,1)S(1)}, bf16[272,512]{1,0:T(8,128)(2,1)S(1)}, u32[]{:S(2)}, u32[]{:S(2)}) collective-permute-start(bf16[272,512]{1,0:T(8,128)(2,1)S(1)} %fusion.1.m0), channel_id=1, source_target_pairs={{0,1},{1,2},{2,3},{3,0},{4,5},{5,6},{6,7},{7,4},{8,9},{9,10},{10,1... | collective-permute-start | bytes 835592 | tf_op jit(solution)/shard_map/ppermute | solution.py:271
  13.4 3.6 %collective-permute-start.1 = (bf16[272,512]{1,0:T(8,128)(2,1)S(1)}, bf16[272,512]{1,0:T(8,128)(2,1)S(1)}, u32[]{:S(2)}, u32[]{:S(2)}) collective-permute-start(bf16[272,512]{1,0:T(8,128)(2,1)S(1)} %fusion.1.m0), channel_id=1, source_target_pairs={{0,2},{1,3},{2,0},{3,1},{4,6},{5,7},{6,4},{7,5},{8,10},{9,11},{10,... | collective-permute-start | bytes 835592 | tf_op jit(solution)/shard_map/ppermute | solution.py:271
  16.9 1.0 %collective-permute-start.2 = (bf16[272,512]{1,0:T(8,128)(2,1)S(1)}, bf16[272,512]{1,0:T(8,128)(2,1)S(1)}, u32[]{:S(2)}, u32[]{:S(2)}) collective-permute-start(bf16[272,512]{1,0:T(8,128)(2,1)S(1)} %fusion.1.m0), channel_id=1, source_target_pairs={{0,3},{1,0},{2,1},{3,2},{4,7},{5,4},{6,5},{7,6},{8,11},{9,8},{10,9... | collective-permute-start | bytes 835592 | tf_op jit(solution)/shard_map/ppermute | solution.py:271
  18.6 0.0 copy-done.11
  18.6 0.0 copy-done.1
  18.6 0.0 copy-done.2
  18.7 0.0 copy-done.9
  18.7 0.0 copy-done.10
  18.7 0.0 copy-start.5
  18.7 1.6 %copy-done.5 = f32[1024,512]{1,0:T(8,128)S(1)} copy-done((f32[1024,512]{1,0:T(8,128)S(1)}, f32[1024,512]{1,0:T(8,128)}, u32[]{:S(2)}) %copy-start.5) | copy-done | bytes 2097176
  20.3 0.2 shard_map.140
  20.5 2.1 %collective-permute-done.m1 = bf16[272,512]{1,0:T(8,128)(2,1)S(1)} collective-permute-done((bf16[272,512]{1,0:T(8,128)(2,1)S(1)}, bf16[272,512]{1,0:T(8,128)(2,1)S(1)}, u32[]{:S(2)}, u32[]{:S(2)}) %collective-permute-start) | collective-permute-done | bytes 278560 | tf_op jit(solution)/shard_map/ppermute | solution.py:271
  22.6 7.1 %collective-permute-done.1.m2 = bf16[272,512]{1,0:T(8,128)(2,1)S(1)} collective-permute-done((bf16[272,512]{1,0:T(8,128)(2,1)S(1)}, bf16[272,512]{1,0:T(8,128)(2,1)S(1)}, u32[]{:S(2)}, u32[]{:S(2)}) %collective-permute-start.1) | collective-permute-done | bytes 278560 | tf_op jit(solution)/shard_map/ppermute | solution.py:271
  29.7 0.0 collective-permute-done.2.m3
  29.7 0.5 shard_map.139
  30.2 1.1 %copy-done.3 = bf16[1280,512]{1,0:T(8,128)(2,1)} copy-done((bf16[1280,512]{1,0:T(8,128)(2,1)}, bf16[1280,512]{1,0:T(8,128)(2,1)S(1)}, u32[]{:S(2)}) %copy-start.3) | copy-done | bytes 1310744
  31.3 1.1 %copy-done.4 = bf16[512,1280]{1,0:T(8,128)(2,1)} copy-done((bf16[512,1280]{1,0:T(8,128)(2,1)}, bf16[512,1280]{1,0:T(8,128)(2,1)S(1)}, u32[]{:S(2)}) %copy-start.4) | copy-done | bytes 1310744
  32.4 0.7 copy-done.6
  33.1 0.0 all-to-all-done.k_ref
  33.1 0.9 %copy-done.7 = bf16[1024,128]{1,0:T(8,128)(2,1)S(1)} copy-done((bf16[1024,128]{1,0:T(8,128)(2,1)S(1)}, bf16[1024,128]{1,0:T(8,128)(2,1)}, u32[]{:S(2)}) %copy-start.7) | copy-done | bytes 262168
  34.0 6.0 %shard_map.141 = (f32[1,512]{1,0:T(1,128)S(1)}, f32[1024,128]{1,0:T(8,128)S(1)}, bf16[1024,128]{1,0:T(8,128)(2,1)S(1)}, bf16[3,512,384]{2,1,0:T(8,128)(2,1)S(1)}...) custom-call(s32[1]{0:T(128)} %bitcast.z_ref, bf16[1280,512]{1,0:T(8,128)(2,1)} %copy-done.3, bf16[512,1280]{1,0:T(8,128)(2,1)} %copy-done.4, ...), custom_call_target="tpu_custom_call" | custom-call | tf_op jit(solution)/shard_map/pallas_call | solution.py:308
  40.1 1.3 %collective-permute-start.3 = (f32[1,512]{1,0:T(1,128)S(1)}, f32[1,512]{1,0:T(1,128)S(1)}, u32[]{:S(2)}, u32[]{:S(2)}) collective-permute-start(f32[1,512]{1,0:T(1,128)S(1)} %get-tuple-element.25.u0), channel_id=1, source_target_pairs={{0,1},{1,2},{2,3},{3,0},{4,5},{5,6},{6,7},{7,4},{8,9},{9,10},{10,1... | collective-permute-start | bytes 6152 | tf_op jit(solution)/shard_map/ppermute | solution.py:271
  41.4 2.4 %collective-permute-start.4 = (f32[1,512]{1,0:T(1,128)S(1)}, f32[1,512]{1,0:T(1,128)S(1)}, u32[]{:S(2)}, u32[]{:S(2)}) collective-permute-start(f32[1,512]{1,0:T(1,128)S(1)} %get-tuple-element.25.u0), channel_id=1, source_target_pairs={{0,2},{1,3},{2,0},{3,1},{4,6},{5,7},{6,4},{7,5},{8,10},{9,11},{10,... | collective-permute-start | bytes 6152 | tf_op jit(solution)/shard_map/ppermute | solution.py:271
  43.8 1.3 %collective-permute-start.5 = (f32[1,512]{1,0:T(1,128)S(1)}, f32[1,512]{1,0:T(1,128)S(1)}, u32[]{:S(2)}, u32[]{:S(2)}) collective-permute-start(f32[1,512]{1,0:T(1,128)S(1)} %get-tuple-element.25.u0), channel_id=1, source_target_pairs={{0,3},{1,0},{2,1},{3,2},{4,7},{5,4},{6,5},{7,6},{8,11},{9,8},{10,9... | collective-permute-start | bytes 6152 | tf_op jit(solution)/shard_map/ppermute | solution.py:271
  45.0 0.0 collective-permute-done.3.u1
  45.0 1.4 %collective-permute-done.4.u2 = f32[1,512]{1,0:T(1,128)S(1)} collective-permute-done((f32[1,512]{1,0:T(1,128)S(1)}, f32[1,512]{1,0:T(1,128)S(1)}, u32[]{:S(2)}, u32[]{:S(2)}) %collective-permute-start.4) | collective-permute-done | bytes 2080 | tf_op jit(solution)/shard_map/ppermute | solution.py:271
  46.5 0.9 collective-permute-done.5.u3
  47.4 7.1 %shard_map.142 = (bf16[32,10,16,128]{3,2,1,0:T(8,128)(2,1)}, f32[8,128]{1,0:T(8,128)S(1)}) custom-call(s32[1]{0:T(128)} %bitcast.z_ref, f32[1,512]{1,0:T(1,128)S(1)} %get-tuple-element.25.u0, f32[1,512]{1,0:T(1,128)S(1)} %collective-permute-done.3.u1, f32[1,512]{1,0:T(1,128)S(1)} %collective-permute-done.4.u2, f32[1,512]{1,0:T(1,128)S(1)} %collective-permute-done.5.u3, ...), custom_call_target="tpu_custom_call" | custom-call | tf_op jit(solution)/shard_map/pallas_call | solution.py:321
  54.5 7.3 %all-to-all-start.1 = ((bf16[32,10,16,128]{3,2,1,0:T(8,128)(2,1)}), bf16[32,10,16,128]{3,2,1,0:T(8,128)(2,1)S(1)}, u32[]{:S(2)}, u32[]{:S(2)}) async-start(bf16[32,10,16,128]{3,2,1,0:T(8,128)(2,1)} %get-tuple-element.31), calls=%async_computation.1 | async-start | bytes 2621440 | tf_op jit(solution)/shard_map/all_to_all | solution.py:331
  62.4 19.3 %all-to-all-done.1.part_ref = bf16[32,10,16,128]{3,2,1,0:T(8,128)(2,1)S(1)} async-done(((bf16[32,10,16,128]{3,2,1,0:T(8,128)(2,1)}), bf16[32,10,16,128]{3,2,1,0:T(8,128)(2,1)S(1)}, u32[]{:S(2)}, u32[]{:S(2)}) %all-to-all-start.1) | async-done | bytes 1310752 | tf_op jit(solution)/shard_map/all_to_all | solution.py:331
  81.7 0.3 shard_map.143
  82.0 0.5 collective-permute-start.6
  82.6 3.5 %collective-permute-start.7 = (bf16[144,128]{1,0:T(8,128)(2,1)S(1)}, bf16[144,128]{1,0:T(8,128)(2,1)S(1)}, u32[]{:S(2)}, u32[]{:S(2)}) collective-permute-start(bf16[144,128]{1,0:T(8,128)(2,1)S(1)} %get-tuple-element.32.p0), channel_id=1, source_target_pairs={{0,2},{1,3},{2,0},{3,1},{4,6},{5,7},{6,4},{7,5},{8,10},{9,11},{10,... | collective-permute-start | bytes 110600 | tf_op jit(solution)/shard_map/ppermute | solution.py:271
  86.0 0.2 collective-permute-start.8
  86.3 0.5 slice.6
  86.8 0.5 slice.7
  87.3 0.4 collective-permute-done.6.p1
  87.7 0.7 collective-permute-done.7.p2
  88.4 1.6 %collective-permute-done.8.p3 = bf16[144,128]{1,0:T(8,128)(2,1)S(1)} collective-permute-done((bf16[144,128]{1,0:T(8,128)(2,1)S(1)}, bf16[144,128]{1,0:T(8,128)(2,1)S(1)}, u32[]{:S(2)}, u32[]{:S(2)}) %collective-permute-start.8) | collective-permute-done | bytes 36896 | tf_op jit(solution)/shard_map/ppermute | solution.py:271
  90.0 0.8 shard_map.144
  (16 shorter events, 0.1 us)
Async XLA Ops:
  0.6 0.9 %copy-start = (bf16[3,3,16,512]{3,2,1,0:T(8,128)(2,1)S(1)}, bf16[3,3,16,512]{3,2,1,0:T(8,128)(2,1)}, u32[]{:S(2)}) copy-start(bf16[3,3,16,512]{3,2,1,0:T(8,128)(2,1)} %param.15) | copy-start | bytes 442372
  2.7 7.6 %copy-start.12 = (f32[1,3,2,128]{3,2,1,0:T(2,128)S(1)}, f32[1,3,2,128]{3,2,1,0:T(2,128)}, u32[]{:S(2)}) copy-start(f32[1,3,2,128]{3,2,1,0:T(2,128)} %param.22) | copy-start | bytes 9220
  2.7 15.9 %copy-start.11 = (f32[512,3]{0,1:T(4,128)S(1)}, f32[512,3]{0,1:T(4,128)}, u32[]{:S(2)}) copy-start(f32[512,3]{0,1:T(4,128)} %param.20) | copy-start | bytes 18436
  2.7 15.9 %copy-start.1 = (f32[512,512]{1,0:T(8,128)S(1)}, f32[512,512]{1,0:T(8,128)}, u32[]{:S(2)}) copy-start(f32[512,512]{1,0:T(8,128)} %w1_ref.5) | copy-start | bytes 3145732
  2.7 15.9 %copy-start.2 = (f32[512,512]{1,0:T(8,128)S(1)}, f32[512,512]{1,0:T(8,128)}, u32[]{:S(2)}) copy-start(f32[512,512]{1,0:T(8,128)} %w2_ref.5) | copy-start | bytes 3145732
  2.7 15.9 %copy-start.9 = (f32[512]{0:T(512)S(1)}, f32[512]{0:T(512)}, u32[]{:S(2)}) copy-start(f32[512]{0:T(512)} %param.17) | copy-start | bytes 6148
  2.8 15.9 %copy-start.10 = (f32[512]{0:T(512)S(1)}, f32[512]{0:T(512)}, u32[]{:S(2)}) copy-start(f32[512]{0:T(512)} %param.19) | copy-start | bytes 6148
  2.8 30.3 %all-to-all-start = ((bf16[32,9,16,128]{3,2,1,0:T(8,128)(2,1)}), bf16[32,9,16,128]{3,2,1,0:T(8,128)(2,1)S(1)}, u32[]{:S(2)}, u32[]{:S(2)}) async-start(bf16[32,9,16,128]{3,2,1,0:T(8,128)(2,1)} %broadcast_in_dim.2), calls=%async_computation | async-start | bytes 2359296 | tf_op jit(solution)/shard_map/all_to_all | solution.py:287
  11.4 11.2 %collective-permute-start = (bf16[272,512]{1,0:T(8,128)(2,1)S(1)}, bf16[272,512]{1,0:T(8,128)(2,1)S(1)}, u32[]{:S(2)}, u32[]{:S(2)}) collective-permute-start(bf16[272,512]{1,0:T(8,128)(2,1)S(1)} %fusion.1.m0), channel_id=1, source_target_pairs={{0,1},{1,2},{2,3},{3,0},{4,5},{5,6},{6,7},{7,4},{8,9},{9,10},{10,1... | collective-permute-start | bytes 835592 | tf_op jit(solution)/shard_map/ppermute | solution.py:271
  13.4 16.4 %collective-permute-start.1 = (bf16[272,512]{1,0:T(8,128)(2,1)S(1)}, bf16[272,512]{1,0:T(8,128)(2,1)S(1)}, u32[]{:S(2)}, u32[]{:S(2)}) collective-permute-start(bf16[272,512]{1,0:T(8,128)(2,1)S(1)} %fusion.1.m0), channel_id=1, source_target_pairs={{0,2},{1,3},{2,0},{3,1},{4,6},{5,7},{6,4},{7,5},{8,10},{9,11},{10,... | collective-permute-start | bytes 835592 | tf_op jit(solution)/shard_map/ppermute | solution.py:271
  16.9 12.8 %collective-permute-start.2 = (bf16[272,512]{1,0:T(8,128)(2,1)S(1)}, bf16[272,512]{1,0:T(8,128)(2,1)S(1)}, u32[]{:S(2)}, u32[]{:S(2)}) collective-permute-start(bf16[272,512]{1,0:T(8,128)(2,1)S(1)} %fusion.1.m0), channel_id=1, source_target_pairs={{0,3},{1,0},{2,1},{3,2},{4,7},{5,4},{6,5},{7,6},{8,11},{9,8},{10,9... | collective-permute-start | bytes 835592 | tf_op jit(solution)/shard_map/ppermute | solution.py:271
  18.7 1.6 %copy-start.5 = (f32[1024,512]{1,0:T(8,128)S(1)}, f32[1024,512]{1,0:T(8,128)}, u32[]{:S(2)}) copy-start(f32[1024,512]{1,0:T(8,128)} %bank_ref.1) | copy-start | bytes 6291460
  20.3 12.8 %copy-start.8 = (f32[512]{0:T(512)S(1)}, f32[512]{0:T(512)}, u32[]{:S(2)}) copy-start(f32[512]{0:T(512)} %param.21) | copy-start | bytes 6148
  30.2 1.1 %copy-start.3 = (bf16[1280,512]{1,0:T(8,128)(2,1)}, bf16[1280,512]{1,0:T(8,128)(2,1)S(1)}, u32[]{:S(2)}) copy-start(bf16[1280,512]{1,0:T(8,128)(2,1)S(1)} %get-tuple-element.19.f_ref) | copy-start | bytes 3932164
  31.3 1.1 %copy-start.4 = (bf16[512,1280]{1,0:T(8,128)(2,1)}, bf16[512,1280]{1,0:T(8,128)(2,1)S(1)}, u32[]{:S(2)}) copy-start(bf16[512,1280]{1,0:T(8,128)(2,1)S(1)} %get-tuple-element.20.ft_ref) | copy-start | bytes 3932164
  32.4 0.7 copy-start.6
  33.1 1.0 %copy-start.7 = (bf16[1024,128]{1,0:T(8,128)(2,1)S(1)}, bf16[1024,128]{1,0:T(8,128)(2,1)}, u32[]{:S(2)}) copy-start(bf16[1024,128]{1,0:T(8,128)(2,1)} %copy-done.6) | copy-start | bytes 786436
  40.1 5.0 %collective-permute-start.3 = (f32[1,512]{1,0:T(1,128)S(1)}, f32[1,512]{1,0:T(1,128)S(1)}, u32[]{:S(2)}, u32[]{:S(2)}) collective-permute-start(f32[1,512]{1,0:T(1,128)S(1)} %get-tuple-element.25.u0), channel_id=1, source_target_pairs={{0,1},{1,2},{2,3},{3,0},{4,5},{5,6},{6,7},{7,4},{8,9},{9,10},{10,1... | collective-permute-start | bytes 6152 | tf_op jit(solution)/shard_map/ppermute | solution.py:271
  41.4 5.1 %collective-permute-start.4 = (f32[1,512]{1,0:T(1,128)S(1)}, f32[1,512]{1,0:T(1,128)S(1)}, u32[]{:S(2)}, u32[]{:S(2)}) collective-permute-start(f32[1,512]{1,0:T(1,128)S(1)} %get-tuple-element.25.u0), channel_id=1, source_target_pairs={{0,2},{1,3},{2,0},{3,1},{4,6},{5,7},{6,4},{7,5},{8,10},{9,11},{10,... | collective-permute-start | bytes 6152 | tf_op jit(solution)/shard_map/ppermute | solution.py:271
  43.8 3.6 %collective-permute-start.5 = (f32[1,512]{1,0:T(1,128)S(1)}, f32[1,512]{1,0:T(1,128)S(1)}, u32[]{:S(2)}, u32[]{:S(2)}) collective-permute-start(f32[1,512]{1,0:T(1,128)S(1)} %get-tuple-element.25.u0), channel_id=1, source_target_pairs={{0,3},{1,0},{2,1},{3,2},{4,7},{5,4},{6,5},{7,6},{8,11},{9,8},{10,9... | collective-permute-start | bytes 6152 | tf_op jit(solution)/shard_map/ppermute | solution.py:271
  54.5 27.2 %all-to-all-start.1 = ((bf16[32,10,16,128]{3,2,1,0:T(8,128)(2,1)}), bf16[32,10,16,128]{3,2,1,0:T(8,128)(2,1)S(1)}, u32[]{:S(2)}, u32[]{:S(2)}) async-start(bf16[32,10,16,128]{3,2,1,0:T(8,128)(2,1)} %get-tuple-element.31), calls=%async_computation.1 | async-start | bytes 2621440 | tf_op jit(solution)/shard_map/all_to_all | solution.py:331
  82.0 5.6 %collective-permute-start.6 = (bf16[144,128]{1,0:T(8,128)(2,1)S(1)}, bf16[144,128]{1,0:T(8,128)(2,1)S(1)}, u32[]{:S(2)}, u32[]{:S(2)}) collective-permute-start(bf16[144,128]{1,0:T(8,128)(2,1)S(1)} %get-tuple-element.32.p0), channel_id=1, source_target_pairs={{0,1},{1,2},{2,3},{3,0},{4,5},{5,6},{6,7},{7,4},{8,9},{9,10},{10,1... | collective-permute-start | bytes 110600 | tf_op jit(solution)/shard_map/ppermute | solution.py:271
  82.6 5.8 %collective-permute-start.7 = (bf16[144,128]{1,0:T(8,128)(2,1)S(1)}, bf16[144,128]{1,0:T(8,128)(2,1)S(1)}, u32[]{:S(2)}, u32[]{:S(2)}) collective-permute-start(bf16[144,128]{1,0:T(8,128)(2,1)S(1)} %get-tuple-element.32.p0), channel_id=1, source_target_pairs={{0,2},{1,3},{2,0},{3,1},{4,6},{5,7},{6,4},{7,5},{8,10},{9,11},{10,... | collective-permute-start | bytes 110600 | tf_op jit(solution)/shard_map/ppermute | solution.py:271
  86.0 4.0 %collective-permute-start.8 = (bf16[144,128]{1,0:T(8,128)(2,1)S(1)}, bf16[144,128]{1,0:T(8,128)(2,1)S(1)}, u32[]{:S(2)}, u32[]{:S(2)}) collective-permute-start(bf16[144,128]{1,0:T(8,128)(2,1)S(1)} %get-tuple-element.32.p0), channel_id=1, source_target_pairs={{0,3},{1,0},{2,1},{3,2},{4,7},{5,4},{6,5},{7,6},{8,11},{9,8},{10,9... | collective-permute-start | bytes 110600 | tf_op jit(solution)/shard_map/ppermute | solution.py:271

commit v2 on v1

--- a/solution.py
+++ b/solution.py
@@ -57,14 +57,20 @@
     c_ref[...] = jnp.sum(w * w2_ref[:, mine], axis=0, keepdims=True) + b2_ref[:, mine]
 
 
-def image_kernel(z_ref, m0, m1, m2, m3, f_ref, ft_ref, d_ref, dt_ref):
-    z = z_ref[0]
+def image_kernel(z_ref, m0, m1, m2, m3, arrived, f_ref, ft_ref, d_ref, dt_ref, held, sems):
+    del arrived
+    z = z_ref[0]
+    copies = [pltpu.make_async_copy(m, held.at[k], sems.at[k]) for k, m in enumerate((m0, m1, m2, m3))]
+    for copy in copies:
+        copy.start()
     zero = jnp.zeros((COLS, CH), BF16)
     f_ref[0:COLS, :] = zero
     f_ref[NPOS + COLS :, :] = zero
     ft_ref[:, 0:COLS] = jnp.zeros((CH, COLS), BF16)
     ft_ref[:, NPOS + COLS :] = jnp.zeros((CH, COLS), BF16)
-    for k, m in enumerate((m0, m1, m2, m3)):
+    for k, copy in enumerate(copies):
+        copy.wait()
+        m = held.at[k]
         at = pl.multiple_of(lax.rem(z + 4 - k, 4) * 256, 256)
         feat = m[0:256, :]
         f_ref[pl.ds(at + COLS, 256), :] = feat
@@ -165,7 +171,7 @@
 def second_kernel(
     z_ref, u0, u1, u2, u3, f_ref, ft_ref, dt_ref, k_ref, s_ref, rgb_ref, bias_ref, w1_ref, w2_ref,
     pre_ref, ga_ref, gm_ref, e_ref, rows_ref,
-    out_ref, len_ref, u_buf,
+    out_ref, len_ref, u_buf, parts, sems,
 ):
     z = z_ref[0]
     lo = pl.multiple_of(z * OC, OC)
@@ -174,7 +180,20 @@
         u_buf[pl.ds(lax.rem(z + 4 - k, 4), 1), :] = u[...]
     grad = (u_buf[0:1, :] + u_buf[1:2, :]) + (u_buf[2:3, :] + u_buf[3:4, :])
     length = jnp.sqrt(jnp.sum(grad * grad, axis=1, keepdims=True) + 1e-08)
-    len_ref[...] = jnp.broadcast_to(length, (8, OC))
+    len_ref[0] = length[0, 0]
+    high = length.astype(BF16)
+    rest = length - high.astype(F32)
+    middle = rest.astype(BF16)
+    low = (rest - middle.astype(F32)).astype(BF16)
+    row = lax.broadcasted_iota(jnp.int32, (16, OC), 0)
+    pieces = jnp.where(row == 0, high.astype(F32), jnp.where(row == 1, middle.astype(F32), low.astype(F32)))
+    parts[:, 9] = jnp.broadcast_to(pieces.astype(BF16)[None], (NDP, 16, OC))
+    copies = []
+    for dy in range(3):
+        some = pl.ds(3 * dy, 3)
+        copies.append(pltpu.make_async_copy(parts.at[:, some], out_ref.at[:, some], sems.at[dy]))
+    copies.append(pltpu.make_async_copy(parts.at[:, pl.ds(9, 1)], out_ref.at[:, pl.ds(9, 1)], sems.at[3]))
+    copies[3].start()
     point = lanes_of(grad)
     ds = lanes_of(
         jnp.concatenate(
@@ -216,14 +235,10 @@
             t = 3 * dy + dx
             cut = slice(dx * OC, (dx + 1) * OC)
             value = gm2[:, cut] * sd + gm_ref[dy, :, cut].astype(F32) * dsd + tap(k_ref, t) * cot_e
-            out_ref[:, t] = value.astype(BF16).reshape(NDP, 16, OC)
-    high = length.astype(BF16)
-    rest = length - high.astype(F32)
-    middle = rest.astype(BF16)
-    low = (rest - middle.astype(F32)).astype(BF16)
-    row = lax.broadcasted_iota(jnp.int32, (16, OC), 0)
-    pieces = jnp.where(row == 0, high.astype(F32), jnp.where(row == 1, middle.astype(F32), low.astype(F32)))
-    out_ref[:, 9] = jnp.broadcast_to(pieces.astype(BF16)[None], (NDP, 16, OC))
+            parts[:, t] = value.astype(BF16).reshape(NDP, 16, OC)
+        copies[dy].start()
+    for copy in copies:
+        copy.wait()
 
 
 def sum_kernel(part_ref, target_ref, out_ref, new_ref):
@@ -236,7 +251,7 @@
         total = total + lengths[b]
     old = target_ref[0]
     target = old + PL_DECAY * (total / NDP - old)
-    new_ref[...] = jnp.broadcast_to(target, (8, OC))
+    new_ref[0] = target[0, 0]
     value = None
     for b in range(NDP):
         factor = 2.0 * PL_WEIGHT * (lengths[b] - target) / lengths[b]
@@ -256,12 +271,12 @@
     return jax.ShapeDtypeStruct(dims, kind)
 
 
-def call(kernel, outs, specs, mib, scratch=()):
+def call(kernel, outs, specs, mib, scratch=(), out_specs=None):
     return pl.pallas_call(
         kernel,
         out_shape=outs,
         in_specs=specs,
-        out_specs=jax.tree.map(lambda _: full(), outs),
+        out_specs=out_specs or jax.tree.map(lambda _: full(), outs),
         scratch_shapes=list(scratch),
         compiler_params=params(mib),
     )
@@ -295,16 +310,17 @@
     s, c = call(
         styles_kernel,
         (shape((1, CH), F32), shape((1, OC), F32)),
-        [full(SMEM), full(SMEM), full(pl.ANY)] + [full()] * 4,
-        16,
+        [full(SMEM), full(SMEM), full(pltpu.HBM)] + [full()] * 4,
+        8,
         [VMEM((1, CH), F32), pltpu.SemaphoreType.DMA],
-    )(z, latent_ids, latent_bank, style_one, b1, style_two, b2)
+    )(z, latent_ids, pltpu.with_memory_space_constraint(latent_bank, pltpu.HBM), style_one, b1, style_two, b2)
     image, turned, marks_all, marks_turned = call(
         image_kernel,
         (shape((NPOS + 256, CH), BF16), shape((CH, NPOS + 256), BF16), shape((16, NPOS), BF16), shape((NPOS, OC), BF16)),
-        [full(SMEM)] + [full()] * 4,
-        24,
-    )(z, message, *others)
+        [full(SMEM)] + [full(pltpu.HBM)] * 4 + [full(pl.ANY)],
+        16,
+        [VMEM((4, 272, CH), BF16), pltpu.SemaphoreType.DMA((4,))],
+    )(z, *[pltpu.with_memory_space_constraint(x, pltpu.HBM) for x in (message, *others)], kernel)
     u, pre, ga, gm, energy, rows = call(
         first_kernel,
         (
@@ -316,14 +332,15 @@
             shape((8, OC), F32),
         ),
         [full(SMEM)] + [full()] * 11,
-        48,
+        16,
     )(z, image, turned, marks_all, marks_turned, kernel, s, c, rgb, bias, style_one, style_two)
     parts, length = call(
         second_kernel,
-        (shape((NDP, 10, 16, OC), BF16), shape((8, OC), F32)),
+        (pltpu.HBM((NDP, 10, 16, OC), BF16), shape((1,), F32)),
         [full(SMEM)] + [full()] * 18,
-        48,
-        [VMEM((8, CH), F32)],
+        16,
+        [VMEM((8, CH), F32), VMEM((NDP, 10, 16, OC), BF16), pltpu.SemaphoreType.DMA((4,))],
+        (full(pltpu.HBM), full(SMEM)),
     )(
         z, u, *ring(u, "space", 4), image, turned, marks_turned, kernel, s, rgb, bias, style_one, style_two,
         pre, ga, gm, energy, rows,
@@ -331,9 +348,10 @@
     received = lax.all_to_all(parts, "dp", 0, 0, tiled=True)
     shard, target = call(
         sum_kernel,
-        (shape((144, OC), BF16), shape((8, OC), F32)),
+        (shape((144, OC), BF16), shape((1,), F32)),
         [full(), full(SMEM)],
-        16,
+        8,
+        out_specs=(full(), full(SMEM)),
     )(received, length_target)
     kernel_grad = call(
         last_kernel,
@@ -341,7 +359,7 @@
         [full(SMEM)] + [full()] * 4,
         16,
     )(z, shard, *ring(shard, "space", 4))
-    return (kernel_grad.reshape(3, 3, 16, CH), length[0, 0:1], target[0, 0:1])
+    return (kernel_grad.reshape(3, 3, 16, CH), length, target)
 
 
 def solution(mesh):

time: 91.3 us -> 85.9 us (0.941)
  local copies, waits for them, and re-layouts: 8.55 us -> 2.87 us
  waiting for transfers between devices: 33.6 us -> 35.8 us
    unnamed x26 -> x22, local copies, waits for them, and re-layouts: 6.32 us -> 1.65 us
    ppermute x9, waiting for transfers between devices: 14.3 us -> 16.5 us  [ring(): lax.ppermute(x, axis, [(i, (i + k) % size) for i in range(size)])]
    pallas_call x1, Pallas kernels: 6.03 us -> 4.35 us  [per_device(): call(first_kernel, (shape((1, CH), F32), shape((NPOS, OC), F32), shape((N...]
    pallas_call x1, Pallas kernels: 0.49 us -> 1.69 us  [per_device(): call(image_kernel, (shape((NPOS + 256, CH), BF16), shape((CH, NPOS + 256)...]
    pallas_call x2, Pallas kernels: 7.45 us -> 6.31 us  [the longest x1 5.7 us: per_device(): call(second_kernel, (pltpu.HBM((NDP, 10, 16, OC), BF16), shape((1,), F32)...]
    slice x2 -> x0, local copies, waits for them, and re-layouts: 1.02 us -> none  [per_device(): return (kernel_grad.reshape(3, 3, 16, CH), length[0, 0:1], target[0, 0:1])]
  transfers between devices with their start and end apart: 11 -> 11, of which waited for: 8 -> 8; matrix products, arithmetic and copies ran while one was open for 2% -> 1% of each run, Pallas kernels for 1% -> 1%
where the time goes in v2:
time: 85.9 us; the launch traced here: 85.5 us
  waiting for transfers between devices  35.8 us (42%)
  starting transfers between devices  29.7 us (35%)
  Pallas kernels  14 us (16%)
  local copies, waits for them, and re-layouts  2.87 us (3%)
  between operations  2.14 us (2%)
  other arithmetic  1 us (1%)
    all_to_all x1, waiting for transfers between devices, per_device(): received = lax.all_to_all(parts, 'dp', 0, 0, tiled=True)  19.3 us
    ppermute x9, waiting for transfers between devices, ring(): lax.ppermute(x, axis, [(i, (i + k) % size) for i in range(size)])  16.5 us
    ppermute x9, starting transfers between devices, ring(): lax.ppermute(x, axis, [(i, (i + k) % size) for i in range(size)])  15.6 us
    all_to_all x1, starting transfers between devices, per_device(): lax.all_to_all(jnp.broadcast_to(mine[None], (NDP, 9, 16, OC)), 'dp', 0, 0...  7.55 us
    all_to_all x1, starting transfers between devices, per_device(): received = lax.all_to_all(parts, 'dp', 0, 0, tiled=True)  6.55 us
    pallas_call x1, Pallas kernels, per_device(): call(second_kernel, (pltpu.HBM((NDP, 10, 16, OC), BF16), shape((1,), F32)...  5.7 us
    pallas_call x1, Pallas kernels, per_device(): call(first_kernel, (shape((1, CH), F32), shape((NPOS, OC), F32), shape((N...  4.35 us
  transfers between devices with their start and end apart: 11, of which 8 were waited for; matrix products, arithmetic and copies ran while one was open for 1% of the time, Pallas kernels for 1%

profile of v2, /device:TPU:0, one launch (start us, length us, event | category | flops | bytes accessed | tf_op | source)
XLA Modules:
  0.0 85.5 jit_solution(9929234292509822030)
XLA Ops:
  0.6 0.0 copy-start
  0.6 0.9 %copy-done = bf16[3,3,16,512]{3,2,1,0:T(8,128)(2,1)S(1)} copy-done((bf16[3,3,16,512]{3,2,1,0:T(8,128)(2,1)S(1)}, bf16[3,3,16,512]{3,2,1,0:T(8,128)(2,1)}, u32[]{:S(2)}) %copy-start) | copy-done | bytes 147480
  1.6 1.2 %broadcast_in_dim.2 = bf16[32,9,16,128]{3,2,1,0:T(8,128)(2,1)} broadcast(bf16[9,16,128]{2,1,0:T(8,128)(2,1)S(1)} %constant_dynamic-slice_fusion), dimensions={1,2,3} | broadcast | bytes 1216512 | tf_op jit(solution)/shard_map/broadcast_in_dim | solution.py:302
  2.7 0.0 copy-start.10
  2.7 0.0 copy-start.9
  2.7 0.0 copy-start.4
  2.8 0.0 copy-start.5
  2.8 7.5 %all-to-all-start = ((bf16[32,9,16,128]{3,2,1,0:T(8,128)(2,1)}), bf16[32,9,16,128]{3,2,1,0:T(8,128)(2,1)S(1)}, u32[]{:S(2)}, u32[]{:S(2)}) async-start(bf16[32,9,16,128]{3,2,1,0:T(8,128)(2,1)} %broadcast_in_dim.2), calls=%async_computation | async-start | bytes 2359296 | tf_op jit(solution)/shard_map/all_to_all | solution.py:302
  10.3 0.0 copy-done.10
  10.4 1.0 %fusion.1.m0 = bf16[272,512]{1,0:T(8,128)(2,1)S(1)} fusion(bf16[9,256]{1,0:T(8,128)(2,1)S(1)} %reshape.82, bf16[256,512]{1,0:T(8,128)(2,1)} %bitcast.15), kind=kLoop, calls=%fused_computation.2 | loop fusion | flops 835584 | bytes 545280 | tf_op jit(solution)/shard_map/concatenate | solution.py:304
  11.4 0.0 copy-start.6
  11.4 2.0 %collective-permute-start = (bf16[272,512]{1,0:T(8,128)(2,1)S(1)}, bf16[272,512]{1,0:T(8,128)(2,1)S(1)}, u32[]{:S(2)}, u32[]{:S(2)}) collective-permute-start(bf16[272,512]{1,0:T(8,128)(2,1)S(1)} %fusion.1.m0), channel_id=1, source_target_pairs={{0,1},{1,2},{2,3},{3,0},{4,5},{5,6},{6,7},{7,4},{8,9},{9,10},{10,1... | collective-permute-start | bytes 835592 | tf_op jit(solution)/shard_map/ppermute | solution.py:286
  13.4 3.6 %collective-permute-start.1 = (bf16[272,512]{1,0:T(8,128)(2,1)S(1)}, bf16[272,512]{1,0:T(8,128)(2,1)S(1)}, u32[]{:S(2)}, u32[]{:S(2)}) collective-permute-start(bf16[272,512]{1,0:T(8,128)(2,1)S(1)} %fusion.1.m0), channel_id=1, source_target_pairs={{0,2},{1,3},{2,0},{3,1},{4,6},{5,7},{6,4},{7,5},{8,10},{9,11},{10,... | collective-permute-start | bytes 835592 | tf_op jit(solution)/shard_map/ppermute | solution.py:286
  17.0 1.0 %collective-permute-start.2 = (bf16[272,512]{1,0:T(8,128)(2,1)S(1)}, bf16[272,512]{1,0:T(8,128)(2,1)}, u32[]{:S(2)}, u32[]{:S(2)}) collective-permute-start(bf16[272,512]{1,0:T(8,128)(2,1)S(1)} %fusion.1.m0), channel_id=1, source_target_pairs={{0,3},{1,0},{2,1},{3,2},{4,7},{5,4},{6,5},{7,6},{8,11},{9,8},{10,9... | collective-permute-start | bytes 835592 | tf_op jit(solution)/shard_map/ppermute | solution.py:286
  18.6 0.0 copy-done.9
  18.6 0.0 copy-done.1
  18.7 0.0 copy-done.2
  18.7 0.0 copy-done.4
  18.7 0.0 copy-done.5
  18.7 0.9 %shard_map.140 = (f32[1,512]{1,0:T(1,128)S(1)}, f32[1,128]{1,0:T(1,128)S(1)}) custom-call(s32[1]{0:T(128)} %bitcast.z_ref, s32[1]{0:T(128)S(6)} %copy.16.id_ref, f32[1024,512]{1,0:T(8,128)} %bank_ref.1, f32[512,512]{1,0:T(8,128)S(1)} %copy-done.1, f32[1,512]{1,0:T(1,128)S(1)} %bitcast.12, f32[512,512]{1,0:T(8,128)S(1)} %copy-done.2, f32[1,512]{1,0:T(1,128)S(1)} %bitcast.13), custom_call_target="tpu_custom_call" | custom-call | tf_op jit(solution)/shard_map/pallas_call | solution.py:310
  19.6 0.0 copy-done.6
  19.6 0.0 copy-start.3
  19.6 3.0 %collective-permute-done.m1 = bf16[272,512]{1,0:T(8,128)(2,1)S(1)} collective-permute-done((bf16[272,512]{1,0:T(8,128)(2,1)S(1)}, bf16[272,512]{1,0:T(8,128)(2,1)S(1)}, u32[]{:S(2)}, u32[]{:S(2)}) %collective-permute-start) | collective-permute-done | bytes 278560 | tf_op jit(solution)/shard_map/ppermute | solution.py:286
  22.6 7.1 %collective-permute-done.1.m2 = bf16[272,512]{1,0:T(8,128)(2,1)S(1)} collective-permute-done((bf16[272,512]{1,0:T(8,128)(2,1)S(1)}, bf16[272,512]{1,0:T(8,128)(2,1)S(1)}, u32[]{:S(2)}, u32[]{:S(2)}) %collective-permute-start.1) | collective-permute-done | bytes 278560 | tf_op jit(solution)/shard_map/ppermute | solution.py:286
  29.7 0.0 copy-done.7
  29.7 0.7 copy-done.8
  30.5 0.0 collective-permute-done.2.m3
  30.5 0.0 all-to-all-done.arrived.k_ref
  30.5 1.7 %shard_map.139 = (bf16[1280,512]{1,0:T(8,128)(2,1)S(1)}, bf16[512,1280]{1,0:T(8,128)(2,1)S(1)}, bf16[16,1024]{1,0:T(8,128)(2,1)S(1)}, bf16[1024,128]{1,0:T(8,128)(2,1)S(1)}) custom-call(s32[1]{0:T(128)} %bitcast.z_ref, bf16[272,512]{1,0:T(8,128)(2,1)} %copy-done.6, bf16[272,512]{1,0:T(8,128)(2,1)} %copy-done.7, bf16[272,512]{1,0:T(8,128)(2,1)} %copy-done.8, ...), custom_call_target="tpu_custom_call" | custom-call | tf_op jit(solution)/shard_map/pallas_call | solution.py:317
  32.2 0.0 copy-done.3
  32.2 4.3 %shard_map.141 = (f32[1,512]{1,0:T(1,128)S(1)}, f32[1024,128]{1,0:T(8,128)S(1)}, bf16[1024,128]{1,0:T(8,128)(2,1)S(1)}, bf16[3,512,384]{2,1,0:T(8,128)(2,1)S(1)}...) custom-call(s32[1]{0:T(128)} %bitcast.z_ref, bf16[1280,512]{1,0:T(8,128)(2,1)S(1)} %get-tuple-element.19.f_ref, ...), custom_call_target="tpu_custom_call" | custom-call | tf_op jit(solution)/shard_map/pallas_call | solution.py:324
  36.5 0.7 collective-permute-start.3
  37.2 3.1 %collective-permute-start.4 = (f32[1,512]{1,0:T(1,128)S(1)}, f32[1,512]{1,0:T(1,128)S(1)}, u32[]{:S(2)}, u32[]{:S(2)}) collective-permute-start(f32[1,512]{1,0:T(1,128)S(1)} %get-tuple-element.25.u0), channel_id=1, source_target_pairs={{0,2},{1,3},{2,0},{3,1},{4,6},{5,7},{6,4},{7,5},{8,10},{9,11},{10,... | collective-permute-start | bytes 6152 | tf_op jit(solution)/shard_map/ppermute | solution.py:286
  40.3 1.0 %collective-permute-start.5 = (f32[1,512]{1,0:T(1,128)S(1)}, f32[1,512]{1,0:T(1,128)S(1)}, u32[]{:S(2)}, u32[]{:S(2)}) collective-permute-start(f32[1,512]{1,0:T(1,128)S(1)} %get-tuple-element.25.u0), channel_id=1, source_target_pairs={{0,3},{1,0},{2,1},{3,2},{4,7},{5,4},{6,5},{7,6},{8,11},{9,8},{10,9... | collective-permute-start | bytes 6152 | tf_op jit(solution)/shard_map/ppermute | solution.py:286
  41.3 0.0 collective-permute-done.3.u1
  41.4 0.9 %collective-permute-done.4.u2 = f32[1,512]{1,0:T(1,128)S(1)} collective-permute-done((f32[1,512]{1,0:T(1,128)S(1)}, f32[1,512]{1,0:T(1,128)S(1)}, u32[]{:S(2)}, u32[]{:S(2)}) %collective-permute-start.4) | collective-permute-done | bytes 2080 | tf_op jit(solution)/shard_map/ppermute | solution.py:286
  42.3 1.6 %collective-permute-done.5.u3 = f32[1,512]{1,0:T(1,128)S(1)} collective-permute-done((f32[1,512]{1,0:T(1,128)S(1)}, f32[1,512]{1,0:T(1,128)S(1)}, u32[]{:S(2)}, u32[]{:S(2)}) %collective-permute-start.5) | collective-permute-done | bytes 2080 | tf_op jit(solution)/shard_map/ppermute | solution.py:286
  43.9 5.7 %shard_map.142 = (bf16[32,10,16,128]{3,2,1,0:T(8,128)(2,1)}, f32[1]{0:T(128)}) custom-call(s32[1]{0:T(128)} %bitcast.z_ref, f32[1,512]{1,0:T(1,128)S(1)} %get-tuple-element.25.u0, f32[1,512]{1,0:T(1,128)S(1)} %collective-permute-done.3.u1, f32[1,512]{1,0:T(1,128)S(1)} %collective-permute-done.4.u2, f32[1,512]{1,0:T(1,128)S(1)} %collective-permute-done.5.u3, ...), custom_call_target="tpu_custom_call" | custom-call | tf_op jit(solution)/shard_map/pallas_call | solution.py:337
  49.6 6.6 %all-to-all-start.1 = ((bf16[32,10,16,128]{3,2,1,0:T(8,128)(2,1)}), bf16[32,10,16,128]{3,2,1,0:T(8,128)(2,1)S(1)}, u32[]{:S(2)}, u32[]{:S(2)}) async-start(bf16[32,10,16,128]{3,2,1,0:T(8,128)(2,1)} %get-tuple-element.31), calls=%async_computation.1 | async-start | bytes 2621440 | tf_op jit(solution)/shard_map/all_to_all | solution.py:348
  56.8 19.3 %all-to-all-done.1.part_ref = bf16[32,10,16,128]{3,2,1,0:T(8,128)(2,1)S(1)} async-done(((bf16[32,10,16,128]{3,2,1,0:T(8,128)(2,1)}), bf16[32,10,16,128]{3,2,1,0:T(8,128)(2,1)S(1)}, u32[]{:S(2)}, u32[]{:S(2)}) %all-to-all-start.1) | async-done | bytes 1310752 | tf_op jit(solution)/shard_map/all_to_all | solution.py:348
  76.1 0.6 shard_map.143
  76.7 1.2 %collective-permute-start.6 = (bf16[144,128]{1,0:T(8,128)(2,1)S(1)}, bf16[144,128]{1,0:T(8,128)(2,1)S(1)}, u32[]{:S(2)}, u32[]{:S(2)}) collective-permute-start(bf16[144,128]{1,0:T(8,128)(2,1)S(1)} %get-tuple-element.32.p0), channel_id=1, source_target_pairs={{0,1},{1,2},{2,3},{3,0},{4,5},{5,6},{6,7},{7,4},{8,9},{9,10},{10,1... | collective-permute-start | bytes 110600 | tf_op jit(solution)/shard_map/ppermute | solution.py:286
  77.9 2.8 %collective-permute-start.7 = (bf16[144,128]{1,0:T(8,128)(2,1)S(1)}, bf16[144,128]{1,0:T(8,128)(2,1)S(1)}, u32[]{:S(2)}, u32[]{:S(2)}) collective-permute-start(bf16[144,128]{1,0:T(8,128)(2,1)S(1)} %get-tuple-element.32.p0), channel_id=1, source_target_pairs={{0,2},{1,3},{2,0},{3,1},{4,6},{5,7},{6,4},{7,5},{8,10},{9,11},{10,... | collective-permute-start | bytes 110600 | tf_op jit(solution)/shard_map/ppermute | solution.py:286
  80.7 0.2 collective-permute-start.8
  81.0 1.4 %collective-permute-done.6.p1 = bf16[144,128]{1,0:T(8,128)(2,1)S(1)} collective-permute-done((bf16[144,128]{1,0:T(8,128)(2,1)S(1)}, bf16[144,128]{1,0:T(8,128)(2,1)S(1)}, u32[]{:S(2)}, u32[]{:S(2)}) %collective-permute-start.6) | collective-permute-done | bytes 36896 | tf_op jit(solution)/shard_map/ppermute | solution.py:286
  82.4 1.0 %collective-permute-done.7.p2 = bf16[144,128]{1,0:T(8,128)(2,1)S(1)} collective-permute-done((bf16[144,128]{1,0:T(8,128)(2,1)S(1)}, bf16[144,128]{1,0:T(8,128)(2,1)S(1)}, u32[]{:S(2)}, u32[]{:S(2)}) %collective-permute-start.7) | collective-permute-done | bytes 36896 | tf_op jit(solution)/shard_map/ppermute | solution.py:286
  83.4 1.3 %collective-permute-done.8.p3 = bf16[144,128]{1,0:T(8,128)(2,1)S(1)} collective-permute-done((bf16[144,128]{1,0:T(8,128)(2,1)S(1)}, bf16[144,128]{1,0:T(8,128)(2,1)S(1)}, u32[]{:S(2)}, u32[]{:S(2)}) %collective-permute-start.8) | collective-permute-done | bytes 36896 | tf_op jit(solution)/shard_map/ppermute | solution.py:286
  84.7 0.8 shard_map.144
  (10 shorter events, 0.1 us)
Async XLA Ops:
  0.6 0.9 %copy-start = (bf16[3,3,16,512]{3,2,1,0:T(8,128)(2,1)S(1)}, bf16[3,3,16,512]{3,2,1,0:T(8,128)(2,1)}, u32[]{:S(2)}) copy-start(bf16[3,3,16,512]{3,2,1,0:T(8,128)(2,1)} %param.15) | copy-start | bytes 442372
  2.7 7.6 %copy-start.10 = (f32[1,3,2,128]{3,2,1,0:T(2,128)S(1)}, f32[1,3,2,128]{3,2,1,0:T(2,128)}, u32[]{:S(2)}) copy-start(f32[1,3,2,128]{3,2,1,0:T(2,128)} %param.22) | copy-start | bytes 9220
  2.7 15.9 %copy-start.9 = (f32[512,3]{0,1:T(4,128)S(1)}, f32[512,3]{0,1:T(4,128)}, u32[]{:S(2)}) copy-start(f32[512,3]{0,1:T(4,128)} %param.20) | copy-start | bytes 18436
  2.7 15.9 %copy-start.1 = (f32[512,512]{1,0:T(8,128)S(1)}, f32[512,512]{1,0:T(8,128)}, u32[]{:S(2)}) copy-start(f32[512,512]{1,0:T(8,128)} %w1_ref.5) | copy-start | bytes 3145732
  2.7 15.9 %copy-start.2 = (f32[512,512]{1,0:T(8,128)S(1)}, f32[512,512]{1,0:T(8,128)}, u32[]{:S(2)}) copy-start(f32[512,512]{1,0:T(8,128)} %w2_ref.5) | copy-start | bytes 3145732
  2.7 15.9 %copy-start.4 = (f32[512]{0:T(512)S(1)}, f32[512]{0:T(512)}, u32[]{:S(2)}) copy-start(f32[512]{0:T(512)} %param.17) | copy-start | bytes 6148
  2.8 15.9 %copy-start.5 = (f32[512]{0:T(512)S(1)}, f32[512]{0:T(512)}, u32[]{:S(2)}) copy-start(f32[512]{0:T(512)} %param.19) | copy-start | bytes 6148
  2.8 27.7 %all-to-all-start = ((bf16[32,9,16,128]{3,2,1,0:T(8,128)(2,1)}), bf16[32,9,16,128]{3,2,1,0:T(8,128)(2,1)S(1)}, u32[]{:S(2)}, u32[]{:S(2)}) async-start(bf16[32,9,16,128]{3,2,1,0:T(8,128)(2,1)} %broadcast_in_dim.2), calls=%async_computation | async-start | bytes 2359296 | tf_op jit(solution)/shard_map/all_to_all | solution.py:302
  11.4 8.2 %copy-start.6 = (bf16[272,512]{1,0:T(8,128)(2,1)}, bf16[272,512]{1,0:T(8,128)(2,1)S(1)}, u32[]{:S(2)}) copy-start(bf16[272,512]{1,0:T(8,128)(2,1)S(1)} %fusion.1.m0) | copy-start | bytes 835588
  11.4 11.2 %collective-permute-start = (bf16[272,512]{1,0:T(8,128)(2,1)S(1)}, bf16[272,512]{1,0:T(8,128)(2,1)S(1)}, u32[]{:S(2)}, u32[]{:S(2)}) collective-permute-start(bf16[272,512]{1,0:T(8,128)(2,1)S(1)} %fusion.1.m0), channel_id=1, source_target_pairs={{0,1},{1,2},{2,3},{3,0},{4,5},{5,6},{6,7},{7,4},{8,9},{9,10},{10,1... | collective-permute-start | bytes 835592 | tf_op jit(solution)/shard_map/ppermute | solution.py:286
  13.4 16.4 %collective-permute-start.1 = (bf16[272,512]{1,0:T(8,128)(2,1)S(1)}, bf16[272,512]{1,0:T(8,128)(2,1)S(1)}, u32[]{:S(2)}, u32[]{:S(2)}) collective-permute-start(bf16[272,512]{1,0:T(8,128)(2,1)S(1)} %fusion.1.m0), channel_id=1, source_target_pairs={{0,2},{1,3},{2,0},{3,1},{4,6},{5,7},{6,4},{7,5},{8,10},{9,11},{10,... | collective-permute-start | bytes 835592 | tf_op jit(solution)/shard_map/ppermute | solution.py:286
  17.0 13.5 %collective-permute-start.2 = (bf16[272,512]{1,0:T(8,128)(2,1)S(1)}, bf16[272,512]{1,0:T(8,128)(2,1)}, u32[]{:S(2)}, u32[]{:S(2)}) collective-permute-start(bf16[272,512]{1,0:T(8,128)(2,1)S(1)} %fusion.1.m0), channel_id=1, source_target_pairs={{0,3},{1,0},{2,1},{3,2},{4,7},{5,4},{6,5},{7,6},{8,11},{9,8},{10,9... | collective-permute-start | bytes 835592 | tf_op jit(solution)/shard_map/ppermute | solution.py:286
  19.6 12.6 %copy-start.3 = (f32[512]{0:T(512)S(1)}, f32[512]{0:T(512)}, u32[]{:S(2)}) copy-start(f32[512]{0:T(512)} %param.21) | copy-start | bytes 6148
  22.6 7.1 %copy-start.7 = (bf16[272,512]{1,0:T(8,128)(2,1)}, bf16[272,512]{1,0:T(8,128)(2,1)S(1)}, u32[]{:S(2)}) copy-start(bf16[272,512]{1,0:T(8,128)(2,1)S(1)} %collective-permute-done.m1) | copy-start | bytes 835588
  29.7 0.7 copy-start.8
  36.5 4.9 %collective-permute-start.3 = (f32[1,512]{1,0:T(1,128)S(1)}, f32[1,512]{1,0:T(1,128)S(1)}, u32[]{:S(2)}, u32[]{:S(2)}) collective-permute-start(f32[1,512]{1,0:T(1,128)S(1)} %get-tuple-element.25.u0), channel_id=1, source_target_pairs={{0,1},{1,2},{2,3},{3,0},{4,5},{5,6},{6,7},{7,4},{8,9},{9,10},{10,1... | collective-permute-start | bytes 6152 | tf_op jit(solution)/shard_map/ppermute | solution.py:286
  37.2 5.1 %collective-permute-start.4 = (f32[1,512]{1,0:T(1,128)S(1)}, f32[1,512]{1,0:T(1,128)S(1)}, u32[]{:S(2)}, u32[]{:S(2)}) collective-permute-start(f32[1,512]{1,0:T(1,128)S(1)} %get-tuple-element.25.u0), channel_id=1, source_target_pairs={{0,2},{1,3},{2,0},{3,1},{4,6},{5,7},{6,4},{7,5},{8,10},{9,11},{10,... | collective-permute-start | bytes 6152 | tf_op jit(solution)/shard_map/ppermute | solution.py:286
  40.3 3.6 %collective-permute-start.5 = (f32[1,512]{1,0:T(1,128)S(1)}, f32[1,512]{1,0:T(1,128)S(1)}, u32[]{:S(2)}, u32[]{:S(2)}) collective-permute-start(f32[1,512]{1,0:T(1,128)S(1)} %get-tuple-element.25.u0), channel_id=1, source_target_pairs={{0,3},{1,0},{2,1},{3,2},{4,7},{5,4},{6,5},{7,6},{8,11},{9,8},{10,9... | collective-permute-start | bytes 6152 | tf_op jit(solution)/shard_map/ppermute | solution.py:286
  49.6 26.5 %all-to-all-start.1 = ((bf16[32,10,16,128]{3,2,1,0:T(8,128)(2,1)}), bf16[32,10,16,128]{3,2,1,0:T(8,128)(2,1)S(1)}, u32[]{:S(2)}, u32[]{:S(2)}) async-start(bf16[32,10,16,128]{3,2,1,0:T(8,128)(2,1)} %get-tuple-element.31), calls=%async_computation.1 | async-start | bytes 2621440 | tf_op jit(solution)/shard_map/all_to_all | solution.py:348
  76.7 5.6 %collective-permute-start.6 = (bf16[144,128]{1,0:T(8,128)(2,1)S(1)}, bf16[144,128]{1,0:T(8,128)(2,1)S(1)}, u32[]{:S(2)}, u32[]{:S(2)}) collective-permute-start(bf16[144,128]{1,0:T(8,128)(2,1)S(1)} %get-tuple-element.32.p0), channel_id=1, source_target_pairs={{0,1},{1,2},{2,3},{3,0},{4,5},{5,6},{6,7},{7,4},{8,9},{9,10},{10,1... | collective-permute-start | bytes 110600 | tf_op jit(solution)/shard_map/ppermute | solution.py:286
  77.9 5.5 %collective-permute-start.7 = (bf16[144,128]{1,0:T(8,128)(2,1)S(1)}, bf16[144,128]{1,0:T(8,128)(2,1)S(1)}, u32[]{:S(2)}, u32[]{:S(2)}) collective-permute-start(bf16[144,128]{1,0:T(8,128)(2,1)S(1)} %get-tuple-element.32.p0), channel_id=1, source_target_pairs={{0,2},{1,3},{2,0},{3,1},{4,6},{5,7},{6,4},{7,5},{8,10},{9,11},{10,... | collective-permute-start | bytes 110600 | tf_op jit(solution)/shard_map/ppermute | solution.py:286
  80.7 4.0 %collective-permute-start.8 = (bf16[144,128]{1,0:T(8,128)(2,1)S(1)}, bf16[144,128]{1,0:T(8,128)(2,1)S(1)}, u32[]{:S(2)}, u32[]{:S(2)}) collective-permute-start(bf16[144,128]{1,0:T(8,128)(2,1)S(1)} %get-tuple-element.32.p0), channel_id=1, source_target_pairs={{0,3},{1,0},{2,1},{3,2},{4,7},{5,4},{6,5},{7,6},{8,11},{9,8},{10,9... | collective-permute-start | bytes 110600 | tf_op jit(solution)/shard_map/ppermute | solution.py:286

commit v3 on v2

--- a/solution.py
+++ b/solution.py
@@ -57,24 +57,13 @@
     c_ref[...] = jnp.sum(w * w2_ref[:, mine], axis=0, keepdims=True) + b2_ref[:, mine]
 
 
-def image_kernel(z_ref, m0, m1, m2, m3, arrived, f_ref, ft_ref, d_ref, dt_ref, held, sems):
-    del arrived
+def image_kernel(z_ref, m0, m1, m2, m3, f_ref, ft_ref, d_ref, dt_ref):
     z = z_ref[0]
-    copies = [pltpu.make_async_copy(m, held.at[k], sems.at[k]) for k, m in enumerate((m0, m1, m2, m3))]
-    for copy in copies:
-        copy.start()
-    zero = jnp.zeros((COLS, CH), BF16)
-    f_ref[0:COLS, :] = zero
-    f_ref[NPOS + COLS :, :] = zero
-    ft_ref[:, 0:COLS] = jnp.zeros((CH, COLS), BF16)
-    ft_ref[:, NPOS + COLS :] = jnp.zeros((CH, COLS), BF16)
-    for k, copy in enumerate(copies):
-        copy.wait()
-        m = held.at[k]
+    for k, m in enumerate((m0, m1, m2, m3)):
         at = pl.multiple_of(lax.rem(z + 4 - k, 4) * 256, 256)
         feat = m[0:256, :]
-        f_ref[pl.ds(at + COLS, 256), :] = feat
-        ft_ref[:, pl.ds(at + COLS, 256)] = jnp.transpose(feat)
+        f_ref[pl.ds(at, 256), :] = feat
+        ft_ref[:, pl.ds(at, 256)] = jnp.transpose(feat)
         part = m[256:272, 0:256]
         d_ref[:, pl.ds(at, 256)] = part
         wide = jnp.concatenate([part.astype(F32), jnp.zeros((112, 256), F32)], axis=0)
@@ -97,16 +86,24 @@
     return k_ref[:, t].reshape(CH, OC).astype(F32)
 
 
-def conv(f_ref, mod_of):
-    total = None
-    for dy in range(3):
-        part = dot(f_ref[dy * COLS : dy * COLS + NPOS, :], mod_of(dy))
-        total = part if total is None else total + part
+def from_above(x):
+    return jnp.concatenate([jnp.zeros((COLS, x.shape[1]), x.dtype), x[: NPOS - COLS]], axis=0)
+
+
+def from_below(x):
+    return jnp.concatenate([x[COLS:], jnp.zeros((COLS, x.shape[1]), x.dtype)], axis=0)
+
+
+def conv(f_ref, mod):
+    every = dot(f_ref[...], mod)
+    wide = 3 * OC
+    total = from_above(every[:, :wide]) + every[:, wide : 2 * wide] + from_below(every[:, 2 * wide :])
     return from_left(total[:, 0:OC]) + total[:, OC : 2 * OC] + from_right(total[:, 2 * OC :])
 
 
 def spread(h):
-    return jnp.concatenate([from_right(h), h, from_left(h)], axis=1).astype(BF16)
+    row = jnp.concatenate([from_right(h), h, from_left(h)], axis=1).astype(BF16)
+    return jnp.concatenate([from_below(row), row, from_above(row)], axis=1)
 
 
 def colours_of(rgb_ref, colour, z):
@@ -117,12 +114,18 @@
 
 
 def first_kernel(
-    z_ref, f_ref, ft_ref, d_ref, dt_ref, k_ref, s_ref, c_ref, rgb_ref, bias_ref, w1_ref, w2_ref,
-    u_ref, pre_ref, ga_ref, gm_ref, e_ref, rows_ref,
+    z_ref, p_ref, f_ref, ft_ref, d_ref, dt_ref, k0_ref, k1_ref, s_ref, c_ref, rgb_ref, bias_ref, w1_ref, w2_ref,
+    k_ref, u_ref, pre_ref, ga_ref, gm_ref, e_ref, rows_ref,
 ):
     z = z_ref[0]
     lo = pl.multiple_of(z * OC, OC)
     scaling = 1.0 / math.sqrt(NPOS)
+    core = lax.rem(p_ref[0], 2)
+    for x in range(4):
+        for y in range(4):
+            chip = 8 * x + 2 * y
+            k_ref[chip + core] = k0_ref[x, y]
+            k_ref[chip + 1 - core] = k1_ref[x, y]
     energy = None
     for t in range(9):
         k = tap(k_ref, t)
@@ -132,10 +135,8 @@
     demod = lax.rsqrt(jnp.sum(s * s * energy, axis=0, keepdims=True) + 1e-08)
     sd = s * demod
 
-    def mod_of(dy):
-        return jnp.concatenate([(tap(k_ref, 3 * dy + dx) * sd).astype(BF16) for dx in range(3)], axis=1)
-
-    bare = conv(f_ref, mod_of)
+    mod = jnp.concatenate([(tap(k_ref, t) * sd).astype(BF16) for t in range(9)], axis=1)
+    bare = conv(f_ref, mod)
     pre = bare + bias_ref[:, pl.ds(lo, OC)]
     pre_ref[...] = pre
     square = pre * pre + 0.25
@@ -153,7 +154,7 @@
     hs = spread(h)
     along = None
     for dy in range(3):
-        gm = dot(ft_ref[:, dy * COLS : dy * COLS + NPOS], hs).astype(BF16)
+        gm = dot(ft_ref[...], hs[:, 3 * OC * dy : 3 * OC * (dy + 1)]).astype(BF16)
         gm_ref[dy] = gm
         gm = gm.astype(F32)
         for dx in range(3):
@@ -180,7 +181,7 @@
         u_buf[pl.ds(lax.rem(z + 4 - k, 4), 1), :] = u[...]
     grad = (u_buf[0:1, :] + u_buf[1:2, :]) + (u_buf[2:3, :] + u_buf[3:4, :])
     length = jnp.sqrt(jnp.sum(grad * grad, axis=1, keepdims=True) + 1e-08)
-    len_ref[0] = length[0, 0]
+    len_ref[...] = jnp.broadcast_to(length, (8, OC))
     high = length.astype(BF16)
     rest = length - high.astype(F32)
     middle = rest.astype(BF16)
@@ -211,10 +212,8 @@
     sd = s * demod
     dsd = ds * demod + s * dd
 
-    def mod_of(dy):
-        return jnp.concatenate([(tap(k_ref, 3 * dy + dx) * dsd).astype(BF16) for dx in range(3)], axis=1)
-
-    dpre = conv(f_ref, mod_of)
+    mod = jnp.concatenate([(tap(k_ref, t) * dsd).astype(BF16) for t in range(9)], axis=1)
+    dpre = conv(f_ref, mod)
     pre = pre_ref[...]
     root = lax.rsqrt(pre * pre + 0.25)
     slope = (0.6 + 0.4 * (pre * root)) * SQRT_TWO
@@ -230,7 +229,7 @@
     cot_e = 2.0 * s * (cot_q * s + 2.0 * cot_dq * ds)
     hs = spread(h2)
     for dy in range(3):
-        gm2 = dot(ft_ref[:, dy * COLS : dy * COLS + NPOS], hs)
+        gm2 = dot(ft_ref[...], hs[:, 3 * OC * dy : 3 * OC * (dy + 1)])
         for dx in range(3):
             t = 3 * dy + dx
             cut = slice(dx * OC, (dx + 1) * OC)
@@ -251,7 +250,7 @@
         total = total + lengths[b]
     old = target_ref[0]
     target = old + PL_DECAY * (total / NDP - old)
-    new_ref[0] = target[0, 0]
+    new_ref[...] = jnp.broadcast_to(target, (8, OC))
     value = None
     for b in range(NDP):
         factor = 2.0 * PL_WEIGHT * (lengths[b] - target) / lengths[b]
@@ -286,10 +285,54 @@
     return [lax.ppermute(x, axis, [(i, (i + k) % size) for i in range(size)]) for k in range(1, size)]
 
 
-def thirds(x):
-    high = lax.reduce_precision(x, 8, 7)
-    middle = lax.reduce_precision(x - high, 8, 7)
-    return [high.astype(BF16), middle.astype(BF16), ((x - high) - middle).astype(BF16)]
+def place(x, y, c):
+    return ((x % 4) * 4 + y % 4) * 2 + c % 2
+
+
+def permuted(value, to):
+    return [
+        lax.ppermute(
+            value, "dp", [(place(x, y, c), place(*to(x, y, c, k))) for x in range(4) for y in range(4) for c in range(2)]
+        )
+        for k in range(1, 4)
+    ]
+
+
+def pack_kernel(z_ref, f_ref, d_hbm, k_ref, message_ref, mine_ref, d_ref, sems):
+    lo = pl.multiple_of(z_ref[0] * OC, OC)
+    copies = [
+        pltpu.make_async_copy(f_ref, message_ref.at[pl.ds(0, 256)], sems.at[0]),
+        pltpu.make_async_copy(k_ref.at[:, :, pl.ds(lo, OC)], mine_ref, sems.at[1]),
+    ]
+    marks = pltpu.make_async_copy(d_hbm, d_ref, sems.at[2])
+    marks.start()
+    for copy in copies:
+        copy.start()
+    marks.wait()
+    rows = jnp.concatenate([d_ref[:, 0], d_ref[:, 1]], axis=1)
+    high = rows.astype(BF16).astype(F32)
+    middle = (rows - high).astype(BF16).astype(F32)
+    low = (rows - high) - middle
+    parts = jnp.concatenate([high, middle, low, jnp.zeros((7, 256), F32)], axis=0).astype(BF16)
+    message_ref[256:272, :] = jnp.concatenate([parts, jnp.zeros((16, 256), BF16)], axis=1)
+    for copy in copies:
+        copy.wait()
+
+
+def stack_kernel(step, p_ref, own, r1, r2, r3, *rest):
+    out_ref = rest[-1]
+    at = lax.rem(lax.div(p_ref[0], step), 4)
+    for k, part in enumerate((own, r1, r2, r3)):
+        out_ref[lax.rem(at + 4 - k, 4)] = part[...]
+
+
+def stacked(place_of, step, own, parts, arrived):
+    return call(
+        functools.partial(stack_kernel, step),
+        shape((4,) + own.shape, BF16),
+        [full(SMEM)] + [full()] * 4 + [full(pl.ANY)] * len(arrived),
+        8,
+    )(place_of, own, *parts, *arrived)
 
 
 def per_device(
@@ -298,11 +341,23 @@
 ):
     zi = lax.axis_index("space")
     z = zi.reshape(1)
-    mine = lax.dynamic_slice_in_dim(conv_kernel.reshape(9, 16, CH), zi * OC, OC, axis=2)
-    kernel = lax.all_to_all(jnp.broadcast_to(mine[None], (NDP, 9, 16, OC)), "dp", 0, 0, tiled=True)
-    marks = jnp.stack(thirds(direction.reshape(3, 256))).reshape(9, 256)
-    message = jnp.concatenate([features.reshape(256, CH), jnp.pad(marks, ((0, 7), (0, 256)))], axis=0)
+    di = lax.axis_index("dp").reshape(1)
+    message, mine = call(
+        pack_kernel,
+        (shape((272, CH), BF16), shape((9, 16, OC), BF16)),
+        [full(SMEM)] + [full(pltpu.HBM)] * 3,
+        8,
+        [VMEM((3, 2, COLS), F32), pltpu.SemaphoreType.DMA((3,))],
+    )(
+        z,
+        pltpu.with_memory_space_constraint(features.reshape(256, CH), pltpu.HBM),
+        pltpu.with_memory_space_constraint(direction.reshape(3, 2, COLS), pltpu.HBM),
+        pltpu.with_memory_space_constraint(conv_kernel.reshape(9, 16, CH), pltpu.HBM),
+    )
     others = ring(message, "space", 4)
+    column = stacked(di, 2, mine, permuted(mine, lambda x, y, c, k: (x, y + k, c)), others[:1])
+    plane = stacked(di, 8, column, permuted(column, lambda x, y, c, k: (x + k, y, c)), others[1:])
+    sibling = lax.ppermute(plane, "dp", [(i, i ^ 1) for i in range(NDP)])
     b1 = bias_one.reshape(1, CH)
     b2 = bias_two.reshape(1, CH)
     bias = conv_bias.reshape(1, CH)
@@ -316,14 +371,14 @@
     )(z, latent_ids, pltpu.with_memory_space_constraint(latent_bank, pltpu.HBM), style_one, b1, style_two, b2)
     image, turned, marks_all, marks_turned = call(
         image_kernel,
-        (shape((NPOS + 256, CH), BF16), shape((CH, NPOS + 256), BF16), shape((16, NPOS), BF16), shape((NPOS, OC), BF16)),
-        [full(SMEM)] + [full(pltpu.HBM)] * 4 + [full(pl.ANY)],
+        (shape((NPOS, CH), BF16), shape((CH, NPOS), BF16), shape((16, NPOS), BF16), shape((NPOS, OC), BF16)),
+        [full(SMEM)] + [full()] * 4,
         16,
-        [VMEM((4, 272, CH), BF16), pltpu.SemaphoreType.DMA((4,))],
-    )(z, *[pltpu.with_memory_space_constraint(x, pltpu.HBM) for x in (message, *others)], kernel)
-    u, pre, ga, gm, energy, rows = call(
+    )(z, message, *others)
+    kernel, u, pre, ga, gm, energy, rows = call(
         first_kernel,
         (
+            shape((NDP, 9, 16, OC), BF16),
             shape((1, CH), F32),
             shape((NPOS, OC), F32),
             shape((NPOS, OC), BF16),
@@ -331,16 +386,16 @@
             shape((CH, OC), F32),
             shape((8, OC), F32),
         ),
-        [full(SMEM)] + [full()] * 11,
+        [full(SMEM)] * 2 + [full()] * 12,
         16,
-    )(z, image, turned, marks_all, marks_turned, kernel, s, c, rgb, bias, style_one, style_two)
+    )(z, di, image, turned, marks_all, marks_turned, plane, sibling, s, c, rgb, bias, style_one, style_two)
     parts, length = call(
         second_kernel,
-        (pltpu.HBM((NDP, 10, 16, OC), BF16), shape((1,), F32)),
+        (pltpu.HBM((NDP, 10, 16, OC), BF16), shape((8, OC), F32)),
         [full(SMEM)] + [full()] * 18,
         16,
         [VMEM((8, CH), F32), VMEM((NDP, 10, 16, OC), BF16), pltpu.SemaphoreType.DMA((4,))],
-        (full(pltpu.HBM), full(SMEM)),
+        (full(pltpu.HBM), full()),
     )(
         z, u, *ring(u, "space", 4), image, turned, marks_turned, kernel, s, rgb, bias, style_one, style_two,
         pre, ga, gm, energy, rows,
@@ -348,10 +403,9 @@
     received = lax.all_to_all(parts, "dp", 0, 0, tiled=True)
     shard, target = call(
         sum_kernel,
-        (shape((144, OC), BF16), shape((1,), F32)),
+        (shape((144, OC), BF16), shape((8, OC), F32)),
         [full(), full(SMEM)],
         8,
-        out_specs=(full(), full(SMEM)),
     )(received, length_target)
     kernel_grad = call(
         last_kernel,
@@ -359,7 +413,7 @@
         [full(SMEM)] + [full()] * 4,
         16,
     )(z, shard, *ring(shard, "space", 4))
-    return (kernel_grad.reshape(3, 3, 16, CH), length, target)
+    return (kernel_grad.reshape(3, 3, 16, CH), length[0, 0:1], target[0, 0:1])
 
 
 def solution(mesh):

time: 85.9 us -> 82.8 us (0.964)
  starting transfers between devices: 29.7 us -> 35.9 us
  waiting for transfers between devices: 35.8 us -> 30.2 us
  local copies, waits for them, and re-layouts: 2.87 us -> 1.06 us
  other arithmetic: 1 us -> 0 us
    ppermute x9, waiting for transfers between devices: 16.5 us -> 4.25 us  [ring(): lax.ppermute(x, axis, [(i, (i + k) % size) for i in range(size)])]
    ppermute x0 -> x7, starting transfers between devices: none -> 12 us  [the longest x6 11.9 us: permuted(): lax.ppermute(value, 'dp', [(place(x, y, c), place(*to(x, y, c, k))) for x...]
    all_to_all x1 -> x0, starting transfers between devices: 7.55 us -> none  [per_device(): lax.all_to_all(jnp.broadcast_to(mine[None], (NDP, 9, 16, OC)), 'dp', 0, 0...]
    ppermute x0 -> x7, waiting for transfers between devices: none -> 6.66 us  [the longest x6 6.66 us: permuted(): lax.ppermute(value, 'dp', [(place(x, y, c), place(*to(x, y, c, k))) for x...]
    unnamed x22 -> x12, local copies, waits for them, and re-layouts: 1.65 us -> 0.03 us
    ppermute x9, starting transfers between devices: 15.6 us -> 16.9 us  [ring(): lax.ppermute(x, axis, [(i, (i + k) % size) for i in range(size)])]
    broadcast_in_dim x1 -> x0, local copies, waits for them, and re-layouts: 1.18 us -> none  [per_device(): jnp.broadcast_to(mine[None], (NDP, 9, 16, OC))]
    slice x0 -> x2, local copies, waits for them, and re-layouts: none -> 1.02 us  [per_device(): return (kernel_grad.reshape(3, 3, 16, CH), length[0, 0:1], target[0, 0:1])]
  transfers between devices with their start and end apart: 11 -> 17, of which waited for: 8 -> 11; matrix products, arithmetic and copies ran while one was open for 1% -> 1% of each run, Pallas kernels for 1% -> 2%
where the time goes in v3:
time: 82.8 us; the launch traced here: 82.5 us
  starting transfers between devices  35.9 us (43%)
  waiting for transfers between devices  30.2 us (36%)
  Pallas kernels  13.2 us (16%)
  between operations  2.13 us (3%)
  local copies, waits for them, and re-layouts  1.06 us (1%)
    all_to_all x1, waiting for transfers between devices, per_device(): received = lax.all_to_all(parts, 'dp', 0, 0, tiled=True)  19.3 us
    ppermute x9, starting transfers between devices, ring(): lax.ppermute(x, axis, [(i, (i + k) % size) for i in range(size)])  16.9 us
    ppermute x6, starting transfers between devices, permuted(): lax.ppermute(value, 'dp', [(place(x, y, c), place(*to(x, y, c, k))) for x...  11.9 us
    all_to_all x1, starting transfers between devices, per_device(): received = lax.all_to_all(parts, 'dp', 0, 0, tiled=True)  6.95 us
    ppermute x6, waiting for transfers between devices, permuted(): lax.ppermute(value, 'dp', [(place(x, y, c), place(*to(x, y, c, k))) for x...  6.66 us
    pallas_call x1, Pallas kernels, per_device(): call(second_kernel, (pltpu.HBM((NDP, 10, 16, OC), BF16), shape((8, OC), F...  5.13 us
    pallas_call x1, Pallas kernels, per_device(): call(first_kernel, (shape((NDP, 9, 16, OC), BF16), shape((1, CH), F32), s...  4.42 us
    ppermute x9, waiting for transfers between devices, ring(): lax.ppermute(x, axis, [(i, (i + k) % size) for i in range(size)])  4.25 us
  transfers between devices with their start and end apart: 17, of which 11 were waited for; matrix products, arithmetic and copies ran while one was open for 1% of the time, Pallas kernels for 2%

profile of v3, /device:TPU:0, one launch (start us, length us, event | category | flops | bytes accessed | tf_op | source)
XLA Modules:
  0.0 82.5 jit_solution(17078096958390330070)
XLA Ops:
  0.7 1.1 %shard_map.139 = (bf16[272,512]{1,0:T(8,128)(2,1)S(1)}, bf16[9,16,128]{2,1,0:T(8,128)(2,1)S(1)}) custom-call(s32[1]{0:T(128)} %bitcast.z_ref, bf16[256,512]{1,0:T(8,128)(2,1)} %bitcast.17, f32[3,2,128]{2,1,0:T(2,128)} %bitcast.20, bf16[9,16,512]{2,1,0:T(8,128)(2,1)} %bitcast.18), custom_call_target="tpu_custom_call" | custom-call | tf_op jit(solution)/shard_map/pallas_call | solution.py:345
  1.8 2.1 %collective-permute-start = (bf16[272,512]{1,0:T(8,128)(2,1)S(1)}, bf16[272,512]{1,0:T(8,128)(2,1)S(1)}, u32[]{:S(2)}, u32[]{:S(2)}) collective-permute-start(bf16[272,512]{1,0:T(8,128)(2,1)S(1)} %get-tuple-element.22.m0), channel_id=1, source_target_pairs={{0,1},{1,2},{2,3},{3,0},{4,5},{5,6},{6,7},{7,4},{8,9},{9,10},{10,1... | collective-permute-start | bytes 835592 | tf_op jit(solution)/shard_map/ppermute | solution.py:285
  3.9 3.6 %collective-permute-start.1 = (bf16[272,512]{1,0:T(8,128)(2,1)S(1)}, bf16[272,512]{1,0:T(8,128)(2,1)S(1)}, u32[]{:S(2)}, u32[]{:S(2)}) collective-permute-start(bf16[272,512]{1,0:T(8,128)(2,1)S(1)} %get-tuple-element.22.m0), channel_id=1, source_target_pairs={{0,2},{1,3},{2,0},{3,1},{4,6},{5,7},{6,4},{7,5},{8,10},{9,11},{10,... | collective-permute-start | bytes 835592 | tf_op jit(solution)/shard_map/ppermute | solution.py:285
  7.5 1.0 %collective-permute-start.2 = (bf16[272,512]{1,0:T(8,128)(2,1)S(1)}, bf16[272,512]{1,0:T(8,128)(2,1)S(1)}, u32[]{:S(2)}, u32[]{:S(2)}) collective-permute-start(bf16[272,512]{1,0:T(8,128)(2,1)S(1)} %get-tuple-element.22.m0), channel_id=1, source_target_pairs={{0,3},{1,0},{2,1},{3,2},{4,7},{5,4},{6,5},{7,6},{8,11},{9,8},{10,9... | collective-permute-start | bytes 835592 | tf_op jit(solution)/shard_map/ppermute | solution.py:285
  8.5 1.6 %collective-permute-start.3 = (bf16[9,16,128]{2,1,0:T(8,128)(2,1)S(1)}, bf16[9,16,128]{2,1,0:T(8,128)(2,1)S(1)}, u32[]{:S(2)}, u32[]{:S(2)}) collective-permute-start(bf16[9,16,128]{2,1,0:T(8,128)(2,1)S(1)} %get-tuple-element.27.own), channel_id=1, source_target_pairs={{0,8},{4,12},{8,16},{12,20},{16,24},{20,28},{24,0},{28,4},{32,40},... | collective-permute-start | bytes 110600 | tf_op jit(solution)/shard_map/ppermute | solution.py:294
  10.1 2.9 %collective-permute-start.4 = (bf16[9,16,128]{2,1,0:T(8,128)(2,1)S(1)}, bf16[9,16,128]{2,1,0:T(8,128)(2,1)S(1)}, u32[]{:S(2)}, u32[]{:S(2)}) collective-permute-start(bf16[9,16,128]{2,1,0:T(8,128)(2,1)S(1)} %get-tuple-element.27.own), channel_id=1, source_target_pairs={{0,16},{4,20},{8,24},{12,28},{16,0},{20,4},{24,8},{28,12},{32,48},... | collective-permute-start | bytes 110600 | tf_op jit(solution)/shard_map/ppermute | solution.py:294
  13.0 0.7 collective-permute-done.3.r1
  13.7 1.7 %collective-permute-start.5 = (bf16[9,16,128]{2,1,0:T(8,128)(2,1)S(1)}, bf16[9,16,128]{2,1,0:T(8,128)(2,1)S(1)}, u32[]{:S(2)}, u32[]{:S(2)}) collective-permute-start(bf16[9,16,128]{2,1,0:T(8,128)(2,1)S(1)} %get-tuple-element.27.own), channel_id=1, source_target_pairs={{0,24},{4,28},{8,0},{12,4},{16,8},{20,12},{24,16},{28,20},{32,56},... | collective-permute-start | bytes 110600 | tf_op jit(solution)/shard_map/ppermute | solution.py:294
  15.5 0.1 collective-permute-done.4.r2
  15.5 2.1 %collective-permute-done.5.r3 = bf16[9,16,128]{2,1,0:T(8,128)(2,1)S(1)} collective-permute-done((bf16[9,16,128]{2,1,0:T(8,128)(2,1)S(1)}, bf16[9,16,128]{2,1,0:T(8,128)(2,1)S(1)}, u32[]{:S(2)}, u32[]{:S(2)}) %collective-permute-start.5) | collective-permute-done | bytes 36896 | tf_op jit(solution)/shard_map/ppermute | solution.py:294
  17.7 0.0 collective-permute-done.m1.rest_0_
  17.7 1.6 %collective-permute-start.6 = (bf16[4,9,16,128]{3,2,1,0:T(8,128)(2,1)S(1)}, bf16[4,9,16,128]{3,2,1,0:T(8,128)(2,1)S(1)}, u32[]{:S(2)}, u32[]{:S(2)}) collective-permute-start(bf16[4,9,16,128]{3,2,1,0:T(8,128)(2,1)S(1)} %shard_map.141.own), channel_id=1, source_target_pairs={{0,32},{4,36},{8,40},{12,44},{16,48},{20,52},{24,56},{28,60},{32,6... | collective-permute-start | bytes 442376 | tf_op jit(solution)/shard_map/ppermute | solution.py:294
  19.3 2.7 %collective-permute-start.7 = (bf16[4,9,16,128]{3,2,1,0:T(8,128)(2,1)S(1)}, bf16[4,9,16,128]{3,2,1,0:T(8,128)(2,1)S(1)}, u32[]{:S(2)}, u32[]{:S(2)}) collective-permute-start(bf16[4,9,16,128]{3,2,1,0:T(8,128)(2,1)S(1)} %shard_map.141.own), channel_id=1, source_target_pairs={{0,64},{4,68},{8,72},{12,76},{16,80},{20,84},{24,88},{28,92},{32,9... | collective-permute-start | bytes 442376 | tf_op jit(solution)/shard_map/ppermute | solution.py:294
  22.0 1.4 %collective-permute-start.8 = (bf16[4,9,16,128]{3,2,1,0:T(8,128)(2,1)S(1)}, bf16[4,9,16,128]{3,2,1,0:T(8,128)(2,1)S(1)}, u32[]{:S(2)}, u32[]{:S(2)}) collective-permute-start(bf16[4,9,16,128]{3,2,1,0:T(8,128)(2,1)S(1)} %shard_map.141.own), channel_id=1, source_target_pairs={{0,96},{4,100},{8,104},{12,108},{16,112},{20,116},{24,120},{28,124... | collective-permute-start | bytes 442376 | tf_op jit(solution)/shard_map/ppermute | solution.py:294
  23.4 0.0 collective-permute-done.1.m2.rest_0_
  23.4 0.0 collective-permute-done.2.m3.rest_1_
  23.4 1.2 %collective-permute-done.6.r1 = bf16[4,9,16,128]{3,2,1,0:T(8,128)(2,1)S(1)} collective-permute-done((bf16[4,9,16,128]{3,2,1,0:T(8,128)(2,1)S(1)}, bf16[4,9,16,128]{3,2,1,0:T(8,128)(2,1)S(1)}, u32[]{:S(2)}, u32[]{:S(2)}) %collective-permute-start.6) | collective-permute-done | bytes 147488 | tf_op jit(solution)/shard_map/ppermute | solution.py:294
  24.7 2.0 %collective-permute-done.7.r2 = bf16[4,9,16,128]{3,2,1,0:T(8,128)(2,1)S(1)} collective-permute-done((bf16[4,9,16,128]{3,2,1,0:T(8,128)(2,1)S(1)}, bf16[4,9,16,128]{3,2,1,0:T(8,128)(2,1)S(1)}, u32[]{:S(2)}, u32[]{:S(2)}) %collective-permute-start.7) | collective-permute-done | bytes 147488 | tf_op jit(solution)/shard_map/ppermute | solution.py:294
  26.7 0.4 collective-permute-done.8.r3
  27.1 0.1 shard_map.142.k0_ref
  27.2 0.1 collective-permute-start.9
  28.0 0.0 copy-done
  28.0 0.0 copy-done.1
  28.0 0.0 copy-done.3
  28.0 0.0 copy-start.2
  28.0 0.9 %shard_map.143 = (f32[1,512]{1,0:T(1,128)S(1)}, f32[1,128]{1,0:T(1,128)S(1)}) custom-call(s32[1]{0:T(128)} %bitcast.z_ref, s32[1]{0:T(128)S(6)} %copy.15.id_ref, f32[1024,512]{1,0:T(8,128)} %bank_ref.1, f32[512,512]{1,0:T(8,128)S(1)} %copy-done, f32[1,512]{1,0:T(1,128)S(1)} %bitcast.14, f32[512,512]{1,0:T(8,128)S(1)} %copy-done.1, f32[1,512]{1,0:T(1,128)S(1)} %bitcast.15), custom_call_target="tpu_custom_call" | custom-call | tf_op jit(solution)/shard_map/pallas_call | solution.py:365
  28.9 0.5 shard_map.140
  29.4 0.0 collective-permute-done.9.k1_ref
  29.4 4.4 %shard_map.144 = (bf16[32,9,16,128]{3,2,1,0:T(8,128)(2,1)S(1)}, f32[1,512]{1,0:T(1,128)S(1)}, f32[1024,128]{1,0:T(8,128)S(1)}, bf16[1024,128]{1,0:T(8,128)(2,1)S...) custom-call(s32[1]{0:T(128)} %bitcast.z_ref, s32[1]{0:T(128)} %bitcast.1.p_ref, ...), custom_call_target="tpu_custom_call" | custom-call | tf_op jit(solution)/shard_map/pallas_call | solution.py:378
  33.8 1.1 %collective-permute-start.10 = (f32[1,512]{1,0:T(1,128)S(1)}, f32[1,512]{1,0:T(1,128)S(1)}, u32[]{:S(2)}, u32[]{:S(2)}) collective-permute-start(f32[1,512]{1,0:T(1,128)S(1)} %get-tuple-element.30.u0), channel_id=1, source_target_pairs={{0,1},{1,2},{2,3},{3,0},{4,5},{5,6},{6,7},{7,4},{8,9},{9,10},{10,1... | collective-permute-start | bytes 6152 | tf_op jit(solution)/shard_map/ppermute | solution.py:285
  34.9 1.6 %collective-permute-start.11 = (f32[1,512]{1,0:T(1,128)S(1)}, f32[1,512]{1,0:T(1,128)S(1)}, u32[]{:S(2)}, u32[]{:S(2)}) collective-permute-start(f32[1,512]{1,0:T(1,128)S(1)} %get-tuple-element.30.u0), channel_id=1, source_target_pairs={{0,2},{1,3},{2,0},{3,1},{4,6},{5,7},{6,4},{7,5},{8,10},{9,11},{10,... | collective-permute-start | bytes 6152 | tf_op jit(solution)/shard_map/ppermute | solution.py:285
  36.5 2.5 %collective-permute-start.12 = (f32[1,512]{1,0:T(1,128)S(1)}, f32[1,512]{1,0:T(1,128)S(1)}, u32[]{:S(2)}, u32[]{:S(2)}) collective-permute-start(f32[1,512]{1,0:T(1,128)S(1)} %get-tuple-element.30.u0), channel_id=1, source_target_pairs={{0,3},{1,0},{2,1},{3,2},{4,7},{5,4},{6,5},{7,6},{8,11},{9,8},{10,9... | collective-permute-start | bytes 6152 | tf_op jit(solution)/shard_map/ppermute | solution.py:285
  39.1 0.0 collective-permute-done.10.u1
  39.1 0.9 %collective-permute-done.11.u2 = f32[1,512]{1,0:T(1,128)S(1)} collective-permute-done((f32[1,512]{1,0:T(1,128)S(1)}, f32[1,512]{1,0:T(1,128)S(1)}, u32[]{:S(2)}, u32[]{:S(2)}) %collective-permute-start.11) | collective-permute-done | bytes 2080 | tf_op jit(solution)/shard_map/ppermute | solution.py:285
  40.0 0.4 collective-permute-done.12.u3
  40.4 5.1 %shard_map.145 = (bf16[32,10,16,128]{3,2,1,0:T(8,128)(2,1)}, f32[8,128]{1,0:T(8,128)S(1)}) custom-call(s32[1]{0:T(128)} %bitcast.z_ref, f32[1,512]{1,0:T(1,128)S(1)} %get-tuple-element.30.u0, f32[1,512]{1,0:T(1,128)S(1)} %collective-permute-done.10.u1, f32[1,512]{1,0:T(1,128)S(1)} %collective-permute-done.11.u2, f32[1,512]{1,0:T(1,128)S(1)} %collective-permute-done.12.u3, ...), custom_call_target="tpu_custom_call" | custom-call | tf_op jit(solution)/shard_map/pallas_call | solution.py:392
  45.5 7.0 %all-to-all-start = ((bf16[32,10,16,128]{3,2,1,0:T(8,128)(2,1)}), bf16[32,10,16,128]{3,2,1,0:T(8,128)(2,1)S(1)}, u32[]{:S(2)}, u32[]{:S(2)}) async-start(bf16[32,10,16,128]{3,2,1,0:T(8,128)(2,1)} %get-tuple-element.37), calls=%async_computation | async-start | bytes 2621440 | tf_op jit(solution)/shard_map/all_to_all | solution.py:403
  53.1 19.3 %all-to-all-done.part_ref = bf16[32,10,16,128]{3,2,1,0:T(8,128)(2,1)S(1)} async-done(((bf16[32,10,16,128]{3,2,1,0:T(8,128)(2,1)}), bf16[32,10,16,128]{3,2,1,0:T(8,128)(2,1)S(1)}, u32[]{:S(2)}, u32[]{:S(2)}) %all-to-all-start) | async-done | bytes 1310752 | tf_op jit(solution)/shard_map/all_to_all | solution.py:403
  72.4 0.3 shard_map.146
  72.7 1.2 %collective-permute-start.13 = (bf16[144,128]{1,0:T(8,128)(2,1)S(1)}, bf16[144,128]{1,0:T(8,128)(2,1)S(1)}, u32[]{:S(2)}, u32[]{:S(2)}) collective-permute-start(bf16[144,128]{1,0:T(8,128)(2,1)S(1)} %get-tuple-element.38.p0), channel_id=1, source_target_pairs={{0,1},{1,2},{2,3},{3,0},{4,5},{5,6},{6,7},{7,4},{8,9},{9,10},{10,1... | collective-permute-start | bytes 110600 | tf_op jit(solution)/shard_map/ppermute | solution.py:285
  73.9 3.8 %collective-permute-start.14 = (bf16[144,128]{1,0:T(8,128)(2,1)S(1)}, bf16[144,128]{1,0:T(8,128)(2,1)S(1)}, u32[]{:S(2)}, u32[]{:S(2)}) collective-permute-start(bf16[144,128]{1,0:T(8,128)(2,1)S(1)} %get-tuple-element.38.p0), channel_id=1, source_target_pairs={{0,2},{1,3},{2,0},{3,1},{4,6},{5,7},{6,4},{7,5},{8,10},{9,11},{10,... | collective-permute-start | bytes 110600 | tf_op jit(solution)/shard_map/ppermute | solution.py:285
  77.8 0.0 collective-permute-start.15
  77.8 0.5 slice.6
  78.3 0.5 slice.7
  78.8 0.0 collective-permute-done.13.p1
  78.8 1.3 %collective-permute-done.14.p2 = bf16[144,128]{1,0:T(8,128)(2,1)S(1)} collective-permute-done((bf16[144,128]{1,0:T(8,128)(2,1)S(1)}, bf16[144,128]{1,0:T(8,128)(2,1)S(1)}, u32[]{:S(2)}, u32[]{:S(2)}) %collective-permute-start.14) | collective-permute-done | bytes 36896 | tf_op jit(solution)/shard_map/ppermute | solution.py:285
  80.1 1.6 %collective-permute-done.15.p3 = bf16[144,128]{1,0:T(8,128)(2,1)S(1)} collective-permute-done((bf16[144,128]{1,0:T(8,128)(2,1)S(1)}, bf16[144,128]{1,0:T(8,128)(2,1)S(1)}, u32[]{:S(2)}, u32[]{:S(2)}) %collective-permute-start.15) | collective-permute-done | bytes 36896 | tf_op jit(solution)/shard_map/ppermute | solution.py:285
  81.7 0.8 shard_map.147
  (10 shorter events, 0.0 us)
Async XLA Ops:
  0.6 27.3 %copy-start.5 = (f32[512,3]{0,1:T(4,128)S(1)}, f32[512,3]{0,1:T(4,128)}, u32[]{:S(2)}) copy-start(f32[512,3]{0,1:T(4,128)} %param.20) | copy-start | bytes 18436
  0.6 27.3 %copy-start = (f32[512,512]{1,0:T(8,128)S(1)}, f32[512,512]{1,0:T(8,128)}, u32[]{:S(2)}) copy-start(f32[512,512]{1,0:T(8,128)} %w1_ref.5) | copy-start | bytes 3145732
  0.7 27.3 %copy-start.1 = (f32[512,512]{1,0:T(8,128)S(1)}, f32[512,512]{1,0:T(8,128)}, u32[]{:S(2)}) copy-start(f32[512,512]{1,0:T(8,128)} %w2_ref.5) | copy-start | bytes 3145732
  0.7 27.3 %copy-start.3 = (f32[512]{0:T(512)S(1)}, f32[512]{0:T(512)}, u32[]{:S(2)}) copy-start(f32[512]{0:T(512)} %param.17) | copy-start | bytes 6148
  0.7 27.3 %copy-start.4 = (f32[512]{0:T(512)S(1)}, f32[512]{0:T(512)}, u32[]{:S(2)}) copy-start(f32[512]{0:T(512)} %param.19) | copy-start | bytes 6148
  1.8 15.8 %collective-permute-start = (bf16[272,512]{1,0:T(8,128)(2,1)S(1)}, bf16[272,512]{1,0:T(8,128)(2,1)S(1)}, u32[]{:S(2)}, u32[]{:S(2)}) collective-permute-start(bf16[272,512]{1,0:T(8,128)(2,1)S(1)} %get-tuple-element.22.m0), channel_id=1, source_target_pairs={{0,1},{1,2},{2,3},{3,0},{4,5},{5,6},{6,7},{7,4},{8,9},{9,10},{10,1... | collective-permute-start | bytes 835592 | tf_op jit(solution)/shard_map/ppermute | solution.py:285
  3.9 19.5 %collective-permute-start.1 = (bf16[272,512]{1,0:T(8,128)(2,1)S(1)}, bf16[272,512]{1,0:T(8,128)(2,1)S(1)}, u32[]{:S(2)}, u32[]{:S(2)}) collective-permute-start(bf16[272,512]{1,0:T(8,128)(2,1)S(1)} %get-tuple-element.22.m0), channel_id=1, source_target_pairs={{0,2},{1,3},{2,0},{3,1},{4,6},{5,7},{6,4},{7,5},{8,10},{9,11},{10,... | collective-permute-start | bytes 835592 | tf_op jit(solution)/shard_map/ppermute | solution.py:285
  7.5 16.0 %collective-permute-start.2 = (bf16[272,512]{1,0:T(8,128)(2,1)S(1)}, bf16[272,512]{1,0:T(8,128)(2,1)S(1)}, u32[]{:S(2)}, u32[]{:S(2)}) collective-permute-start(bf16[272,512]{1,0:T(8,128)(2,1)S(1)} %get-tuple-element.22.m0), channel_id=1, source_target_pairs={{0,3},{1,0},{2,1},{3,2},{4,7},{5,4},{6,5},{7,6},{8,11},{9,8},{10,9... | collective-permute-start | bytes 835592 | tf_op jit(solution)/shard_map/ppermute | solution.py:285
  8.5 5.2 %collective-permute-start.3 = (bf16[9,16,128]{2,1,0:T(8,128)(2,1)S(1)}, bf16[9,16,128]{2,1,0:T(8,128)(2,1)S(1)}, u32[]{:S(2)}, u32[]{:S(2)}) collective-permute-start(bf16[9,16,128]{2,1,0:T(8,128)(2,1)S(1)} %get-tuple-element.27.own), channel_id=1, source_target_pairs={{0,8},{4,12},{8,16},{12,20},{16,24},{20,28},{24,0},{28,4},{32,40},... | collective-permute-start | bytes 110600 | tf_op jit(solution)/shard_map/ppermute | solution.py:294
  10.1 5.5 %collective-permute-start.4 = (bf16[9,16,128]{2,1,0:T(8,128)(2,1)S(1)}, bf16[9,16,128]{2,1,0:T(8,128)(2,1)S(1)}, u32[]{:S(2)}, u32[]{:S(2)}) collective-permute-start(bf16[9,16,128]{2,1,0:T(8,128)(2,1)S(1)} %get-tuple-element.27.own), channel_id=1, source_target_pairs={{0,16},{4,20},{8,24},{12,28},{16,0},{20,4},{24,8},{28,12},{32,48},... | collective-permute-start | bytes 110600 | tf_op jit(solution)/shard_map/ppermute | solution.py:294
  13.7 4.0 %collective-permute-start.5 = (bf16[9,16,128]{2,1,0:T(8,128)(2,1)S(1)}, bf16[9,16,128]{2,1,0:T(8,128)(2,1)S(1)}, u32[]{:S(2)}, u32[]{:S(2)}) collective-permute-start(bf16[9,16,128]{2,1,0:T(8,128)(2,1)S(1)} %get-tuple-element.27.own), channel_id=1, source_target_pairs={{0,24},{4,28},{8,0},{12,4},{16,8},{20,12},{24,16},{28,20},{32,56},... | collective-permute-start | bytes 110600 | tf_op jit(solution)/shard_map/ppermute | solution.py:294
  17.7 7.0 %collective-permute-start.6 = (bf16[4,9,16,128]{3,2,1,0:T(8,128)(2,1)S(1)}, bf16[4,9,16,128]{3,2,1,0:T(8,128)(2,1)S(1)}, u32[]{:S(2)}, u32[]{:S(2)}) collective-permute-start(bf16[4,9,16,128]{3,2,1,0:T(8,128)(2,1)S(1)} %shard_map.141.own), channel_id=1, source_target_pairs={{0,32},{4,36},{8,40},{12,44},{16,48},{20,52},{24,56},{28,60},{32,6... | collective-permute-start | bytes 442376 | tf_op jit(solution)/shard_map/ppermute | solution.py:294
  19.3 7.4 %collective-permute-start.7 = (bf16[4,9,16,128]{3,2,1,0:T(8,128)(2,1)S(1)}, bf16[4,9,16,128]{3,2,1,0:T(8,128)(2,1)S(1)}, u32[]{:S(2)}, u32[]{:S(2)}) collective-permute-start(bf16[4,9,16,128]{3,2,1,0:T(8,128)(2,1)S(1)} %shard_map.141.own), channel_id=1, source_target_pairs={{0,64},{4,68},{8,72},{12,76},{16,80},{20,84},{24,88},{28,92},{32,9... | collective-permute-start | bytes 442376 | tf_op jit(solution)/shard_map/ppermute | solution.py:294
  22.0 5.1 %collective-permute-start.8 = (bf16[4,9,16,128]{3,2,1,0:T(8,128)(2,1)S(1)}, bf16[4,9,16,128]{3,2,1,0:T(8,128)(2,1)S(1)}, u32[]{:S(2)}, u32[]{:S(2)}) collective-permute-start(bf16[4,9,16,128]{3,2,1,0:T(8,128)(2,1)S(1)} %shard_map.141.own), channel_id=1, source_target_pairs={{0,96},{4,100},{8,104},{12,108},{16,112},{20,116},{24,120},{28,124... | collective-permute-start | bytes 442376 | tf_op jit(solution)/shard_map/ppermute | solution.py:294
  27.2 2.2 %collective-permute-start.9 = (bf16[4,4,9,16,128]{4,3,2,1,0:T(8,128)(2,1)S(1)}, bf16[4,4,9,16,128]{4,3,2,1,0:T(8,128)(2,1)S(1)}, u32[]{:S(2)}, u32[]{:S(2)}) collective-permute-start(bf16[4,4,9,16,128]{4,3,2,1,0:T(8,128)(2,1)S(1)} %shard_map.142.k0_ref), channel_id=1, source_target_pairs={{0,4},{4,0},{8,12},{12,8},{16,20},{20,16},{24,28},{28,24},{32,36},... | collective-permute-start | bytes 1769480 | tf_op jit(solution)/shard_map/ppermute | solution.py:360
  28.0 1.4 %copy-start.2 = (f32[512]{0:T(512)S(1)}, f32[512]{0:T(512)}, u32[]{:S(2)}) copy-start(f32[512]{0:T(512)} %param.21) | copy-start | bytes 6148
  33.8 5.3 %collective-permute-start.10 = (f32[1,512]{1,0:T(1,128)S(1)}, f32[1,512]{1,0:T(1,128)S(1)}, u32[]{:S(2)}, u32[]{:S(2)}) collective-permute-start(f32[1,512]{1,0:T(1,128)S(1)} %get-tuple-element.30.u0), channel_id=1, source_target_pairs={{0,1},{1,2},{2,3},{3,0},{4,5},{5,6},{6,7},{7,4},{8,9},{9,10},{10,1... | collective-permute-start | bytes 6152 | tf_op jit(solution)/shard_map/ppermute | solution.py:285
  34.9 5.1 %collective-permute-start.11 = (f32[1,512]{1,0:T(1,128)S(1)}, f32[1,512]{1,0:T(1,128)S(1)}, u32[]{:S(2)}, u32[]{:S(2)}) collective-permute-start(f32[1,512]{1,0:T(1,128)S(1)} %get-tuple-element.30.u0), channel_id=1, source_target_pairs={{0,2},{1,3},{2,0},{3,1},{4,6},{5,7},{6,4},{7,5},{8,10},{9,11},{10,... | collective-permute-start | bytes 6152 | tf_op jit(solution)/shard_map/ppermute | solution.py:285
  36.5 3.8 %collective-permute-start.12 = (f32[1,512]{1,0:T(1,128)S(1)}, f32[1,512]{1,0:T(1,128)S(1)}, u32[]{:S(2)}, u32[]{:S(2)}) collective-permute-start(f32[1,512]{1,0:T(1,128)S(1)} %get-tuple-element.30.u0), channel_id=1, source_target_pairs={{0,3},{1,0},{2,1},{3,2},{4,7},{5,4},{6,5},{7,6},{8,11},{9,8},{10,9... | collective-permute-start | bytes 6152 | tf_op jit(solution)/shard_map/ppermute | solution.py:285
  45.5 26.9 %all-to-all-start = ((bf16[32,10,16,128]{3,2,1,0:T(8,128)(2,1)}), bf16[32,10,16,128]{3,2,1,0:T(8,128)(2,1)S(1)}, u32[]{:S(2)}, u32[]{:S(2)}) async-start(bf16[32,10,16,128]{3,2,1,0:T(8,128)(2,1)} %get-tuple-element.37), calls=%async_computation | async-start | bytes 2621440 | tf_op jit(solution)/shard_map/all_to_all | solution.py:403
  72.7 6.1 %collective-permute-start.13 = (bf16[144,128]{1,0:T(8,128)(2,1)S(1)}, bf16[144,128]{1,0:T(8,128)(2,1)S(1)}, u32[]{:S(2)}, u32[]{:S(2)}) collective-permute-start(bf16[144,128]{1,0:T(8,128)(2,1)S(1)} %get-tuple-element.38.p0), channel_id=1, source_target_pairs={{0,1},{1,2},{2,3},{3,0},{4,5},{5,6},{6,7},{7,4},{8,9},{9,10},{10,1... | collective-permute-start | bytes 110600 | tf_op jit(solution)/shard_map/ppermute | solution.py:285
  73.9 6.2 %collective-permute-start.14 = (bf16[144,128]{1,0:T(8,128)(2,1)S(1)}, bf16[144,128]{1,0:T(8,128)(2,1)S(1)}, u32[]{:S(2)}, u32[]{:S(2)}) collective-permute-start(bf16[144,128]{1,0:T(8,128)(2,1)S(1)} %get-tuple-element.38.p0), channel_id=1, source_target_pairs={{0,2},{1,3},{2,0},{3,1},{4,6},{5,7},{6,4},{7,5},{8,10},{9,11},{10,... | collective-permute-start | bytes 110600 | tf_op jit(solution)/shard_map/ppermute | solution.py:285
  77.8 4.0 %collective-permute-start.15 = (bf16[144,128]{1,0:T(8,128)(2,1)S(1)}, bf16[144,128]{1,0:T(8,128)(2,1)S(1)}, u32[]{:S(2)}, u32[]{:S(2)}) collective-permute-start(bf16[144,128]{1,0:T(8,128)(2,1)S(1)} %get-tuple-element.38.p0), channel_id=1, source_target_pairs={{0,3},{1,0},{2,1},{3,2},{4,7},{5,4},{6,5},{7,6},{8,11},{9,8},{10,9... | collective-permute-start | bytes 110600 | tf_op jit(solution)/shard_map/ppermute | solution.py:285

commit v4 on v3

--- a/solution.py
+++ b/solution.py
@@ -39,22 +39,26 @@
     return jnp.transpose(jnp.broadcast_to(row, (OC, row.shape[1])))
 
 
-def row_of(lanes):
-    return jnp.sum(jnp.transpose(lanes), axis=0, keepdims=True)
-
-
-def styles_kernel(z_ref, id_ref, bank_ref, w1_ref, b1_ref, w2_ref, b2_ref, s_ref, c_ref, w_buf, sem):
-    copy = pltpu.make_async_copy(bank_ref.at[pl.ds(id_ref[0], 1)], w_buf, sem)
-    copy.start()
-    copy.wait()
-    z = z_ref[0]
-    lo = pl.multiple_of(z * OC, OC)
+def styles_kernel(
+    z_ref, id_ref, bank_ref, w1_hbm, b1_ref, w2_hbm, b2_ref, s_ref, c_ref, w1t_ref, w2t_ref, w_buf, w1_ref, w2_ref, sems
+):
+    mine = pl.ds(pl.multiple_of(z_ref[0] * OC, OC), OC)
+    copies = [
+        pltpu.make_async_copy(bank_ref.at[pl.ds(id_ref[0], 1)], w_buf, sems.at[0]),
+        pltpu.make_async_copy(w2_hbm.at[:, mine], w2_ref, sems.at[1]),
+        pltpu.make_async_copy(w1_hbm, w1_ref, sems.at[2]),
+    ]
+    for copy in copies:
+        copy.start()
+    for copy in copies:
+        copy.wait()
     w = lanes_of(w_buf[...])
     for j in range(4):
         block = pl.ds(j * OC, OC)
         s_ref[:, block] = jnp.sum(w * w1_ref[:, block], axis=0, keepdims=True) + b1_ref[:, block]
-    mine = pl.ds(lo, OC)
-    c_ref[...] = jnp.sum(w * w2_ref[:, mine], axis=0, keepdims=True) + b2_ref[:, mine]
+    c_ref[...] = jnp.sum(w * w2_ref[...], axis=0, keepdims=True) + b2_ref[:, mine]
+    w1t_ref[...] = jnp.transpose(w1_ref[...])
+    w2t_ref[...] = jnp.transpose(w2_ref[...])
 
 
 def image_kernel(z_ref, m0, m1, m2, m3, f_ref, ft_ref, d_ref, dt_ref):
@@ -114,7 +118,7 @@
 
 
 def first_kernel(
-    z_ref, p_ref, f_ref, ft_ref, d_ref, dt_ref, k0_ref, k1_ref, s_ref, c_ref, rgb_ref, bias_ref, w1_ref, w2_ref,
+    z_ref, p_ref, f_ref, ft_ref, d_ref, dt_ref, k0_ref, k1_ref, s_ref, c_ref, rgb_ref, bias_ref, w1t_ref, w2t_ref,
     k_ref, u_ref, pre_ref, ga_ref, gm_ref, e_ref, rows_ref,
 ):
     z = z_ref[0]
@@ -154,25 +158,24 @@
     hs = spread(h)
     along = None
     for dy in range(3):
-        gm = dot(ft_ref[...], hs[:, 3 * OC * dy : 3 * OC * (dy + 1)]).astype(BF16)
-        gm_ref[dy] = gm
-        gm = gm.astype(F32)
+        gm = dot(ft_ref[...], hs[:, 3 * OC * dy : 3 * OC * (dy + 1)])
+        gm_ref[dy] = gm.astype(BF16)
         for dx in range(3):
             term = tap(k_ref, 3 * dy + dx) * gm[:, dx * OC : (dx + 1) * OC]
             along = term if along is None else along + term
-    grad_s = row_of(along * demod + 2.0 * s * energy * grad_q)
-    total = jnp.broadcast_to(grad_colour, (CH, OC)) * w2_ref[:, pl.ds(lo, OC)]
-    for j in range(4):
-        total = total + w1_ref[:, j * OC : (j + 1) * OC] * grad_s[:, j * OC : (j + 1) * OC]
-    u_ref[...] = row_of(total)
+    grad_s = jnp.sum(along * demod + 2.0 * s * energy * grad_q, axis=1, keepdims=True)
+    colour_lanes = lanes_of(grad_colour)[:, 0:1]
+    u_ref[...] = jnp.sum(w1t_ref[...] * grad_s, axis=0, keepdims=True) + jnp.sum(
+        w2t_ref[...] * colour_lanes, axis=0, keepdims=True
+    )
     rows_ref[0:1, :] = demod
     rows_ref[1:2, :] = grad_demod
 
 
 def second_kernel(
-    z_ref, u0, u1, u2, u3, f_ref, ft_ref, dt_ref, k_ref, s_ref, rgb_ref, bias_ref, w1_ref, w2_ref,
+    z_ref, u0, u1, u2, u3, f_ref, ft_ref, dt_ref, k_ref, s_ref, rgb_ref, bias_ref, w1t_ref, w2t_ref,
     pre_ref, ga_ref, gm_ref, e_ref, rows_ref,
-    out_ref, len_ref, u_buf, parts, sems,
+    out_ref, len_ref, u_buf,
 ):
     z = z_ref[0]
     lo = pl.multiple_of(z * OC, OC)
@@ -186,22 +189,12 @@
     rest = length - high.astype(F32)
     middle = rest.astype(BF16)
     low = (rest - middle.astype(F32)).astype(BF16)
-    row = lax.broadcasted_iota(jnp.int32, (16, OC), 0)
+    row = lax.broadcasted_iota(jnp.int32, (8, OC), 0)
     pieces = jnp.where(row == 0, high.astype(F32), jnp.where(row == 1, middle.astype(F32), low.astype(F32)))
-    parts[:, 9] = jnp.broadcast_to(pieces.astype(BF16)[None], (NDP, 16, OC))
-    copies = []
-    for dy in range(3):
-        some = pl.ds(3 * dy, 3)
-        copies.append(pltpu.make_async_copy(parts.at[:, some], out_ref.at[:, some], sems.at[dy]))
-    copies.append(pltpu.make_async_copy(parts.at[:, pl.ds(9, 1)], out_ref.at[:, pl.ds(9, 1)], sems.at[3]))
-    copies[3].start()
-    point = lanes_of(grad)
-    ds = lanes_of(
-        jnp.concatenate(
-            [jnp.sum(point * w1_ref[:, j * OC : (j + 1) * OC], axis=0, keepdims=True) for j in range(4)], axis=1
-        )
-    )
-    dc = jnp.sum(point * w2_ref[:, pl.ds(lo, OC)], axis=0, keepdims=True)
+    out_ref[:, 144:152] = jnp.broadcast_to(pieces.astype(BF16)[None], (NDP, 8, OC))
+    ds = jnp.broadcast_to(jnp.sum(w1t_ref[...] * grad, axis=1, keepdims=True), (CH, OC))
+    dc_lanes = jnp.broadcast_to(jnp.sum(w2t_ref[...] * grad, axis=1, keepdims=True), (OC, OC))
+    dc = jnp.transpose(dc_lanes)[0:1, :]
     s = lanes_of(s_ref[...])
     energy = e_ref[...]
     demod = rows_ref[0:1, :]
@@ -234,16 +227,13 @@
             t = 3 * dy + dx
             cut = slice(dx * OC, (dx + 1) * OC)
             value = gm2[:, cut] * sd + gm_ref[dy, :, cut].astype(F32) * dsd + tap(k_ref, t) * cot_e
-            parts[:, t] = value.astype(BF16).reshape(NDP, 16, OC)
-        copies[dy].start()
-    for copy in copies:
-        copy.wait()
+            out_ref[:, 16 * t : 16 * (t + 1)] = value.astype(BF16).reshape(NDP, 16, OC)
 
 
 def sum_kernel(part_ref, target_ref, out_ref, new_ref):
     lengths = []
     for b in range(NDP):
-        tile = part_ref[b, 9].astype(F32)
+        tile = part_ref[b, 144:152].astype(F32)
         lengths.append(tile[0:1] + tile[1:2] + tile[2:3])
     total = lengths[0]
     for b in range(1, NDP):
@@ -254,7 +244,7 @@
     value = None
     for b in range(NDP):
         factor = 2.0 * PL_WEIGHT * (lengths[b] - target) / lengths[b]
-        term = part_ref[b, 0:9].astype(F32).reshape(144, OC) * factor
+        term = part_ref[b, 0:144].astype(F32) * factor
         value = term if value is None else value + term
     out_ref[...] = value.astype(BF16)
 
@@ -283,6 +273,10 @@
 
 def ring(x, axis, size):
     return [lax.ppermute(x, axis, [(i, (i + k) % size) for i in range(size)]) for k in range(1, size)]
+
+
+def pinned(x):
+    return pltpu.with_memory_space_constraint(x, pltpu.HBM)
 
 
 def place(x, y, c):
@@ -350,31 +344,31 @@
         [VMEM((3, 2, COLS), F32), pltpu.SemaphoreType.DMA((3,))],
     )(
         z,
-        pltpu.with_memory_space_constraint(features.reshape(256, CH), pltpu.HBM),
+        pinned(features.reshape(256, CH)),
         pltpu.with_memory_space_constraint(direction.reshape(3, 2, COLS), pltpu.HBM),
         pltpu.with_memory_space_constraint(conv_kernel.reshape(9, 16, CH), pltpu.HBM),
     )
     others = ring(message, "space", 4)
-    column = stacked(di, 2, mine, permuted(mine, lambda x, y, c, k: (x, y + k, c)), others[:1])
-    plane = stacked(di, 8, column, permuted(column, lambda x, y, c, k: (x + k, y, c)), others[1:])
-    sibling = lax.ppermute(plane, "dp", [(i, i ^ 1) for i in range(NDP)])
+    column = stacked(di, 2, mine, permuted(mine, lambda x, y, c, k: (x, y + k, c)), [])
     b1 = bias_one.reshape(1, CH)
     b2 = bias_two.reshape(1, CH)
     bias = conv_bias.reshape(1, CH)
     rgb = jnp.pad(rgb_weight.T, ((0, 5), (0, 0)))
-    s, c = call(
+    s, c, w1t, w2t = call(
         styles_kernel,
-        (shape((1, CH), F32), shape((1, OC), F32)),
-        [full(SMEM), full(SMEM), full(pltpu.HBM)] + [full()] * 4,
+        (shape((1, CH), F32), shape((1, OC), F32), shape((CH, CH), F32), shape((OC, CH), F32)),
+        [full(SMEM), full(SMEM), full(pltpu.HBM), full(pltpu.HBM), full(), full(pltpu.HBM), full()],
         8,
-        [VMEM((1, CH), F32), pltpu.SemaphoreType.DMA],
-    )(z, latent_ids, pltpu.with_memory_space_constraint(latent_bank, pltpu.HBM), style_one, b1, style_two, b2)
+        [VMEM((1, CH), F32), VMEM((CH, CH), F32), VMEM((CH, OC), F32), pltpu.SemaphoreType.DMA((3,))],
+    )(z, latent_ids, pinned(latent_bank), pinned(style_one), b1, pinned(style_two), b2)
     image, turned, marks_all, marks_turned = call(
         image_kernel,
         (shape((NPOS, CH), BF16), shape((CH, NPOS), BF16), shape((16, NPOS), BF16), shape((NPOS, OC), BF16)),
         [full(SMEM)] + [full()] * 4,
         16,
     )(z, message, *others)
+    plane = stacked(di, 8, column, permuted(column, lambda x, y, c, k: (x + k, y, c)), [s, marks_all])
+    sibling = lax.ppermute(plane, "dp", [(i, i ^ 1) for i in range(NDP)])
     kernel, u, pre, ga, gm, energy, rows = call(
         first_kernel,
         (
@@ -388,16 +382,15 @@
         ),
         [full(SMEM)] * 2 + [full()] * 12,
         16,
-    )(z, di, image, turned, marks_all, marks_turned, plane, sibling, s, c, rgb, bias, style_one, style_two)
+    )(z, di, image, turned, marks_all, marks_turned, plane, sibling, s, c, rgb, bias, w1t, w2t)
     parts, length = call(
         second_kernel,
-        (pltpu.HBM((NDP, 10, 16, OC), BF16), shape((8, OC), F32)),
+        (pltpu.HBM((NDP, 152, OC), BF16), shape((8, OC), F32)),
         [full(SMEM)] + [full()] * 18,
         16,
-        [VMEM((8, CH), F32), VMEM((NDP, 10, 16, OC), BF16), pltpu.SemaphoreType.DMA((4,))],
-        (full(pltpu.HBM), full()),
+        [VMEM((8, CH), F32)],
     )(
-        z, u, *ring(u, "space", 4), image, turned, marks_turned, kernel, s, rgb, bias, style_one, style_two,
+        z, u, *ring(u, "space", 4), image, turned, marks_turned, kernel, s, rgb, bias, w1t, w2t,
         pre, ga, gm, energy, rows,
     )
     received = lax.all_to_all(parts, "dp", 0, 0, tiled=True)

time: 82.8 us -> 80.1 us (0.967)
  starting transfers between devices: 35.9 us -> 33.3 us
  waiting for transfers between devices: 30.2 us -> 28 us
  local copies, waits for them, and re-layouts: 1.06 us -> 2.4 us
    ppermute x6, waiting for transfers between devices: 6.66 us -> 2.96 us  [permuted(): lax.ppermute(value, 'dp', [(place(x, y, c), place(*to(x, y, c, k))) for x...]
    ppermute x1, waiting for transfers between devices: 0.01 us -> 1.97 us  [per_device(): sibling = lax.ppermute(plane, 'dp', [(i, i ^ 1) for i in range(NDP)])]
    ppermute x9, starting transfers between devices: 16.9 us -> 15.2 us  [ring(): lax.ppermute(x, axis, [(i, (i + k) % size) for i in range(size)])]
    unnamed x12 -> x8, local copies, waits for them, and re-layouts: 0.03 us -> 1.37 us
    pallas_call x2, Pallas kernels: 5.99 us -> 7.1 us  [the longest x1 5.27 us: per_device(): call(second_kernel, (pltpu.HBM((NDP, 152, OC), BF16), shape((8, OC), F32)...]
    all_to_all x1, starting transfers between devices: 6.95 us -> 5.99 us  [per_device(): received = lax.all_to_all(parts, 'dp', 0, 0, tiled=True)]
  transfers between devices with their start and end apart: 17 -> 17, of which waited for: 11 -> 9; matrix products, arithmetic and copies ran while one was open for 1% -> 1% of each run, Pallas kernels for 2% -> 3%
where the time goes in v4:
time: 80.1 us; the launch traced here: 79.7 us
  starting transfers between devices  33.3 us (42%)
  waiting for transfers between devices  28 us (35%)
  Pallas kernels  14 us (17%)
  local copies, waits for them, and re-layouts  2.4 us (3%)
  between operations  2.08 us (3%)
    all_to_all x1, waiting for transfers between devices, per_device(): received = lax.all_to_all(parts, 'dp', 0, 0, tiled=True)  18.5 us
    ppermute x9, starting transfers between devices, ring(): lax.ppermute(x, axis, [(i, (i + k) % size) for i in range(size)])  15.2 us
    ppermute x6, starting transfers between devices, permuted(): lax.ppermute(value, 'dp', [(place(x, y, c), place(*to(x, y, c, k))) for x...  11.9 us
    all_to_all x1, starting transfers between devices, per_device(): received = lax.all_to_all(parts, 'dp', 0, 0, tiled=True)  5.99 us
    pallas_call x1, Pallas kernels, per_device(): call(second_kernel, (pltpu.HBM((NDP, 152, OC), BF16), shape((8, OC), F32)...  5.27 us
    ppermute x9, waiting for transfers between devices, ring(): lax.ppermute(x, axis, [(i, (i + k) % size) for i in range(size)])  4.54 us
    pallas_call x1, Pallas kernels, per_device(): call(first_kernel, (shape((NDP, 9, 16, OC), BF16), shape((1, CH), F32), s...  4.28 us
    ppermute x6, waiting for transfers between devices, permuted(): lax.ppermute(value, 'dp', [(place(x, y, c), place(*to(x, y, c, k))) for x...  2.96 us
  transfers between devices with their start and end apart: 17, of which 9 were waited for; matrix products, arithmetic and copies ran while one was open for 1% of the time, Pallas kernels for 3%

profile of v4, /device:TPU:0, one launch (start us, length us, event | category | flops | bytes accessed | tf_op | source)
XLA Modules:
  0.0 79.7 jit_solution(7928576418728550358)
XLA Ops:
  0.6 1.0 %shard_map.139 = (bf16[272,512]{1,0:T(8,128)(2,1)S(1)}, bf16[9,16,128]{2,1,0:T(8,128)(2,1)S(1)}) custom-call(s32[1]{0:T(128)} %bitcast.z_ref, bf16[256,512]{1,0:T(8,128)(2,1)} %bitcast.17, f32[3,2,128]{2,1,0:T(2,128)} %bitcast.20, bf16[9,16,512]{2,1,0:T(8,128)(2,1)} %bitcast.18), custom_call_target="tpu_custom_call" | custom-call | tf_op jit(solution)/shard_map/pallas_call | solution.py:339
  1.6 2.1 %collective-permute-start = (bf16[272,512]{1,0:T(8,128)(2,1)S(1)}, bf16[272,512]{1,0:T(8,128)(2,1)S(1)}, u32[]{:S(2)}, u32[]{:S(2)}) collective-permute-start(bf16[272,512]{1,0:T(8,128)(2,1)S(1)} %get-tuple-element.24.m0), channel_id=1, source_target_pairs={{0,1},{1,2},{2,3},{3,0},{4,5},{5,6},{6,7},{7,4},{8,9},{9,10},{10,1... | collective-permute-start | bytes 835592 | tf_op jit(solution)/shard_map/ppermute | solution.py:275
  3.7 3.6 %collective-permute-start.1 = (bf16[272,512]{1,0:T(8,128)(2,1)S(1)}, bf16[272,512]{1,0:T(8,128)(2,1)S(1)}, u32[]{:S(2)}, u32[]{:S(2)}) collective-permute-start(bf16[272,512]{1,0:T(8,128)(2,1)S(1)} %get-tuple-element.24.m0), channel_id=1, source_target_pairs={{0,2},{1,3},{2,0},{3,1},{4,6},{5,7},{6,4},{7,5},{8,10},{9,11},{10,... | collective-permute-start | bytes 835592 | tf_op jit(solution)/shard_map/ppermute | solution.py:275
  7.3 1.0 %collective-permute-start.2 = (bf16[272,512]{1,0:T(8,128)(2,1)S(1)}, bf16[272,512]{1,0:T(8,128)(2,1)S(1)}, u32[]{:S(2)}, u32[]{:S(2)}) collective-permute-start(bf16[272,512]{1,0:T(8,128)(2,1)S(1)} %get-tuple-element.24.m0), channel_id=1, source_target_pairs={{0,3},{1,0},{2,1},{3,2},{4,7},{5,4},{6,5},{7,6},{8,11},{9,8},{10,9... | collective-permute-start | bytes 835592 | tf_op jit(solution)/shard_map/ppermute | solution.py:275
  8.3 1.6 %collective-permute-start.3 = (bf16[9,16,128]{2,1,0:T(8,128)(2,1)S(1)}, bf16[9,16,128]{2,1,0:T(8,128)(2,1)S(1)}, u32[]{:S(2)}, u32[]{:S(2)}) collective-permute-start(bf16[9,16,128]{2,1,0:T(8,128)(2,1)S(1)} %get-tuple-element.29.own), channel_id=1, source_target_pairs={{0,8},{4,12},{8,16},{12,20},{16,24},{20,28},{24,0},{28,4},{32,40},... | collective-permute-start | bytes 110600 | tf_op jit(solution)/shard_map/ppermute | solution.py:288
  9.9 2.9 %collective-permute-start.4 = (bf16[9,16,128]{2,1,0:T(8,128)(2,1)S(1)}, bf16[9,16,128]{2,1,0:T(8,128)(2,1)S(1)}, u32[]{:S(2)}, u32[]{:S(2)}) collective-permute-start(bf16[9,16,128]{2,1,0:T(8,128)(2,1)S(1)} %get-tuple-element.29.own), channel_id=1, source_target_pairs={{0,16},{4,20},{8,24},{12,28},{16,0},{20,4},{24,8},{28,12},{32,48},... | collective-permute-start | bytes 110600 | tf_op jit(solution)/shard_map/ppermute | solution.py:288
  12.8 0.7 collective-permute-done.3.r1
  13.5 1.7 %collective-permute-start.5 = (bf16[9,16,128]{2,1,0:T(8,128)(2,1)S(1)}, bf16[9,16,128]{2,1,0:T(8,128)(2,1)S(1)}, u32[]{:S(2)}, u32[]{:S(2)}) collective-permute-start(bf16[9,16,128]{2,1,0:T(8,128)(2,1)S(1)} %get-tuple-element.29.own), channel_id=1, source_target_pairs={{0,24},{4,28},{8,0},{12,4},{16,8},{20,12},{24,16},{28,20},{32,56},... | collective-permute-start | bytes 110600 | tf_op jit(solution)/shard_map/ppermute | solution.py:288
  15.3 0.1 collective-permute-done.4.r2
  15.3 2.1 %collective-permute-done.5.r3 = bf16[9,16,128]{2,1,0:T(8,128)(2,1)S(1)} collective-permute-done((bf16[9,16,128]{2,1,0:T(8,128)(2,1)S(1)}, bf16[9,16,128]{2,1,0:T(8,128)(2,1)S(1)}, u32[]{:S(2)}, u32[]{:S(2)}) %collective-permute-start.5) | collective-permute-done | bytes 36896 | tf_op jit(solution)/shard_map/ppermute | solution.py:288
  17.5 1.6 %collective-permute-start.6 = (bf16[4,9,16,128]{3,2,1,0:T(8,128)(2,1)S(1)}, bf16[4,9,16,128]{3,2,1,0:T(8,128)(2,1)S(1)}, u32[]{:S(2)}, u32[]{:S(2)}) collective-permute-start(bf16[4,9,16,128]{3,2,1,0:T(8,128)(2,1)S(1)} %shard_map.141.own), channel_id=1, source_target_pairs={{0,32},{4,36},{8,40},{12,44},{16,48},{20,52},{24,56},{28,60},{32,6... | collective-permute-start | bytes 442376 | tf_op jit(solution)/shard_map/ppermute | solution.py:288
  19.1 2.7 %collective-permute-start.7 = (bf16[4,9,16,128]{3,2,1,0:T(8,128)(2,1)S(1)}, bf16[4,9,16,128]{3,2,1,0:T(8,128)(2,1)S(1)}, u32[]{:S(2)}, u32[]{:S(2)}) collective-permute-start(bf16[4,9,16,128]{3,2,1,0:T(8,128)(2,1)S(1)} %shard_map.141.own), channel_id=1, source_target_pairs={{0,64},{4,68},{8,72},{12,76},{16,80},{20,84},{24,88},{28,92},{32,9... | collective-permute-start | bytes 442376 | tf_op jit(solution)/shard_map/ppermute | solution.py:288
  21.8 0.0 collective-permute-done.m1
  21.8 1.4 %collective-permute-start.8 = (bf16[4,9,16,128]{3,2,1,0:T(8,128)(2,1)S(1)}, bf16[4,9,16,128]{3,2,1,0:T(8,128)(2,1)S(1)}, u32[]{:S(2)}, u32[]{:S(2)}) collective-permute-start(bf16[4,9,16,128]{3,2,1,0:T(8,128)(2,1)S(1)} %shard_map.141.own), channel_id=1, source_target_pairs={{0,96},{4,100},{8,104},{12,108},{16,112},{20,116},{24,120},{28,124... | collective-permute-start | bytes 442376 | tf_op jit(solution)/shard_map/ppermute | solution.py:288
  23.9 0.0 copy-start.1
  23.9 0.7 copy-done.1
  24.6 0.7 copy-done.2
  25.3 1.8 %shard_map.142 = (f32[1,512]{1,0:T(1,128)S(1)}, f32[1,128]{1,0:T(1,128)S(1)}, f32[512,512]{1,0:T(8,128)S(1)}, f32[128,512]{1,0:T(8,128)S(1)}) custom-call(s32[1]{0:T(128)} %bitcast.z_ref, s32[1]{0:T(128)S(6)} %copy.15.id_ref, f32[1024,512]{1,0:T(8,128)} %bank_ref.1, f32[512,512]{1,0:T(8,128)} %w1_hbm.1, f32[1,512]{1,0:T(1,128)S(1)} %bitcast.14, ...), custom_call_target="tpu_custom_call" | custom-call | tf_op jit(solution)/shard_map/pallas_call | solution.py:357
  27.1 0.0 copy-start.3
  27.1 0.0 copy-start
  27.1 0.0 collective-permute-done.1.m2
  27.1 0.0 collective-permute-done.2.m3
  27.1 0.5 shard_map.140
  27.6 0.0 collective-permute-done.6.r1
  27.6 0.0 collective-permute-done.7.r2
  27.7 0.1 shard_map.143.k0_ref
  27.7 0.1 collective-permute-start.9
  27.8 2.0 %collective-permute-done.9.k1_ref = bf16[4,4,9,16,128]{4,3,2,1,0:T(8,128)(2,1)S(1)} collective-permute-done((bf16[4,4,9,16,128]{4,3,2,1,0:T(8,128)(2,1)S(1)}, bf16[4,4,9,16,128]{4,3,2,1,0:T(8,128)(2,1)S(1)}, u32[]{:S(2)}, u32[]{:S(2)}) %collective-permute-start.9) | collective-permute-done | bytes 589856 | tf_op jit(solution)/shard_map/ppermute | solution.py:371
  29.8 4.3 %shard_map.144 = (bf16[32,9,16,128]{3,2,1,0:T(8,128)(2,1)S(1)}, f32[1,512]{1,0:T(1,128)S(1)}, f32[1024,128]{1,0:T(8,128)S(1)}, bf16[1024,128]{1,0:T(8,128)(2,1)S...) custom-call(s32[1]{0:T(128)} %bitcast.z_ref, s32[1]{0:T(128)} %bitcast.1.p_ref, ...), custom_call_target="tpu_custom_call" | custom-call | tf_op jit(solution)/shard_map/pallas_call | solution.py:372
  34.1 1.1 %collective-permute-start.10 = (f32[1,512]{1,0:T(1,128)S(1)}, f32[1,512]{1,0:T(1,128)S(1)}, u32[]{:S(2)}, u32[]{:S(2)}) collective-permute-start(f32[1,512]{1,0:T(1,128)S(1)} %get-tuple-element.34.u0), channel_id=1, source_target_pairs={{0,1},{1,2},{2,3},{3,0},{4,5},{5,6},{6,7},{7,4},{8,9},{9,10},{10,1... | collective-permute-start | bytes 6152 | tf_op jit(solution)/shard_map/ppermute | solution.py:275
  35.2 0.7 collective-permute-start.11
  35.9 2.0 %collective-permute-start.12 = (f32[1,512]{1,0:T(1,128)S(1)}, f32[1,512]{1,0:T(1,128)S(1)}, u32[]{:S(2)}, u32[]{:S(2)}) collective-permute-start(f32[1,512]{1,0:T(1,128)S(1)} %get-tuple-element.34.u0), channel_id=1, source_target_pairs={{0,3},{1,0},{2,1},{3,2},{4,7},{5,4},{6,5},{7,6},{8,11},{9,8},{10,9... | collective-permute-start | bytes 6152 | tf_op jit(solution)/shard_map/ppermute | solution.py:275
  37.9 1.0 %collective-permute-done.10.u1 = f32[1,512]{1,0:T(1,128)S(1)} collective-permute-done((f32[1,512]{1,0:T(1,128)S(1)}, f32[1,512]{1,0:T(1,128)S(1)}, u32[]{:S(2)}, u32[]{:S(2)}) %collective-permute-start.10) | collective-permute-done | bytes 2080 | tf_op jit(solution)/shard_map/ppermute | solution.py:275
  39.0 1.3 %collective-permute-done.11.u2 = f32[1,512]{1,0:T(1,128)S(1)} collective-permute-done((f32[1,512]{1,0:T(1,128)S(1)}, f32[1,512]{1,0:T(1,128)S(1)}, u32[]{:S(2)}, u32[]{:S(2)}) %collective-permute-start.11) | collective-permute-done | bytes 2080 | tf_op jit(solution)/shard_map/ppermute | solution.py:275
  40.3 0.0 collective-permute-done.12.u3
  40.3 5.3 %shard_map.145 = (bf16[32,152,128]{2,1,0:T(8,128)(2,1)}, f32[8,128]{1,0:T(8,128)S(1)}) custom-call(s32[1]{0:T(128)} %bitcast.z_ref, f32[1,512]{1,0:T(1,128)S(1)} %get-tuple-element.34.u0, f32[1,512]{1,0:T(1,128)S(1)} %collective-permute-done.10.u1, f32[1,512]{1,0:T(1,128)S(1)} %collective-permute-done.11.u2, f32[1,512]{1,0:T(1,128)S(1)} %collective-permute-done.12.u3, ...), custom_call_target="tpu_custom_call" | custom-call | tf_op jit(solution)/shard_map/pallas_call | solution.py:386
  45.5 6.0 %all-to-all-start = ((bf16[32,152,128]{2,1,0:T(8,128)(2,1)}), bf16[32,152,128]{2,1,0:T(8,128)(2,1)S(1)}, u32[]{:S(2)}, u32[]{:S(2)}) async-start(bf16[32,152,128]{2,1,0:T(8,128)(2,1)} %get-tuple-element.41), calls=%async_computation | async-start | bytes 2490368 | tf_op jit(solution)/shard_map/all_to_all | solution.py:396
  52.2 18.5 %all-to-all-done.part_ref = bf16[32,152,128]{2,1,0:T(8,128)(2,1)S(1)} async-done(((bf16[32,152,128]{2,1,0:T(8,128)(2,1)}), bf16[32,152,128]{2,1,0:T(8,128)(2,1)S(1)}, u32[]{:S(2)}, u32[]{:S(2)}) %all-to-all-start) | async-done | bytes 1245216 | tf_op jit(solution)/shard_map/all_to_all | solution.py:396
  70.7 0.3 shard_map.146
  71.0 1.6 %collective-permute-start.13 = (bf16[144,128]{1,0:T(8,128)(2,1)S(1)}, bf16[144,128]{1,0:T(8,128)(2,1)S(1)}, u32[]{:S(2)}, u32[]{:S(2)}) collective-permute-start(bf16[144,128]{1,0:T(8,128)(2,1)S(1)} %get-tuple-element.42.p0), channel_id=1, source_target_pairs={{0,1},{1,2},{2,3},{3,0},{4,5},{5,6},{6,7},{7,4},{8,9},{9,10},{10,1... | collective-permute-start | bytes 110600 | tf_op jit(solution)/shard_map/ppermute | solution.py:275
  72.6 2.4 %collective-permute-start.14 = (bf16[144,128]{1,0:T(8,128)(2,1)S(1)}, bf16[144,128]{1,0:T(8,128)(2,1)S(1)}, u32[]{:S(2)}, u32[]{:S(2)}) collective-permute-start(bf16[144,128]{1,0:T(8,128)(2,1)S(1)} %get-tuple-element.42.p0), channel_id=1, source_target_pairs={{0,2},{1,3},{2,0},{3,1},{4,6},{5,7},{6,4},{7,5},{8,10},{9,11},{10,... | collective-permute-start | bytes 110600 | tf_op jit(solution)/shard_map/ppermute | solution.py:275
  75.0 0.7 collective-permute-start.15
  75.7 0.5 slice.6
  76.2 0.5 slice.7
  76.8 0.0 collective-permute-done.13.p1
  76.8 1.3 %collective-permute-done.14.p2 = bf16[144,128]{1,0:T(8,128)(2,1)S(1)} collective-permute-done((bf16[144,128]{1,0:T(8,128)(2,1)S(1)}, bf16[144,128]{1,0:T(8,128)(2,1)S(1)}, u32[]{:S(2)}, u32[]{:S(2)}) %collective-permute-start.14) | collective-permute-done | bytes 36896 | tf_op jit(solution)/shard_map/ppermute | solution.py:275
  78.1 0.9 %collective-permute-done.15.p3 = bf16[144,128]{1,0:T(8,128)(2,1)S(1)} collective-permute-done((bf16[144,128]{1,0:T(8,128)(2,1)S(1)}, bf16[144,128]{1,0:T(8,128)(2,1)S(1)}, u32[]{:S(2)}, u32[]{:S(2)}) %collective-permute-start.15) | collective-permute-done | bytes 36896 | tf_op jit(solution)/shard_map/ppermute | solution.py:275
  79.0 0.8 shard_map.147
  (6 shorter events, 0.0 us)
Async XLA Ops:
  1.6 20.2 %collective-permute-start = (bf16[272,512]{1,0:T(8,128)(2,1)S(1)}, bf16[272,512]{1,0:T(8,128)(2,1)S(1)}, u32[]{:S(2)}, u32[]{:S(2)}) collective-permute-start(bf16[272,512]{1,0:T(8,128)(2,1)S(1)} %get-tuple-element.24.m0), channel_id=1, source_target_pairs={{0,1},{1,2},{2,3},{3,0},{4,5},{5,6},{6,7},{7,4},{8,9},{9,10},{10,1... | collective-permute-start | bytes 835592 | tf_op jit(solution)/shard_map/ppermute | solution.py:275
  3.7 23.4 %collective-permute-start.1 = (bf16[272,512]{1,0:T(8,128)(2,1)S(1)}, bf16[272,512]{1,0:T(8,128)(2,1)S(1)}, u32[]{:S(2)}, u32[]{:S(2)}) collective-permute-start(bf16[272,512]{1,0:T(8,128)(2,1)S(1)} %get-tuple-element.24.m0), channel_id=1, source_target_pairs={{0,2},{1,3},{2,0},{3,1},{4,6},{5,7},{6,4},{7,5},{8,10},{9,11},{10,... | collective-permute-start | bytes 835592 | tf_op jit(solution)/shard_map/ppermute | solution.py:275
  7.3 19.8 %collective-permute-start.2 = (bf16[272,512]{1,0:T(8,128)(2,1)S(1)}, bf16[272,512]{1,0:T(8,128)(2,1)S(1)}, u32[]{:S(2)}, u32[]{:S(2)}) collective-permute-start(bf16[272,512]{1,0:T(8,128)(2,1)S(1)} %get-tuple-element.24.m0), channel_id=1, source_target_pairs={{0,3},{1,0},{2,1},{3,2},{4,7},{5,4},{6,5},{7,6},{8,11},{9,8},{10,9... | collective-permute-start | bytes 835592 | tf_op jit(solution)/shard_map/ppermute | solution.py:275
  8.3 5.2 %collective-permute-start.3 = (bf16[9,16,128]{2,1,0:T(8,128)(2,1)S(1)}, bf16[9,16,128]{2,1,0:T(8,128)(2,1)S(1)}, u32[]{:S(2)}, u32[]{:S(2)}) collective-permute-start(bf16[9,16,128]{2,1,0:T(8,128)(2,1)S(1)} %get-tuple-element.29.own), channel_id=1, source_target_pairs={{0,8},{4,12},{8,16},{12,20},{16,24},{20,28},{24,0},{28,4},{32,40},... | collective-permute-start | bytes 110600 | tf_op jit(solution)/shard_map/ppermute | solution.py:288
  9.9 5.5 %collective-permute-start.4 = (bf16[9,16,128]{2,1,0:T(8,128)(2,1)S(1)}, bf16[9,16,128]{2,1,0:T(8,128)(2,1)S(1)}, u32[]{:S(2)}, u32[]{:S(2)}) collective-permute-start(bf16[9,16,128]{2,1,0:T(8,128)(2,1)S(1)} %get-tuple-element.29.own), channel_id=1, source_target_pairs={{0,16},{4,20},{8,24},{12,28},{16,0},{20,4},{24,8},{28,12},{32,48},... | collective-permute-start | bytes 110600 | tf_op jit(solution)/shard_map/ppermute | solution.py:288
  13.5 4.0 %collective-permute-start.5 = (bf16[9,16,128]{2,1,0:T(8,128)(2,1)S(1)}, bf16[9,16,128]{2,1,0:T(8,128)(2,1)S(1)}, u32[]{:S(2)}, u32[]{:S(2)}) collective-permute-start(bf16[9,16,128]{2,1,0:T(8,128)(2,1)S(1)} %get-tuple-element.29.own), channel_id=1, source_target_pairs={{0,24},{4,28},{8,0},{12,4},{16,8},{20,12},{24,16},{28,20},{32,56},... | collective-permute-start | bytes 110600 | tf_op jit(solution)/shard_map/ppermute | solution.py:288
  17.5 10.1 %collective-permute-start.6 = (bf16[4,9,16,128]{3,2,1,0:T(8,128)(2,1)S(1)}, bf16[4,9,16,128]{3,2,1,0:T(8,128)(2,1)S(1)}, u32[]{:S(2)}, u32[]{:S(2)}) collective-permute-start(bf16[4,9,16,128]{3,2,1,0:T(8,128)(2,1)S(1)} %shard_map.141.own), channel_id=1, source_target_pairs={{0,32},{4,36},{8,40},{12,44},{16,48},{20,52},{24,56},{28,60},{32,6... | collective-permute-start | bytes 442376 | tf_op jit(solution)/shard_map/ppermute | solution.py:288
  19.1 8.6 %collective-permute-start.7 = (bf16[4,9,16,128]{3,2,1,0:T(8,128)(2,1)S(1)}, bf16[4,9,16,128]{3,2,1,0:T(8,128)(2,1)S(1)}, u32[]{:S(2)}, u32[]{:S(2)}) collective-permute-start(bf16[4,9,16,128]{3,2,1,0:T(8,128)(2,1)S(1)} %shard_map.141.own), channel_id=1, source_target_pairs={{0,64},{4,68},{8,72},{12,76},{16,80},{20,84},{24,88},{28,92},{32,9... | collective-permute-start | bytes 442376 | tf_op jit(solution)/shard_map/ppermute | solution.py:288
  21.8 5.8 %collective-permute-start.8 = (bf16[4,9,16,128]{3,2,1,0:T(8,128)(2,1)S(1)}, bf16[4,9,16,128]{3,2,1,0:T(8,128)(2,1)S(1)}, u32[]{:S(2)}, u32[]{:S(2)}) collective-permute-start(bf16[4,9,16,128]{3,2,1,0:T(8,128)(2,1)S(1)} %shard_map.141.own), channel_id=1, source_target_pairs={{0,96},{4,100},{8,104},{12,108},{16,112},{20,116},{24,120},{28,124... | collective-permute-start | bytes 442376 | tf_op jit(solution)/shard_map/ppermute | solution.py:288
  23.9 0.7 copy-start.1
  24.6 0.7 copy-start.2
  27.1 0.7 copy-start.3
  27.1 2.7 %copy-start = (f32[512]{0:T(512)S(1)}, f32[512]{0:T(512)}, u32[]{:S(2)}) copy-start(f32[512]{0:T(512)} %param.21) | copy-start | bytes 6148
  27.7 2.1 %collective-permute-start.9 = (bf16[4,4,9,16,128]{4,3,2,1,0:T(8,128)(2,1)S(1)}, bf16[4,4,9,16,128]{4,3,2,1,0:T(8,128)(2,1)S(1)}, u32[]{:S(2)}, u32[]{:S(2)}) collective-permute-start(bf16[4,4,9,16,128]{4,3,2,1,0:T(8,128)(2,1)S(1)} %shard_map.143.k0_ref), channel_id=1, source_target_pairs={{0,4},{4,0},{8,12},{12,8},{16,20},{20,16},{24,28},{28,24},{32,36},... | collective-permute-start | bytes 1769480 | tf_op jit(solution)/shard_map/ppermute | solution.py:371
  34.1 4.9 %collective-permute-start.10 = (f32[1,512]{1,0:T(1,128)S(1)}, f32[1,512]{1,0:T(1,128)S(1)}, u32[]{:S(2)}, u32[]{:S(2)}) collective-permute-start(f32[1,512]{1,0:T(1,128)S(1)} %get-tuple-element.34.u0), channel_id=1, source_target_pairs={{0,1},{1,2},{2,3},{3,0},{4,5},{5,6},{6,7},{7,4},{8,9},{9,10},{10,1... | collective-permute-start | bytes 6152 | tf_op jit(solution)/shard_map/ppermute | solution.py:275
  35.2 5.1 %collective-permute-start.11 = (f32[1,512]{1,0:T(1,128)S(1)}, f32[1,512]{1,0:T(1,128)S(1)}, u32[]{:S(2)}, u32[]{:S(2)}) collective-permute-start(f32[1,512]{1,0:T(1,128)S(1)} %get-tuple-element.34.u0), channel_id=1, source_target_pairs={{0,2},{1,3},{2,0},{3,1},{4,6},{5,7},{6,4},{7,5},{8,10},{9,11},{10,... | collective-permute-start | bytes 6152 | tf_op jit(solution)/shard_map/ppermute | solution.py:275
  35.9 4.4 %collective-permute-start.12 = (f32[1,512]{1,0:T(1,128)S(1)}, f32[1,512]{1,0:T(1,128)S(1)}, u32[]{:S(2)}, u32[]{:S(2)}) collective-permute-start(f32[1,512]{1,0:T(1,128)S(1)} %get-tuple-element.34.u0), channel_id=1, source_target_pairs={{0,3},{1,0},{2,1},{3,2},{4,7},{5,4},{6,5},{7,6},{8,11},{9,8},{10,9... | collective-permute-start | bytes 6152 | tf_op jit(solution)/shard_map/ppermute | solution.py:275
  45.5 25.2 %all-to-all-start = ((bf16[32,152,128]{2,1,0:T(8,128)(2,1)}), bf16[32,152,128]{2,1,0:T(8,128)(2,1)S(1)}, u32[]{:S(2)}, u32[]{:S(2)}) async-start(bf16[32,152,128]{2,1,0:T(8,128)(2,1)} %get-tuple-element.41), calls=%async_computation | async-start | bytes 2490368 | tf_op jit(solution)/shard_map/all_to_all | solution.py:396
  71.0 5.7 %collective-permute-start.13 = (bf16[144,128]{1,0:T(8,128)(2,1)S(1)}, bf16[144,128]{1,0:T(8,128)(2,1)S(1)}, u32[]{:S(2)}, u32[]{:S(2)}) collective-permute-start(bf16[144,128]{1,0:T(8,128)(2,1)S(1)} %get-tuple-element.42.p0), channel_id=1, source_target_pairs={{0,1},{1,2},{2,3},{3,0},{4,5},{5,6},{6,7},{7,4},{8,9},{9,10},{10,1... | collective-permute-start | bytes 110600 | tf_op jit(solution)/shard_map/ppermute | solution.py:275
  72.6 5.5 %collective-permute-start.14 = (bf16[144,128]{1,0:T(8,128)(2,1)S(1)}, bf16[144,128]{1,0:T(8,128)(2,1)S(1)}, u32[]{:S(2)}, u32[]{:S(2)}) collective-permute-start(bf16[144,128]{1,0:T(8,128)(2,1)S(1)} %get-tuple-element.42.p0), channel_id=1, source_target_pairs={{0,2},{1,3},{2,0},{3,1},{4,6},{5,7},{6,4},{7,5},{8,10},{9,11},{10,... | collective-permute-start | bytes 110600 | tf_op jit(solution)/shard_map/ppermute | solution.py:275
  75.0 4.0 %collective-permute-start.15 = (bf16[144,128]{1,0:T(8,128)(2,1)S(1)}, bf16[144,128]{1,0:T(8,128)(2,1)S(1)}, u32[]{:S(2)}, u32[]{:S(2)}) collective-permute-start(bf16[144,128]{1,0:T(8,128)(2,1)S(1)} %get-tuple-element.42.p0), channel_id=1, source_target_pairs={{0,3},{1,0},{2,1},{3,2},{4,7},{5,4},{6,5},{7,6},{8,11},{9,8},{10,9... | collective-permute-start | bytes 110600 | tf_op jit(solution)/shard_map/ppermute | solution.py:275

commit v5 on v4

--- a/solution.py
+++ b/solution.py
@@ -40,13 +40,16 @@
 
 
 def styles_kernel(
-    z_ref, id_ref, bank_ref, w1_hbm, b1_ref, w2_hbm, b2_ref, s_ref, c_ref, w1t_ref, w2t_ref, w_buf, w1_ref, w2_ref, sems
+    z_ref, id_ref, bank_ref, w1_hbm, b1_hbm, w2_hbm, b2_hbm, s_ref, c_ref, w1t_ref, w2t_ref,
+    w_buf, w1_ref, w2_ref, b1_ref, b2_ref, sems,
 ):
     mine = pl.ds(pl.multiple_of(z_ref[0] * OC, OC), OC)
     copies = [
         pltpu.make_async_copy(bank_ref.at[pl.ds(id_ref[0], 1)], w_buf, sems.at[0]),
         pltpu.make_async_copy(w2_hbm.at[:, mine], w2_ref, sems.at[1]),
         pltpu.make_async_copy(w1_hbm, w1_ref, sems.at[2]),
+        pltpu.make_async_copy(b1_hbm, b1_ref, sems.at[3]),
+        pltpu.make_async_copy(b2_hbm, b2_ref, sems.at[4]),
     ]
     for copy in copies:
         copy.start()
@@ -117,9 +120,18 @@
     return rgb, jnp.concatenate([mod, mod, mod, jnp.zeros((119, OC), F32)], axis=0).astype(BF16)
 
 
+def ahead_kernel(z_ref, dt_ref, c_ref, rgb_ref, k0_ref, ga_ref, half_ref):
+    _, mix = colours_of(rgb_ref, c_ref[...], z_ref[0])
+    ga_ref[...] = (dot(dt_ref[...], mix) * (1.0 / math.sqrt(NPOS))).astype(BF16)
+    for x in range(4):
+        for y in range(4):
+            k = k0_ref[x, y].astype(F32)
+            half_ref[4 * x + y] = jnp.sum(k * k, axis=0)
+
+
 def first_kernel(
-    z_ref, p_ref, f_ref, ft_ref, d_ref, dt_ref, k0_ref, k1_ref, s_ref, c_ref, rgb_ref, bias_ref, w1t_ref, w2t_ref,
-    k_ref, u_ref, pre_ref, ga_ref, gm_ref, e_ref, rows_ref,
+    z_ref, p_ref, f_ref, ft_ref, d_ref, ga_ref, half_ref, k0_ref, k1_ref, s_ref, rgb_ref, bias_ref, w1t_ref, w2t_ref,
+    k_ref, u_ref, pre_ref, gm_ref, e_ref, rows_ref,
 ):
     z = z_ref[0]
     lo = pl.multiple_of(z * OC, OC)
@@ -130,11 +142,10 @@
             chip = 8 * x + 2 * y
             k_ref[chip + core] = k0_ref[x, y]
             k_ref[chip + 1 - core] = k1_ref[x, y]
-    energy = None
-    for t in range(9):
-        k = tap(k_ref, t)
-        energy = k * k if energy is None else energy + k * k
-    e_ref[...] = energy
+            other = k1_ref[x, y].astype(F32)
+            e_ref[chip + core] = half_ref[4 * x + y]
+            e_ref[chip + 1 - core] = jnp.sum(other * other, axis=0)
+    energy = e_ref[...].reshape(CH, OC)
     s = lanes_of(s_ref[...])
     demod = lax.rsqrt(jnp.sum(s * s * energy, axis=0, keepdims=True) + 1e-08)
     sd = s * demod
@@ -146,10 +157,8 @@
     square = pre * pre + 0.25
     root = lax.rsqrt(square)
     act = ((0.6 * pre + 0.4 * (square * root)) * SQRT_TWO).astype(BF16)
-    rgb, mix = colours_of(rgb_ref, c_ref[...], z)
-    ga = (dot(dt_ref[...], mix) * scaling).astype(BF16)
-    ga_ref[...] = ga
-    h = ga.astype(F32) * ((0.6 + 0.4 * (pre * root)) * SQRT_TWO)
+    rgb = rgb_ref[:, pl.ds(lo, OC)]
+    h = ga_ref[...].astype(F32) * ((0.6 + 0.4 * (pre * root)) * SQRT_TWO)
     parts = dot(d_ref[...], act)
     grad_mix = ((parts[0:3] + parts[3:6] + parts[6:9]) * scaling).astype(BF16).astype(F32)
     grad_colour = jnp.sum(grad_mix * rgb[0:3], axis=0, keepdims=True)
@@ -196,7 +205,7 @@
     dc_lanes = jnp.broadcast_to(jnp.sum(w2t_ref[...] * grad, axis=1, keepdims=True), (OC, OC))
     dc = jnp.transpose(dc_lanes)[0:1, :]
     s = lanes_of(s_ref[...])
-    energy = e_ref[...]
+    energy = e_ref[...].reshape(CH, OC)
     demod = rows_ref[0:1, :]
     grad_demod = rows_ref[1:2, :]
     cube = demod * demod * demod
@@ -357,10 +366,17 @@
     s, c, w1t, w2t = call(
         styles_kernel,
         (shape((1, CH), F32), shape((1, OC), F32), shape((CH, CH), F32), shape((OC, CH), F32)),
-        [full(SMEM), full(SMEM), full(pltpu.HBM), full(pltpu.HBM), full(), full(pltpu.HBM), full()],
+        [full(SMEM)] * 2 + [full(pltpu.HBM)] * 5,
         8,
-        [VMEM((1, CH), F32), VMEM((CH, CH), F32), VMEM((CH, OC), F32), pltpu.SemaphoreType.DMA((3,))],
-    )(z, latent_ids, pinned(latent_bank), pinned(style_one), b1, pinned(style_two), b2)
+        [
+            VMEM((1, CH), F32),
+            VMEM((CH, CH), F32),
+            VMEM((CH, OC), F32),
+            VMEM((1, CH), F32),
+            VMEM((1, CH), F32),
+            pltpu.SemaphoreType.DMA((5,)),
+        ],
+    )(z, latent_ids, pinned(latent_bank), pinned(style_one), pinned(b1), pinned(style_two), pinned(b2))
     image, turned, marks_all, marks_turned = call(
         image_kernel,
         (shape((NPOS, CH), BF16), shape((CH, NPOS), BF16), shape((16, NPOS), BF16), shape((NPOS, OC), BF16)),
@@ -369,20 +385,25 @@
     )(z, message, *others)
     plane = stacked(di, 8, column, permuted(column, lambda x, y, c, k: (x + k, y, c)), [s, marks_all])
     sibling = lax.ppermute(plane, "dp", [(i, i ^ 1) for i in range(NDP)])
-    kernel, u, pre, ga, gm, energy, rows = call(
+    ga, half = call(
+        ahead_kernel,
+        (shape((NPOS, OC), BF16), shape((NDP // 2, 16, OC), F32)),
+        [full(SMEM)] + [full()] * 4,
+        8,
+    )(z, marks_turned, c, rgb, plane)
+    kernel, u, pre, gm, energy, rows = call(
         first_kernel,
         (
             shape((NDP, 9, 16, OC), BF16),
             shape((1, CH), F32),
             shape((NPOS, OC), F32),
-            shape((NPOS, OC), BF16),
             shape((3, CH, 3 * OC), BF16),
-            shape((CH, OC), F32),
+            shape((NDP, 16, OC), F32),
             shape((8, OC), F32),
         ),
         [full(SMEM)] * 2 + [full()] * 12,
         16,
-    )(z, di, image, turned, marks_all, marks_turned, plane, sibling, s, c, rgb, bias, w1t, w2t)
+    )(z, di, image, turned, marks_all, ga, half, plane, sibling, s, rgb, bias, w1t, w2t)
     parts, length = call(
         second_kernel,
         (pltpu.HBM((NDP, 152, OC), BF16), shape((8, OC), F32)),

time: 80.1 us -> 80 us (level)
  local copies, waits for them, and re-layouts: 2.4 us -> 1.04 us
    unnamed x8 -> x4, local copies, waits for them, and re-layouts: 1.37 us -> 0.01 us
  transfers between devices with their start and end apart: 17 -> 17, of which waited for: 9 -> 11; matrix products, arithmetic and copies ran while one was open for 1% -> 1% of each run, Pallas kernels for 3% -> 3%
where the time goes in v5:
time: 80 us; the launch traced here: 79.7 us
  starting transfers between devices  34 us (42%)
  waiting for transfers between devices  28.4 us (36%)
  Pallas kernels  14.2 us (18%)
  between operations  2.06 us (3%)
  local copies, waits for them, and re-layouts  1.04 us (1%)
    all_to_all x1, waiting for transfers between devices, per_device(): received = lax.all_to_all(parts, 'dp', 0, 0, tiled=True)  18.5 us
    ppermute x9, starting transfers between devices, ring(): lax.ppermute(x, axis, [(i, (i + k) % size) for i in range(size)])  15.2 us
    ppermute x6, starting transfers between devices, permuted(): lax.ppermute(value, 'dp', [(place(x, y, c), place(*to(x, y, c, k))) for x...  11.9 us
    all_to_all x1, starting transfers between devices, per_device(): received = lax.all_to_all(parts, 'dp', 0, 0, tiled=True)  6.71 us
    pallas_call x1, Pallas kernels, per_device(): call(second_kernel, (pltpu.HBM((NDP, 152, OC), BF16), shape((8, OC), F32)...  5.35 us
    ppermute x9, waiting for transfers between devices, ring(): lax.ppermute(x, axis, [(i, (i + k) % size) for i in range(size)])  4.54 us
    pallas_call x1, Pallas kernels, per_device(): call(first_kernel, (shape((NDP, 9, 16, OC), BF16), shape((1, CH), F32), s...  4.2 us
    ppermute x6, waiting for transfers between devices, permuted(): lax.ppermute(value, 'dp', [(place(x, y, c), place(*to(x, y, c, k))) for x...  3.61 us
  transfers between devices with their start and end apart: 17, of which 11 were waited for; matrix products, arithmetic and copies ran while one was open for 1% of the time, Pallas kernels for 3%

profile of v5, /device:TPU:0, one launch (start us, length us, event | category | flops | bytes accessed | tf_op | source)
XLA Modules:
  0.0 79.7 jit_solution(12487027122375699772)
XLA Ops:
  0.6 1.0 %shard_map.139 = (bf16[272,512]{1,0:T(8,128)(2,1)S(1)}, bf16[9,16,128]{2,1,0:T(8,128)(2,1)S(1)}) custom-call(s32[1]{0:T(128)} %bitcast.z_ref, bf16[256,512]{1,0:T(8,128)(2,1)} %bitcast.15, f32[3,2,128]{2,1,0:T(2,128)} %bitcast.18, bf16[9,16,512]{2,1,0:T(8,128)(2,1)} %bitcast.16), custom_call_target="tpu_custom_call" | custom-call | tf_op jit(solution)/shard_map/pallas_call | solution.py:348
  1.6 2.1 %collective-permute-start = (bf16[272,512]{1,0:T(8,128)(2,1)S(1)}, bf16[272,512]{1,0:T(8,128)(2,1)S(1)}, u32[]{:S(2)}, u32[]{:S(2)}) collective-permute-start(bf16[272,512]{1,0:T(8,128)(2,1)S(1)} %get-tuple-element.25.m0), channel_id=1, source_target_pairs={{0,1},{1,2},{2,3},{3,0},{4,5},{5,6},{6,7},{7,4},{8,9},{9,10},{10,1... | collective-permute-start | bytes 835592 | tf_op jit(solution)/shard_map/ppermute | solution.py:284
  3.7 3.6 %collective-permute-start.1 = (bf16[272,512]{1,0:T(8,128)(2,1)S(1)}, bf16[272,512]{1,0:T(8,128)(2,1)S(1)}, u32[]{:S(2)}, u32[]{:S(2)}) collective-permute-start(bf16[272,512]{1,0:T(8,128)(2,1)S(1)} %get-tuple-element.25.m0), channel_id=1, source_target_pairs={{0,2},{1,3},{2,0},{3,1},{4,6},{5,7},{6,4},{7,5},{8,10},{9,11},{10,... | collective-permute-start | bytes 835592 | tf_op jit(solution)/shard_map/ppermute | solution.py:284
  7.3 1.0 %collective-permute-start.2 = (bf16[272,512]{1,0:T(8,128)(2,1)S(1)}, bf16[272,512]{1,0:T(8,128)(2,1)S(1)}, u32[]{:S(2)}, u32[]{:S(2)}) collective-permute-start(bf16[272,512]{1,0:T(8,128)(2,1)S(1)} %get-tuple-element.25.m0), channel_id=1, source_target_pairs={{0,3},{1,0},{2,1},{3,2},{4,7},{5,4},{6,5},{7,6},{8,11},{9,8},{10,9... | collective-permute-start | bytes 835592 | tf_op jit(solution)/shard_map/ppermute | solution.py:284
  8.3 1.6 %collective-permute-start.3 = (bf16[9,16,128]{2,1,0:T(8,128)(2,1)S(1)}, bf16[9,16,128]{2,1,0:T(8,128)(2,1)S(1)}, u32[]{:S(2)}, u32[]{:S(2)}) collective-permute-start(bf16[9,16,128]{2,1,0:T(8,128)(2,1)S(1)} %get-tuple-element.31.own), channel_id=1, source_target_pairs={{0,8},{4,12},{8,16},{12,20},{16,24},{20,28},{24,0},{28,4},{32,40},... | collective-permute-start | bytes 110600 | tf_op jit(solution)/shard_map/ppermute | solution.py:297
  9.9 2.9 %collective-permute-start.4 = (bf16[9,16,128]{2,1,0:T(8,128)(2,1)S(1)}, bf16[9,16,128]{2,1,0:T(8,128)(2,1)S(1)}, u32[]{:S(2)}, u32[]{:S(2)}) collective-permute-start(bf16[9,16,128]{2,1,0:T(8,128)(2,1)S(1)} %get-tuple-element.31.own), channel_id=1, source_target_pairs={{0,16},{4,20},{8,24},{12,28},{16,0},{20,4},{24,8},{28,12},{32,48},... | collective-permute-start | bytes 110600 | tf_op jit(solution)/shard_map/ppermute | solution.py:297
  12.8 0.7 collective-permute-done.3.r1
  13.5 1.7 %collective-permute-start.5 = (bf16[9,16,128]{2,1,0:T(8,128)(2,1)S(1)}, bf16[9,16,128]{2,1,0:T(8,128)(2,1)S(1)}, u32[]{:S(2)}, u32[]{:S(2)}) collective-permute-start(bf16[9,16,128]{2,1,0:T(8,128)(2,1)S(1)} %get-tuple-element.31.own), channel_id=1, source_target_pairs={{0,24},{4,28},{8,0},{12,4},{16,8},{20,12},{24,16},{28,20},{32,56},... | collective-permute-start | bytes 110600 | tf_op jit(solution)/shard_map/ppermute | solution.py:297
  15.3 0.1 collective-permute-done.4.r2
  15.3 2.1 %collective-permute-done.5.r3 = bf16[9,16,128]{2,1,0:T(8,128)(2,1)S(1)} collective-permute-done((bf16[9,16,128]{2,1,0:T(8,128)(2,1)S(1)}, bf16[9,16,128]{2,1,0:T(8,128)(2,1)S(1)}, u32[]{:S(2)}, u32[]{:S(2)}) %collective-permute-start.5) | collective-permute-done | bytes 36896 | tf_op jit(solution)/shard_map/ppermute | solution.py:297
  17.5 1.6 %collective-permute-start.6 = (bf16[4,9,16,128]{3,2,1,0:T(8,128)(2,1)S(1)}, bf16[4,9,16,128]{3,2,1,0:T(8,128)(2,1)S(1)}, u32[]{:S(2)}, u32[]{:S(2)}) collective-permute-start(bf16[4,9,16,128]{3,2,1,0:T(8,128)(2,1)S(1)} %shard_map.142.own), channel_id=1, source_target_pairs={{0,32},{4,36},{8,40},{12,44},{16,48},{20,52},{24,56},{28,60},{32,6... | collective-permute-start | bytes 442376 | tf_op jit(solution)/shard_map/ppermute | solution.py:297
  19.1 2.7 %collective-permute-start.7 = (bf16[4,9,16,128]{3,2,1,0:T(8,128)(2,1)S(1)}, bf16[4,9,16,128]{3,2,1,0:T(8,128)(2,1)S(1)}, u32[]{:S(2)}, u32[]{:S(2)}) collective-permute-start(bf16[4,9,16,128]{3,2,1,0:T(8,128)(2,1)S(1)} %shard_map.142.own), channel_id=1, source_target_pairs={{0,64},{4,68},{8,72},{12,76},{16,80},{20,84},{24,88},{28,92},{32,9... | collective-permute-start | bytes 442376 | tf_op jit(solution)/shard_map/ppermute | solution.py:297
  21.8 0.0 collective-permute-done.m1
  21.8 1.4 %collective-permute-start.8 = (bf16[4,9,16,128]{3,2,1,0:T(8,128)(2,1)S(1)}, bf16[4,9,16,128]{3,2,1,0:T(8,128)(2,1)S(1)}, u32[]{:S(2)}, u32[]{:S(2)}) collective-permute-start(bf16[4,9,16,128]{3,2,1,0:T(8,128)(2,1)S(1)} %shard_map.142.own), channel_id=1, source_target_pairs={{0,96},{4,100},{8,104},{12,108},{16,112},{20,116},{24,120},{28,124... | collective-permute-start | bytes 442376 | tf_op jit(solution)/shard_map/ppermute | solution.py:297
  23.9 1.9 %shard_map.141 = (f32[1,512]{1,0:T(1,128)S(1)}, f32[1,128]{1,0:T(1,128)S(1)}, f32[512,512]{1,0:T(8,128)S(1)}, f32[128,512]{1,0:T(8,128)S(1)}) custom-call(s32[1]{0:T(128)} %bitcast.z_ref, s32[1]{0:T(128)S(6)} %copy.15.id_ref, f32[1024,512]{1,0:T(8,128)} %bank_ref.1, f32[512,512]{1,0:T(8,128)} %w1_hbm.1, f32[1,512]{1,0:T(1,128)} %bitcast.19, ...), custom_call_target="tpu_custom_call" | custom-call | tf_op jit(solution)/shard_map/pallas_call | solution.py:366
  25.7 0.0 copy-start.1
  25.8 0.0 collective-permute-done.1.m2
  25.8 0.0 collective-permute-done.2.m3
  25.8 0.5 shard_map.140
  26.3 0.0 copy-start
  26.3 0.0 collective-permute-done.6.r1
  26.3 0.2 collective-permute-done.7.r2
  26.5 0.5 collective-permute-done.8.r3
  26.9 0.1 shard_map.143.k0_ref
  27.0 0.1 collective-permute-start.9
  27.1 0.0 copy-done.1
  27.1 0.2 shard_map.144
  27.3 1.8 %collective-permute-done.9.k1_ref = bf16[4,4,9,16,128]{4,3,2,1,0:T(8,128)(2,1)S(1)} collective-permute-done((bf16[4,4,9,16,128]{4,3,2,1,0:T(8,128)(2,1)S(1)}, bf16[4,4,9,16,128]{4,3,2,1,0:T(8,128)(2,1)S(1)}, u32[]{:S(2)}, u32[]{:S(2)}) %collective-permute-start.9) | collective-permute-done | bytes 589856 | tf_op jit(solution)/shard_map/ppermute | solution.py:387
  29.1 4.2 %shard_map.145 = (bf16[32,9,16,128]{3,2,1,0:T(8,128)(2,1)S(1)}, f32[1,512]{1,0:T(1,128)S(1)}, f32[1024,128]{1,0:T(8,128)S(1)}, bf16[3,512,384]{2,1,0:T(8,128)(2,...) custom-call(s32[1]{0:T(128)} %bitcast.z_ref, s32[1]{0:T(128)} %bitcast.1.p_ref, ...), custom_call_target="tpu_custom_call" | custom-call | tf_op jit(solution)/shard_map/pallas_call | solution.py:394
  33.3 1.1 %collective-permute-start.10 = (f32[1,512]{1,0:T(1,128)S(1)}, f32[1,512]{1,0:T(1,128)S(1)}, u32[]{:S(2)}, u32[]{:S(2)}) collective-permute-start(f32[1,512]{1,0:T(1,128)S(1)} %get-tuple-element.37.u0), channel_id=1, source_target_pairs={{0,1},{1,2},{2,3},{3,0},{4,5},{5,6},{6,7},{7,4},{8,9},{9,10},{10,1... | collective-permute-start | bytes 6152 | tf_op jit(solution)/shard_map/ppermute | solution.py:284
  34.4 0.7 collective-permute-start.11
  35.1 2.0 %collective-permute-start.12 = (f32[1,512]{1,0:T(1,128)S(1)}, f32[1,512]{1,0:T(1,128)S(1)}, u32[]{:S(2)}, u32[]{:S(2)}) collective-permute-start(f32[1,512]{1,0:T(1,128)S(1)} %get-tuple-element.37.u0), channel_id=1, source_target_pairs={{0,3},{1,0},{2,1},{3,2},{4,7},{5,4},{6,5},{7,6},{8,11},{9,8},{10,9... | collective-permute-start | bytes 6152 | tf_op jit(solution)/shard_map/ppermute | solution.py:284
  37.1 1.0 %collective-permute-done.10.u1 = f32[1,512]{1,0:T(1,128)S(1)} collective-permute-done((f32[1,512]{1,0:T(1,128)S(1)}, f32[1,512]{1,0:T(1,128)S(1)}, u32[]{:S(2)}, u32[]{:S(2)}) %collective-permute-start.10) | collective-permute-done | bytes 2080 | tf_op jit(solution)/shard_map/ppermute | solution.py:284
  38.1 1.3 %collective-permute-done.11.u2 = f32[1,512]{1,0:T(1,128)S(1)} collective-permute-done((f32[1,512]{1,0:T(1,128)S(1)}, f32[1,512]{1,0:T(1,128)S(1)}, u32[]{:S(2)}, u32[]{:S(2)}) %collective-permute-start.11) | collective-permute-done | bytes 2080 | tf_op jit(solution)/shard_map/ppermute | solution.py:284
  39.5 0.0 collective-permute-done.12.u3
  39.5 5.4 %shard_map.146 = (bf16[32,152,128]{2,1,0:T(8,128)(2,1)}, f32[8,128]{1,0:T(8,128)S(1)}) custom-call(s32[1]{0:T(128)} %bitcast.z_ref, f32[1,512]{1,0:T(1,128)S(1)} %get-tuple-element.37.u0, f32[1,512]{1,0:T(1,128)S(1)} %collective-permute-done.10.u1, f32[1,512]{1,0:T(1,128)S(1)} %collective-permute-done.11.u2, f32[1,512]{1,0:T(1,128)S(1)} %collective-permute-done.12.u3, ...), custom_call_target="tpu_custom_call" | custom-call | tf_op jit(solution)/shard_map/pallas_call | solution.py:407
  44.8 6.7 %all-to-all-start = ((bf16[32,152,128]{2,1,0:T(8,128)(2,1)}), bf16[32,152,128]{2,1,0:T(8,128)(2,1)S(1)}, u32[]{:S(2)}, u32[]{:S(2)}) async-start(bf16[32,152,128]{2,1,0:T(8,128)(2,1)} %get-tuple-element.43), calls=%async_computation | async-start | bytes 2490368 | tf_op jit(solution)/shard_map/all_to_all | solution.py:417
  52.2 18.5 %all-to-all-done.part_ref = bf16[32,152,128]{2,1,0:T(8,128)(2,1)S(1)} async-done(((bf16[32,152,128]{2,1,0:T(8,128)(2,1)}), bf16[32,152,128]{2,1,0:T(8,128)(2,1)S(1)}, u32[]{:S(2)}, u32[]{:S(2)}) %all-to-all-start) | async-done | bytes 1245216 | tf_op jit(solution)/shard_map/all_to_all | solution.py:417
  70.7 0.3 shard_map.147
  71.0 1.6 %collective-permute-start.13 = (bf16[144,128]{1,0:T(8,128)(2,1)S(1)}, bf16[144,128]{1,0:T(8,128)(2,1)S(1)}, u32[]{:S(2)}, u32[]{:S(2)}) collective-permute-start(bf16[144,128]{1,0:T(8,128)(2,1)S(1)} %get-tuple-element.44.p0), channel_id=1, source_target_pairs={{0,1},{1,2},{2,3},{3,0},{4,5},{5,6},{6,7},{7,4},{8,9},{9,10},{10,1... | collective-permute-start | bytes 110600 | tf_op jit(solution)/shard_map/ppermute | solution.py:284
  72.6 2.4 %collective-permute-start.14 = (bf16[144,128]{1,0:T(8,128)(2,1)S(1)}, bf16[144,128]{1,0:T(8,128)(2,1)S(1)}, u32[]{:S(2)}, u32[]{:S(2)}) collective-permute-start(bf16[144,128]{1,0:T(8,128)(2,1)S(1)} %get-tuple-element.44.p0), channel_id=1, source_target_pairs={{0,2},{1,3},{2,0},{3,1},{4,6},{5,7},{6,4},{7,5},{8,10},{9,11},{10,... | collective-permute-start | bytes 110600 | tf_op jit(solution)/shard_map/ppermute | solution.py:284
  75.0 0.7 collective-permute-start.15
  75.7 0.5 slice.6
  76.2 0.5 slice.7
  76.8 0.0 collective-permute-done.13.p1
  76.8 1.3 %collective-permute-done.14.p2 = bf16[144,128]{1,0:T(8,128)(2,1)S(1)} collective-permute-done((bf16[144,128]{1,0:T(8,128)(2,1)S(1)}, bf16[144,128]{1,0:T(8,128)(2,1)S(1)}, u32[]{:S(2)}, u32[]{:S(2)}) %collective-permute-start.14) | collective-permute-done | bytes 36896 | tf_op jit(solution)/shard_map/ppermute | solution.py:284
  78.1 0.9 %collective-permute-done.15.p3 = bf16[144,128]{1,0:T(8,128)(2,1)S(1)} collective-permute-done((bf16[144,128]{1,0:T(8,128)(2,1)S(1)}, bf16[144,128]{1,0:T(8,128)(2,1)S(1)}, u32[]{:S(2)}, u32[]{:S(2)}) %collective-permute-start.15) | collective-permute-done | bytes 36896 | tf_op jit(solution)/shard_map/ppermute | solution.py:284
  79.0 0.8 shard_map.148
  (3 shorter events, 0.0 us)
Async XLA Ops:
  1.6 20.2 %collective-permute-start = (bf16[272,512]{1,0:T(8,128)(2,1)S(1)}, bf16[272,512]{1,0:T(8,128)(2,1)S(1)}, u32[]{:S(2)}, u32[]{:S(2)}) collective-permute-start(bf16[272,512]{1,0:T(8,128)(2,1)S(1)} %get-tuple-element.25.m0), channel_id=1, source_target_pairs={{0,1},{1,2},{2,3},{3,0},{4,5},{5,6},{6,7},{7,4},{8,9},{9,10},{10,1... | collective-permute-start | bytes 835592 | tf_op jit(solution)/shard_map/ppermute | solution.py:284
  3.7 22.1 %collective-permute-start.1 = (bf16[272,512]{1,0:T(8,128)(2,1)S(1)}, bf16[272,512]{1,0:T(8,128)(2,1)S(1)}, u32[]{:S(2)}, u32[]{:S(2)}) collective-permute-start(bf16[272,512]{1,0:T(8,128)(2,1)S(1)} %get-tuple-element.25.m0), channel_id=1, source_target_pairs={{0,2},{1,3},{2,0},{3,1},{4,6},{5,7},{6,4},{7,5},{8,10},{9,11},{10,... | collective-permute-start | bytes 835592 | tf_op jit(solution)/shard_map/ppermute | solution.py:284
  7.3 18.5 %collective-permute-start.2 = (bf16[272,512]{1,0:T(8,128)(2,1)S(1)}, bf16[272,512]{1,0:T(8,128)(2,1)S(1)}, u32[]{:S(2)}, u32[]{:S(2)}) collective-permute-start(bf16[272,512]{1,0:T(8,128)(2,1)S(1)} %get-tuple-element.25.m0), channel_id=1, source_target_pairs={{0,3},{1,0},{2,1},{3,2},{4,7},{5,4},{6,5},{7,6},{8,11},{9,8},{10,9... | collective-permute-start | bytes 835592 | tf_op jit(solution)/shard_map/ppermute | solution.py:284
  8.3 5.2 %collective-permute-start.3 = (bf16[9,16,128]{2,1,0:T(8,128)(2,1)S(1)}, bf16[9,16,128]{2,1,0:T(8,128)(2,1)S(1)}, u32[]{:S(2)}, u32[]{:S(2)}) collective-permute-start(bf16[9,16,128]{2,1,0:T(8,128)(2,1)S(1)} %get-tuple-element.31.own), channel_id=1, source_target_pairs={{0,8},{4,12},{8,16},{12,20},{16,24},{20,28},{24,0},{28,4},{32,40},... | collective-permute-start | bytes 110600 | tf_op jit(solution)/shard_map/ppermute | solution.py:297
  9.9 5.5 %collective-permute-start.4 = (bf16[9,16,128]{2,1,0:T(8,128)(2,1)S(1)}, bf16[9,16,128]{2,1,0:T(8,128)(2,1)S(1)}, u32[]{:S(2)}, u32[]{:S(2)}) collective-permute-start(bf16[9,16,128]{2,1,0:T(8,128)(2,1)S(1)} %get-tuple-element.31.own), channel_id=1, source_target_pairs={{0,16},{4,20},{8,24},{12,28},{16,0},{20,4},{24,8},{28,12},{32,48},... | collective-permute-start | bytes 110600 | tf_op jit(solution)/shard_map/ppermute | solution.py:297
  13.5 4.0 %collective-permute-start.5 = (bf16[9,16,128]{2,1,0:T(8,128)(2,1)S(1)}, bf16[9,16,128]{2,1,0:T(8,128)(2,1)S(1)}, u32[]{:S(2)}, u32[]{:S(2)}) collective-permute-start(bf16[9,16,128]{2,1,0:T(8,128)(2,1)S(1)} %get-tuple-element.31.own), channel_id=1, source_target_pairs={{0,24},{4,28},{8,0},{12,4},{16,8},{20,12},{24,16},{28,20},{32,56},... | collective-permute-start | bytes 110600 | tf_op jit(solution)/shard_map/ppermute | solution.py:297
  17.5 8.8 %collective-permute-start.6 = (bf16[4,9,16,128]{3,2,1,0:T(8,128)(2,1)S(1)}, bf16[4,9,16,128]{3,2,1,0:T(8,128)(2,1)S(1)}, u32[]{:S(2)}, u32[]{:S(2)}) collective-permute-start(bf16[4,9,16,128]{3,2,1,0:T(8,128)(2,1)S(1)} %shard_map.142.own), channel_id=1, source_target_pairs={{0,32},{4,36},{8,40},{12,44},{16,48},{20,52},{24,56},{28,60},{32,6... | collective-permute-start | bytes 442376 | tf_op jit(solution)/shard_map/ppermute | solution.py:297
  19.1 7.4 %collective-permute-start.7 = (bf16[4,9,16,128]{3,2,1,0:T(8,128)(2,1)S(1)}, bf16[4,9,16,128]{3,2,1,0:T(8,128)(2,1)S(1)}, u32[]{:S(2)}, u32[]{:S(2)}) collective-permute-start(bf16[4,9,16,128]{3,2,1,0:T(8,128)(2,1)S(1)} %shard_map.142.own), channel_id=1, source_target_pairs={{0,64},{4,68},{8,72},{12,76},{16,80},{20,84},{24,88},{28,92},{32,9... | collective-permute-start | bytes 442376 | tf_op jit(solution)/shard_map/ppermute | solution.py:297
  21.8 5.1 %collective-permute-start.8 = (bf16[4,9,16,128]{3,2,1,0:T(8,128)(2,1)S(1)}, bf16[4,9,16,128]{3,2,1,0:T(8,128)(2,1)S(1)}, u32[]{:S(2)}, u32[]{:S(2)}) collective-permute-start(bf16[4,9,16,128]{3,2,1,0:T(8,128)(2,1)S(1)} %shard_map.142.own), channel_id=1, source_target_pairs={{0,96},{4,100},{8,104},{12,108},{16,112},{20,116},{24,120},{28,124... | collective-permute-start | bytes 442376 | tf_op jit(solution)/shard_map/ppermute | solution.py:297
  25.7 1.3 %copy-start.1 = (f32[512,3]{0,1:T(4,128)S(1)}, f32[512,3]{0,1:T(4,128)}, u32[]{:S(2)}) copy-start(f32[512,3]{0,1:T(4,128)} %param.20) | copy-start | bytes 18436
  26.3 2.8 %copy-start = (f32[512]{0:T(512)S(1)}, f32[512]{0:T(512)}, u32[]{:S(2)}) copy-start(f32[512]{0:T(512)} %param.21) | copy-start | bytes 6148
  27.0 2.1 %collective-permute-start.9 = (bf16[4,4,9,16,128]{4,3,2,1,0:T(8,128)(2,1)S(1)}, bf16[4,4,9,16,128]{4,3,2,1,0:T(8,128)(2,1)S(1)}, u32[]{:S(2)}, u32[]{:S(2)}) collective-permute-start(bf16[4,4,9,16,128]{4,3,2,1,0:T(8,128)(2,1)S(1)} %shard_map.143.k0_ref), channel_id=1, source_target_pairs={{0,4},{4,0},{8,12},{12,8},{16,20},{20,16},{24,28},{28,24},{32,36},... | collective-permute-start | bytes 1769480 | tf_op jit(solution)/shard_map/ppermute | solution.py:387
  33.3 4.9 %collective-permute-start.10 = (f32[1,512]{1,0:T(1,128)S(1)}, f32[1,512]{1,0:T(1,128)S(1)}, u32[]{:S(2)}, u32[]{:S(2)}) collective-permute-start(f32[1,512]{1,0:T(1,128)S(1)} %get-tuple-element.37.u0), channel_id=1, source_target_pairs={{0,1},{1,2},{2,3},{3,0},{4,5},{5,6},{6,7},{7,4},{8,9},{9,10},{10,1... | collective-permute-start | bytes 6152 | tf_op jit(solution)/shard_map/ppermute | solution.py:284
  34.4 5.1 %collective-permute-start.11 = (f32[1,512]{1,0:T(1,128)S(1)}, f32[1,512]{1,0:T(1,128)S(1)}, u32[]{:S(2)}, u32[]{:S(2)}) collective-permute-start(f32[1,512]{1,0:T(1,128)S(1)} %get-tuple-element.37.u0), channel_id=1, source_target_pairs={{0,2},{1,3},{2,0},{3,1},{4,6},{5,7},{6,4},{7,5},{8,10},{9,11},{10,... | collective-permute-start | bytes 6152 | tf_op jit(solution)/shard_map/ppermute | solution.py:284
  35.1 4.4 %collective-permute-start.12 = (f32[1,512]{1,0:T(1,128)S(1)}, f32[1,512]{1,0:T(1,128)S(1)}, u32[]{:S(2)}, u32[]{:S(2)}) collective-permute-start(f32[1,512]{1,0:T(1,128)S(1)} %get-tuple-element.37.u0), channel_id=1, source_target_pairs={{0,3},{1,0},{2,1},{3,2},{4,7},{5,4},{6,5},{7,6},{8,11},{9,8},{10,9... | collective-permute-start | bytes 6152 | tf_op jit(solution)/shard_map/ppermute | solution.py:284
  44.8 25.9 %all-to-all-start = ((bf16[32,152,128]{2,1,0:T(8,128)(2,1)}), bf16[32,152,128]{2,1,0:T(8,128)(2,1)S(1)}, u32[]{:S(2)}, u32[]{:S(2)}) async-start(bf16[32,152,128]{2,1,0:T(8,128)(2,1)} %get-tuple-element.43), calls=%async_computation | async-start | bytes 2490368 | tf_op jit(solution)/shard_map/all_to_all | solution.py:417
  71.0 5.7 %collective-permute-start.13 = (bf16[144,128]{1,0:T(8,128)(2,1)S(1)}, bf16[144,128]{1,0:T(8,128)(2,1)S(1)}, u32[]{:S(2)}, u32[]{:S(2)}) collective-permute-start(bf16[144,128]{1,0:T(8,128)(2,1)S(1)} %get-tuple-element.44.p0), channel_id=1, source_target_pairs={{0,1},{1,2},{2,3},{3,0},{4,5},{5,6},{6,7},{7,4},{8,9},{9,10},{10,1... | collective-permute-start | bytes 110600 | tf_op jit(solution)/shard_map/ppermute | solution.py:284
  72.6 5.5 %collective-permute-start.14 = (bf16[144,128]{1,0:T(8,128)(2,1)S(1)}, bf16[144,128]{1,0:T(8,128)(2,1)S(1)}, u32[]{:S(2)}, u32[]{:S(2)}) collective-permute-start(bf16[144,128]{1,0:T(8,128)(2,1)S(1)} %get-tuple-element.44.p0), channel_id=1, source_target_pairs={{0,2},{1,3},{2,0},{3,1},{4,6},{5,7},{6,4},{7,5},{8,10},{9,11},{10,... | collective-permute-start | bytes 110600 | tf_op jit(solution)/shard_map/ppermute | solution.py:284
  75.0 4.0 %collective-permute-start.15 = (bf16[144,128]{1,0:T(8,128)(2,1)S(1)}, bf16[144,128]{1,0:T(8,128)(2,1)S(1)}, u32[]{:S(2)}, u32[]{:S(2)}) collective-permute-start(bf16[144,128]{1,0:T(8,128)(2,1)S(1)} %get-tuple-element.44.p0), channel_id=1, source_target_pairs={{0,3},{1,0},{2,1},{3,2},{4,7},{5,4},{6,5},{7,6},{8,11},{9,8},{10,9... | collective-permute-start | bytes 110600 | tf_op jit(solution)/shard_map/ppermute | solution.py:284
